TPU v7x, 32 devices: a whole 2x2x4 slice. The times are simulated.
32 devices in a mesh: lon: 4 (over z), lat: 8 (over y, x, core).
Axes of the slice: x: 2, y: 2, z: 4, core: 2. Of those that a mesh axis runs over, the one named last changes fastest.
Arguments:
- increment: float32 [4, 32, 64, 512], P(None, None, 'lat', 'lon'), may hold values from -6 to 6
- coef_lon: float32 [4, 64, 512], P(None, 'lat', 'lon'), may hold values from 0.4 to 0.49
- coef_lat: float32 [4, 64, 512], P(None, 'lat', 'lon'), may hold values from 0.4 to 0.49
- obs_values: float32 [4096, 128], P(('lon', 'lat')), may hold values from -1.8 to 1.8
- obs_weight: float32 [4096, 128], P(('lon', 'lat')), may hold values from 0.25 to 4
- obs_operator: float32 [3, 128, 128], replicated, may hold values from -0.5 to 0.5
- obs_columns: int32 [4096], P(('lon', 'lat')), may hold values from 0 to 1023
- obs_types: int32 [4096], P(('lon', 'lat')), may hold values from 0 to 2
- obs_counts: int32 [256], P(('lon', 'lat')), may hold values from 0 to 16, as said below
Outputs:
- gradient: float32 [4, 32, 64, 512], P(None, None, 'lat', 'lon')
- departures: float32 [4096, 128], P(('lon', 'lat'))
Inputs may be any that keep to these rules, and one draw needn't show every extreme that they name: `obs_counts`: each entry counts the live slots of one bucket of 16; slots at or past the count are ignored. In every longitude block some owner latitude block receives full buckets from every source. `obs_columns`: the column within the owner's block, row times 128 plus column. `obs_types`: 0 radiosonde, 1 occultation, 2 radiance.
All inputs are finite; a program needn't handle non-finite values.
Results may differ from a plain program's by a relative error of at most 0.000073.
Values sent between devices are 32-bit elements; how exact they have to be, the bound alone decides.
No kernel may reach another device: no remote copies, remote signals or barrier semaphores. Data moves between devices by JAX's collectives and lax.ppermute only.
A program may use at most 64 MiB of HBM per device.

v0:
```python
import jax
import jax.numpy as jnp
from jax import lax
from jax.sharding import PartitionSpec as P

STEPS = 4


SIGN_TABLE = (1.0, 1.0, -1.0, -1.0)


def with_halo(shard, sides, width, wrap):
    for axis, dim in sides:
        peers, length = (lax.axis_size(axis), shard.shape[dim])
        up = [(i, (i + 1) % peers) for i in range(peers if wrap else peers - 1)]
        down = [(j, i) for i, j in up]
        last = lax.slice_in_dim(shard, length - width, length, axis=dim)
        first = lax.slice_in_dim(shard, 0, width, axis=dim)
        before = lax.ppermute(last, axis, up)
        after = lax.ppermute(first, axis, down)
        shard = jnp.concatenate([before, shard, after], axis=dim)
    return shard


def from_behind(shard, axis, by):
    peers = lax.axis_size(axis)
    return lax.ppermute(shard, axis, [(i, (i + by) % peers) for i in range(peers)])


def extend(block, sign_value, depth):
    lon_count = lax.axis_size("lon")
    lat_count = lax.axis_size("lat")
    lat_index = lax.axis_index("lat")
    wide = with_halo(block, (("lon", 3),), depth, True)
    tall = with_halo(wide, (("lat", 2),), depth, False)
    edge_rows = jnp.stack((wide[:, :, :depth, :], wide[:, :, -depth:, :]))
    mirrored = from_behind(edge_rows, "lon", lon_count // 2)
    mirrored = jnp.flip(mirrored * sign_value, 3)
    south_rim = jnp.where(lat_index == 0, mirrored[0], tall[:, :, :depth, :])
    north_rim = jnp.where(lat_index == lat_count - 1, mirrored[1], tall[:, :, -depth:, :])
    return jnp.concatenate((south_rim, tall[:, :, depth:-depth, :], north_rim), 2)


def spread_inner(field_state, root_lon, root_lat):
    scaled_lon = root_lon * field_state
    scaled_lat = root_lat * field_state
    centre_lon = scaled_lon[:, :, 1:-1, 1:-1]
    centre_lat = scaled_lat[:, :, 1:-1, 1:-1]
    second_lon = scaled_lon[:, :, 1:-1, 2:] + scaled_lon[:, :, 1:-1, :-2] - 2.0 * centre_lon
    second_lat = scaled_lat[:, :, 2:, 1:-1] + scaled_lat[:, :, :-2, 1:-1] - 2.0 * centre_lat
    inner_lon = root_lon[:, :, 1:-1, 1:-1]
    inner_lat = root_lat[:, :, 1:-1, 1:-1]
    updated = field_state[:, :, 1:-1, 1:-1] + inner_lon * second_lon + inner_lat * second_lat
    return (updated, inner_lon, inner_lat)


def diffuse(grid_state, padded_coefs):
    sign_value = jnp.array(SIGN_TABLE, jnp.float32)[:, None, None, None]
    field_state = extend(grid_state, sign_value, STEPS)
    root_lon = padded_coefs[0][:, None]
    root_lat = padded_coefs[1][:, None]
    for turn in range(STEPS):
        field_state, root_lon, root_lat = spread_inner(field_state, root_lon, root_lat)
    return field_state


def decode(slot_code):
    live = slot_code >= 0
    nonneg = jnp.maximum(slot_code, 0)
    return (live, nonneg // 3, nonneg % 3)


def pick_kind(kinds, results):
    return jnp.where(
        (kinds == 0)[:, None], results[0], jnp.where((kinds == 1)[:, None], results[1], results[2])
    )


def observe(live, columns, kinds, observed, weights, obs_operator):
    highest = lax.Precision.HIGHEST
    model = pick_kind(
        kinds, [jnp.dot(columns, obs_operator[kind], precision=highest) for kind in range(3)]
    )
    departures = jnp.where(live[:, None], observed - model, jnp.float32(0.0))
    weighted = weights * departures
    adjoint = pick_kind(
        kinds, [jnp.dot(weighted, obs_operator[kind].T, precision=highest) for kind in range(3)]
    )
    return (departures, adjoint)


def local(
    increment,
    coef_lon,
    coef_lat,
    obs_values,
    obs_weight,
    obs_operator,
    obs_columns,
    obs_types,
    obs_counts,
):
    lat_count = lax.axis_size("lat")
    slot_total = obs_columns.shape[0]
    bucket_size = slot_total // lat_count
    profile_width = increment.shape[0] * increment.shape[1]
    slot_index = jnp.arange(slot_total, dtype=jnp.int32) % bucket_size
    slot_limit = jnp.repeat(obs_counts, bucket_size)
    slot_code = jnp.where(slot_index < slot_limit, obs_columns * 3 + obs_types, -1)
    forcing = jnp.zeros((profile_width, increment.shape[2] * increment.shape[3]), jnp.float32)
    padded_coefs = None
    padded_coefs = extend(jnp.stack((coef_lon, coef_lat)), jnp.float32(1.0), STEPS)
    observed_in, weights_in, code_in = (
        lax.all_to_all(obs_values, "lat", split_axis=0, concat_axis=0, tiled=True),
        lax.all_to_all(obs_weight, "lat", split_axis=0, concat_axis=0, tiled=True),
        lax.all_to_all(slot_code, "lat", split_axis=0, concat_axis=0, tiled=True),
    )
    state = diffuse(increment, padded_coefs)
    flat_state = state.reshape(profile_width, -1)
    live_in, cell_in, kinds_in = decode(code_in)
    columns = flat_state[:, cell_in].T
    owner_departures, adjoint = observe(
        live_in, columns, kinds_in, observed_in, weights_in, obs_operator
    )
    forcing = forcing.at[:, cell_in].add(adjoint.T)
    departures = lax.all_to_all(owner_departures, "lat", split_axis=0, concat_axis=0, tiled=True)
    smoothed = diffuse(forcing.reshape(increment.shape), padded_coefs)
    return (increment - smoothed, departures)


def solution(mesh):
    return jax.shard_map(
        local,
        mesh=mesh,
        in_specs=(
            P(None, None, "lat", "lon"),
            P(None, "lat", "lon"),
            P(None, "lat", "lon"),
            P(("lon", "lat"), None),
            P(("lon", "lat"), None),
            P(),
            P(("lon", "lat")),
            P(("lon", "lat")),
            P(("lon", "lat")),
        ),
        out_specs=(P(None, None, "lat", "lon"), P(("lon", "lat"), None)),
        check_vma=False,
    )
```

profile of v0, /device:TPU:0, one launch (start us, length us, event | category | flops | bytes accessed | tf_op | source)
XLA Modules:
  0.0 226.0 jit_solution(9836623284844980266)
XLA Ops:
  1.6 3.0 %collective-permute-start.5 = (f32[2,4,8,4]{3,2,1,0:T(8,128)S(1)}, f32[2,4,8,4]{3,2,1,0:T(8,128)S(1)}, u32[]{:S(2)}, u32[]{:S(2)}) collective-permute-start(f32[2,4,8,4]{3,2,1,0:T(8,128)S(1)} %get-tuple-element.48), channel_id=1, source_target_pairs={{0,8},{8,16},{16,24},{24,0},{1,9},{9,17},{17,25},{25,1},{2,10},{10... | collective-permute-start | bytes 3080 | tf_op jit(solution)/shard_map/ppermute | solution.py:19
  4.6 2.1 collective-permute-start.6
  9.0 3.9 %all-to-all-start = ((s32[8,16,1]{1,2,0:T(1,128)}), s32[8,16,1]{1,2,0:T(1,128)S(1)}, u32[]{:S(2)}, u32[]{:S(2)}) async-start(s32[8,16,1]{1,2,0:T(1,128)} %bitcast), calls=%async_computation | async-start | bytes 8192 | tf_op jit(solution)/shard_map/all_to_all | solution.py:116
  12.9 3.8 %collective-permute-start.1 = (f32[4,32,8,4]{3,2,1,0:T(8,128)S(1)}, f32[4,32,8,4]{3,2,1,0:T(8,128)S(1)}, u32[]{:S(2)}, u32[]{:S(2)}) collective-permute-start(f32[4,32,8,4]{3,2,1,0:T(8,128)S(1)} %get-tuple-element.37), channel_id=1, source_target_pairs={{8,0},{16,8},{24,16},{0,24},{9,1},{17,9},{25,17},{1,25},{10,2},{18... | collective-permute-start | bytes 49160 | tf_op jit(solution)/shard_map/ppermute | solution.py:20
  17.5 4.0 %all-to-all-start.1 = ((f32[8,16,128]{2,1,0:T(8,128)}), f32[8,16,128]{2,1,0:T(8,128)}, u32[]{:S(2)}, u32[]{:S(2)}) async-start(f32[8,16,128]{2,1,0:T(8,128)} %bitcast.2), calls=%async_computation.1 | async-start | bytes 131072 | tf_op jit(solution)/shard_map/all_to_all | solution.py:115
  23.8 2.4 %collective-permute-start.7 = (f32[2,2,4,4,136]{4,3,2,1,0:T(4,128)S(1)}, f32[2,2,4,4,136]{4,3,2,1,0:T(4,128)S(1)}, u32[]{:S(2)}, u32[]{:S(2)}) collective-permute-start(f32[2,2,4,4,136]{4,3,2,1,0:T(4,128)S(1)} %pad_maximum_fusion.8), channel_id=1, source_target_pairs={{0,16},{8,24},{16,0},{24,8},{1,17},{9,25},{17,1},{25,9},{2,18},{10... | collective-permute-start | bytes 104456 | tf_op jit(solution)/shard_map/ppermute | solution.py:27
  29.5 5.1 %collective-permute-done.1 = f32[4,32,8,4]{3,2,1,0:T(8,128)S(1)} collective-permute-done((f32[4,32,8,4]{3,2,1,0:T(8,128)S(1)}, f32[4,32,8,4]{3,2,1,0:T(8,128)S(1)}, u32[]{:S(2)}, u32[]{:S(2)}) %collective-permute-start.1) | collective-permute-done | bytes 16416 | tf_op jit(solution)/shard_map/ppermute | solution.py:20
  38.9 2.1 collective-permute-start.3
  44.4 41.9 %collective-permute-done.2 = f32[2,4,32,4,136]{4,3,2,1,0:T(4,128)S(1)} collective-permute-done((f32[2,4,32,4,136]{4,3,2,1,0:T(4,128)}, f32[2,4,32,4,136]{4,3,2,1,0:T(4,128)S(1)}, u32[]{:S(2)}, u32[]{:S(2)}) %collective-permute-start.2) | collective-permute-done | bytes 557088 | tf_op jit(solution)/shard_map/ppermute | solution.py:27
  91.2 3.3 %broadcast_multiply_fusion.15 = (f32[4,32,14,134]{3,2,1,0:T(8,128)S(1)}, f32[4,32,14,134]{3,2,1,0:T(8,128)S(1)}) fusion(f32[4,14,134]{2,1,0:T(8,128)S(1)} %get-tuple-element.59, f32[4,32,16,136]{3,2,1,0:T(8,128)S(1)} %broadcast_multiply_fusion.9, f32[4,14,134]{2,1,0:T(8,128)S(1)} %get-tuple-element.58, f32[4,32,16,136]{3,2,1,0:T(8,128)S(1)} %get-tuple-element.20, ...), kind=kLoop, calls=%fused_computation.89 | loop fusion | flops 2641408 | bytes 8704640 | tf_op jit(solution)/shard_map/mul | solution.py:45
  94.8 3.3 %broadcast_multiply_fusion.7 = (f32[4,32,12,132]{3,2,1,0:T(8,128)S(1)}, f32[4,32,12,132]{3,2,1,0:T(8,128)S(1)}) fusion(f32[4,12,132]{2,1,0:T(8,128)S(1)} %get-tuple-element.57, f32[4,32,14,134]{3,2,1,0:T(8,128)S(1)} %broadcast_multiply_fusion.11, f32[4,12,132]{2,1,0:T(8,128)S(1)} %get-tuple-element.56, f32[4,32,14,134]{3,2,1,0:T(8,128)S(1)} %get-tuple-element.18, ...), kind=kLoop, calls=%fused_computation.81 | loop fusion | flops 2230272 | bytes 7349760 | tf_op jit(solution)/shard_map/mul | solution.py:45
  98.4 17.2 %broadcast_multiply_fusion.3 = (f32[4,32,10,130]{3,2,1,0:T(8,128)S(1)}, f32[4,32,10,130]{3,2,1,0:T(8,128)S(1)}) fusion(f32[4,10,130]{2,1,0:T(8,128)S(1)} %get-tuple-element.55, f32[4,32,12,132]{3,2,1,0:T(8,128)S(1)} %broadcast_multiply_fusion.5, f32[4,10,130]{2,1,0:T(8,128)S(1)} %get-tuple-element.54, f32[4,32,12,132]{3,2,1,0:T(8,128)S(1)} %get-tuple-element.16, ...), kind=kLoop, calls=%fused_computation.77 | loop fusion | flops 1830400 | bytes 6032000 | tf_op jit(solution)/shard_map/mul | solution.py:45
  118.6 4.8 %all-to-all-start.2 = ((f32[8,16,128]{2,1,0:T(8,128)}), f32[8,16,128]{2,1,0:T(8,128)S(1)}, u32[]{:S(2)}, u32[]{:S(2)}) async-start(f32[8,16,128]{2,1,0:T(8,128)} %bitcast.4), calls=%async_computation.2 | async-start | bytes 131072 | tf_op jit(solution)/shard_map/all_to_all | solution.py:114
  123.5 4.8 %all-to-all-done.2 = f32[8,16,128]{2,1,0:T(8,128)S(1)} async-done(((f32[8,16,128]{2,1,0:T(8,128)}), f32[8,16,128]{2,1,0:T(8,128)S(1)}, u32[]{:S(2)}, u32[]{:S(2)}) %all-to-all-start.2) | async-done | bytes 65568 | tf_op jit(solution)/shard_map/all_to_all | solution.py:114
  132.9 3.8 %collective-permute-start.11 = (f32[4,32,8,4]{3,2,1,0:T(8,128)S(1)}, f32[4,32,8,4]{3,2,1,0:T(8,128)S(1)}, u32[]{:S(2)}, u32[]{:S(2)}) collective-permute-start(f32[4,32,8,4]{3,2,1,0:T(8,128)S(1)} %get-tuple-element.35), channel_id=1, source_target_pairs={{8,0},{16,8},{24,16},{0,24},{9,1},{17,9},{25,17},{1,25},{10,2},{18... | collective-permute-start | bytes 49160 | tf_op jit(solution)/shard_map/ppermute | solution.py:20
  136.8 12.8 %collective-permute-done.10 = f32[4,32,8,4]{3,2,1,0:T(8,128)S(1)} collective-permute-done((f32[4,32,8,4]{3,2,1,0:T(8,128)S(1)}, f32[4,32,8,4]{3,2,1,0:T(8,128)S(1)}, u32[]{:S(2)}, u32[]{:S(2)}) %collective-permute-start.10) | collective-permute-done | bytes 16416 | tf_op jit(solution)/shard_map/ppermute | solution.py:19
  149.6 8.0 %collective-permute-done.11 = f32[4,32,8,4]{3,2,1,0:T(8,128)S(1)} collective-permute-done((f32[4,32,8,4]{3,2,1,0:T(8,128)S(1)}, f32[4,32,8,4]{3,2,1,0:T(8,128)S(1)}, u32[]{:S(2)}, u32[]{:S(2)}) %collective-permute-start.11) | collective-permute-done | bytes 16416 | tf_op jit(solution)/shard_map/ppermute | solution.py:20
  160.6 2.3 %collective-permute-start.12 = (f32[2,4,32,4,136]{4,3,2,1,0:T(4,128)}, f32[2,4,32,4,136]{4,3,2,1,0:T(4,128)S(1)}, u32[]{:S(2)}, u32[]{:S(2)}) collective-permute-start(f32[2,4,32,4,136]{4,3,2,1,0:T(4,128)} %pad_maximum_fusion.5), channel_id=1, source_target_pairs={{0,16},{8,24},{16,0},{24,8},{1,17},{9,25},{17,1},{25,9},{2,18},{10... | collective-permute-start | bytes 1671176 | tf_op jit(solution)/shard_map/ppermute | solution.py:27
  163.0 3.3 %all-to-all-start.3 = ((f32[8,16,128]{2,1,0:T(8,128)}), f32[8,16,128]{2,1,0:T(8,128)S(1)}, u32[]{:S(2)}, u32[]{:S(2)}) async-start(f32[8,16,128]{2,1,0:T(8,128)} %bitcast.35), calls=%async_computation.3 | async-start | bytes 131072 | tf_op jit(solution)/shard_map/all_to_all | solution.py:126
  166.3 3.1 %collective-permute-start.13 = (f32[4,32,4,136]{3,2,1,0:T(4,128)}, f32[4,32,4,136]{3,2,1,0:T(4,128)}, u32[]{:S(2)}, u32[]{:S(2)}) collective-permute-start(f32[4,32,4,136]{3,2,1,0:T(4,128)} %get-tuple-element.24), channel_id=1, source_target_pairs={{0,1},{1,2},{2,3},{3,4},{4,5},{5,6},{6,7},{8,9},{9,10},{10,11},{11... | collective-permute-start | bytes 835592 | tf_op jit(solution)/shard_map/ppermute | solution.py:19
  171.3 36.3 %collective-permute-done.12 = f32[2,4,32,4,136]{4,3,2,1,0:T(4,128)S(1)} collective-permute-done((f32[2,4,32,4,136]{4,3,2,1,0:T(4,128)}, f32[2,4,32,4,136]{4,3,2,1,0:T(4,128)S(1)}, u32[]{:S(2)}, u32[]{:S(2)}) %collective-permute-start.12) | collective-permute-done | bytes 557088 | tf_op jit(solution)/shard_map/ppermute | solution.py:27
  212.2 3.3 %broadcast_multiply_fusion.14 = (f32[4,32,14,134]{3,2,1,0:T(8,128)S(1)}, f32[4,32,14,134]{3,2,1,0:T(8,128)S(1)}) fusion(f32[4,14,134]{2,1,0:T(8,128)S(1)} %get-tuple-element.59, f32[4,32,16,136]{3,2,1,0:T(8,128)S(1)} %broadcast_multiply_fusion.8, f32[4,14,134]{2,1,0:T(8,128)S(1)} %get-tuple-element.58, f32[4,32,16,136]{3,2,1,0:T(8,128)S(1)} %get-tuple-element.12, ...), kind=kLoop, calls=%fused_computation.88 | loop fusion | flops 2641408 | bytes 8704640 | tf_op jit(solution)/shard_map/mul | solution.py:45
  215.8 3.3 %broadcast_multiply_fusion.6 = (f32[4,32,12,132]{3,2,1,0:T(8,128)S(1)}, f32[4,32,12,132]{3,2,1,0:T(8,128)S(1)}) fusion(f32[4,12,132]{2,1,0:T(8,128)S(1)} %get-tuple-element.57, f32[4,32,14,134]{3,2,1,0:T(8,128)S(1)} %broadcast_multiply_fusion.10, f32[4,12,132]{2,1,0:T(8,128)S(1)} %get-tuple-element.56, f32[4,32,14,134]{3,2,1,0:T(8,128)S(1)} %get-tuple-element.10, ...), kind=kLoop, calls=%fused_computation.80 | loop fusion | flops 2230272 | bytes 7349760 | tf_op jit(solution)/shard_map/mul | solution.py:45
  219.4 3.3 %broadcast_multiply_fusion.2 = (f32[4,32,10,130]{3,2,1,0:T(8,128)S(1)}, f32[4,32,10,130]{3,2,1,0:T(8,128)S(1)}) fusion(f32[4,10,130]{2,1,0:T(8,128)S(1)} %get-tuple-element.55, f32[4,32,12,132]{3,2,1,0:T(8,128)S(1)} %broadcast_multiply_fusion.4, f32[4,10,130]{2,1,0:T(8,128)S(1)} %get-tuple-element.54, f32[4,32,12,132]{3,2,1,0:T(8,128)S(1)} %get-tuple-element.8, ...), kind=kLoop, calls=%fused_computation.76 | loop fusion | flops 1830400 | bytes 6032000 | tf_op jit(solution)/shard_map/mul | solution.py:45
  (139 shorter events, 43.0 us)
Async XLA Ops:
  0.6 23.0 %copy-start.13 = (f32[4,8,128]{2,1,0:T(8,128)S(1)}, f32[4,8,128]{2,1,0:T(8,128)}, u32[]{:S(2)}) copy-start(f32[4,8,128]{2,1,0:T(8,128)} %param.12) | copy-start | bytes 49156
  0.7 33.9 %copy-start = (f32[4,32,8,128]{3,2,1,0:T(8,128)S(1)}, f32[4,32,8,128]{3,2,1,0:T(8,128)}, u32[]{:S(2)}) copy-start(f32[4,32,8,128]{3,2,1,0:T(8,128)} %param.11) | copy-start | bytes 1572868
  1.6 22.0 %collective-permute-start.5 = (f32[2,4,8,4]{3,2,1,0:T(8,128)S(1)}, f32[2,4,8,4]{3,2,1,0:T(8,128)S(1)}, u32[]{:S(2)}, u32[]{:S(2)}) collective-permute-start(f32[2,4,8,4]{3,2,1,0:T(8,128)S(1)} %get-tuple-element.48), channel_id=1, source_target_pairs={{0,8},{8,16},{16,24},{24,0},{1,9},{9,17},{17,25},{25,1},{2,10},{10... | collective-permute-start | bytes 3080 | tf_op jit(solution)/shard_map/ppermute | solution.py:19
  4.6 19.0 %collective-permute-start.6 = (f32[2,4,8,4]{3,2,1,0:T(8,128)S(1)}, f32[2,4,8,4]{3,2,1,0:T(8,128)S(1)}, u32[]{:S(2)}, u32[]{:S(2)}) collective-permute-start(f32[2,4,8,4]{3,2,1,0:T(8,128)S(1)} %get-tuple-element.49), channel_id=1, source_target_pairs={{8,0},{16,8},{24,16},{0,24},{9,1},{17,9},{25,17},{1,25},{10,2},{18... | collective-permute-start | bytes 3080 | tf_op jit(solution)/shard_map/ppermute | solution.py:20
  8.1 21.4 %collective-permute-start = (f32[4,32,8,4]{3,2,1,0:T(8,128)S(1)}, f32[4,32,8,4]{3,2,1,0:T(8,128)S(1)}, u32[]{:S(2)}, u32[]{:S(2)}) collective-permute-start(f32[4,32,8,4]{3,2,1,0:T(8,128)S(1)} %get-tuple-element.36), channel_id=1, source_target_pairs={{0,8},{8,16},{16,24},{24,0},{1,9},{9,17},{17,25},{25,1},{2,10},{10... | collective-permute-start | bytes 49160 | tf_op jit(solution)/shard_map/ppermute | solution.py:19
  9.0 8.5 %all-to-all-start = ((s32[8,16,1]{1,2,0:T(1,128)}), s32[8,16,1]{1,2,0:T(1,128)S(1)}, u32[]{:S(2)}, u32[]{:S(2)}) async-start(s32[8,16,1]{1,2,0:T(1,128)} %bitcast), calls=%async_computation | async-start | bytes 8192 | tf_op jit(solution)/shard_map/all_to_all | solution.py:116
  12.9 21.7 %collective-permute-start.1 = (f32[4,32,8,4]{3,2,1,0:T(8,128)S(1)}, f32[4,32,8,4]{3,2,1,0:T(8,128)S(1)}, u32[]{:S(2)}, u32[]{:S(2)}) collective-permute-start(f32[4,32,8,4]{3,2,1,0:T(8,128)S(1)} %get-tuple-element.37), channel_id=1, source_target_pairs={{8,0},{16,8},{24,16},{0,24},{9,1},{17,9},{25,17},{1,25},{10,2},{18... | collective-permute-start | bytes 49160 | tf_op jit(solution)/shard_map/ppermute | solution.py:20
  17.5 101.1 %all-to-all-start.1 = ((f32[8,16,128]{2,1,0:T(8,128)}), f32[8,16,128]{2,1,0:T(8,128)}, u32[]{:S(2)}, u32[]{:S(2)}) async-start(f32[8,16,128]{2,1,0:T(8,128)} %bitcast.2), calls=%async_computation.1 | async-start | bytes 131072 | tf_op jit(solution)/shard_map/all_to_all | solution.py:115
  23.8 17.2 %collective-permute-start.7 = (f32[2,2,4,4,136]{4,3,2,1,0:T(4,128)S(1)}, f32[2,2,4,4,136]{4,3,2,1,0:T(4,128)S(1)}, u32[]{:S(2)}, u32[]{:S(2)}) collective-permute-start(f32[2,2,4,4,136]{4,3,2,1,0:T(4,128)S(1)} %pad_maximum_fusion.8), channel_id=1, source_target_pairs={{0,16},{8,24},{16,0},{24,8},{1,17},{9,25},{17,1},{25,9},{2,18},{10... | collective-permute-start | bytes 104456 | tf_op jit(solution)/shard_map/ppermute | solution.py:27
  26.2 16.2 %collective-permute-start.8 = (f32[2,4,4,136]{3,2,1,0:T(4,128)S(1)}, f32[2,4,4,136]{3,2,1,0:T(4,128)S(1)}, u32[]{:S(2)}, u32[]{:S(2)}) collective-permute-start(f32[2,4,4,136]{3,2,1,0:T(4,128)S(1)} %get-tuple-element.44), channel_id=1, source_target_pairs={{0,1},{1,2},{2,3},{3,4},{4,5},{5,6},{6,7},{8,9},{9,10},{10,11},{11... | collective-permute-start | bytes 52232 | tf_op jit(solution)/shard_map/ppermute | solution.py:19
  28.2 14.3 %collective-permute-start.9 = (f32[2,4,4,136]{3,2,1,0:T(4,128)S(1)}, f32[2,4,4,136]{3,2,1,0:T(4,128)S(1)}, u32[]{:S(2)}, u32[]{:S(2)}) collective-permute-start(f32[2,4,4,136]{3,2,1,0:T(4,128)S(1)} %get-tuple-element.47), channel_id=1, source_target_pairs={{1,0},{2,1},{3,2},{4,3},{5,4},{6,5},{7,6},{9,8},{10,9},{11,10},{12... | collective-permute-start | bytes 52232 | tf_op jit(solution)/shard_map/ppermute | solution.py:20
  36.3 50.0 %copy-start.14 = (f32[4]{0:T(128)S(1)}, f32[4]{0:T(128)}, u32[]{:S(2)}) copy-start(f32[4]{0:T(128)} %constant.55.clone) | copy-start | bytes 52
  37.6 48.7 %collective-permute-start.2 = (f32[2,4,32,4,136]{4,3,2,1,0:T(4,128)}, f32[2,4,32,4,136]{4,3,2,1,0:T(4,128)S(1)}, u32[]{:S(2)}, u32[]{:S(2)}) collective-permute-start(f32[2,4,32,4,136]{4,3,2,1,0:T(4,128)} %pad_maximum_fusion.3), channel_id=1, source_target_pairs={{0,16},{8,24},{16,0},{24,8},{1,17},{9,25},{17,1},{25,9},{2,18},{10... | collective-permute-start | bytes 1671176 | tf_op jit(solution)/shard_map/ppermute | solution.py:27
  38.9 49.6 %collective-permute-start.3 = (f32[4,32,4,136]{3,2,1,0:T(4,128)}, f32[4,32,4,136]{3,2,1,0:T(4,128)}, u32[]{:S(2)}, u32[]{:S(2)}) collective-permute-start(f32[4,32,4,136]{3,2,1,0:T(4,128)} %get-tuple-element.30), channel_id=1, source_target_pairs={{0,1},{1,2},{2,3},{3,4},{4,5},{5,6},{6,7},{8,9},{9,10},{10,11},{11... | collective-permute-start | bytes 835592 | tf_op jit(solution)/shard_map/ppermute | solution.py:19
  41.0 47.7 %collective-permute-start.4 = (f32[4,32,4,136]{3,2,1,0:T(4,128)}, f32[4,32,4,136]{3,2,1,0:T(4,128)}, u32[]{:S(2)}, u32[]{:S(2)}) collective-permute-start(f32[4,32,4,136]{3,2,1,0:T(4,128)} %get-tuple-element.33), channel_id=1, source_target_pairs={{1,0},{2,1},{3,2},{4,3},{5,4},{6,5},{7,6},{9,8},{10,9},{11,10},{12... | collective-permute-start | bytes 835592 | tf_op jit(solution)/shard_map/ppermute | solution.py:20
  118.6 9.8 %all-to-all-start.2 = ((f32[8,16,128]{2,1,0:T(8,128)}), f32[8,16,128]{2,1,0:T(8,128)S(1)}, u32[]{:S(2)}, u32[]{:S(2)}) async-start(f32[8,16,128]{2,1,0:T(8,128)} %bitcast.4), calls=%async_computation.2 | async-start | bytes 131072 | tf_op jit(solution)/shard_map/all_to_all | solution.py:114
  132.9 16.7 %collective-permute-start.10 = (f32[4,32,8,4]{3,2,1,0:T(8,128)S(1)}, f32[4,32,8,4]{3,2,1,0:T(8,128)S(1)}, u32[]{:S(2)}, u32[]{:S(2)}) collective-permute-start(f32[4,32,8,4]{3,2,1,0:T(8,128)S(1)} %get-tuple-element.34), channel_id=1, source_target_pairs={{0,8},{8,16},{16,24},{24,0},{1,9},{9,17},{17,25},{25,1},{2,10},{10... | collective-permute-start | bytes 49160 | tf_op jit(solution)/shard_map/ppermute | solution.py:19
  132.9 24.6 %collective-permute-start.11 = (f32[4,32,8,4]{3,2,1,0:T(8,128)S(1)}, f32[4,32,8,4]{3,2,1,0:T(8,128)S(1)}, u32[]{:S(2)}, u32[]{:S(2)}) collective-permute-start(f32[4,32,8,4]{3,2,1,0:T(8,128)S(1)} %get-tuple-element.35), channel_id=1, source_target_pairs={{8,0},{16,8},{24,16},{0,24},{9,1},{17,9},{25,17},{1,25},{10,2},{18... | collective-permute-start | bytes 49160 | tf_op jit(solution)/shard_map/ppermute | solution.py:20
  158.0 49.5 %copy-start.15 = (f32[4]{0:T(128)S(1)}, f32[4]{0:T(128)}, u32[]{:S(2)}) copy-start(f32[4]{0:T(128)} %constant.55.clone) | copy-start | bytes 52
  160.6 46.9 %collective-permute-start.12 = (f32[2,4,32,4,136]{4,3,2,1,0:T(4,128)}, f32[2,4,32,4,136]{4,3,2,1,0:T(4,128)S(1)}, u32[]{:S(2)}, u32[]{:S(2)}) collective-permute-start(f32[2,4,32,4,136]{4,3,2,1,0:T(4,128)} %pad_maximum_fusion.5), channel_id=1, source_target_pairs={{0,16},{8,24},{16,0},{24,8},{1,17},{9,25},{17,1},{25,9},{2,18},{10... | collective-permute-start | bytes 1671176 | tf_op jit(solution)/shard_map/ppermute | solution.py:27
  163.0 8.3 %all-to-all-start.3 = ((f32[8,16,128]{2,1,0:T(8,128)}), f32[8,16,128]{2,1,0:T(8,128)S(1)}, u32[]{:S(2)}, u32[]{:S(2)}) async-start(f32[8,16,128]{2,1,0:T(8,128)} %bitcast.35), calls=%async_computation.3 | async-start | bytes 131072 | tf_op jit(solution)/shard_map/all_to_all | solution.py:126
  166.3 43.2 %collective-permute-start.13 = (f32[4,32,4,136]{3,2,1,0:T(4,128)}, f32[4,32,4,136]{3,2,1,0:T(4,128)}, u32[]{:S(2)}, u32[]{:S(2)}) collective-permute-start(f32[4,32,4,136]{3,2,1,0:T(4,128)} %get-tuple-element.24), channel_id=1, source_target_pairs={{0,1},{1,2},{2,3},{3,4},{4,5},{5,6},{6,7},{8,9},{9,10},{10,11},{11... | collective-permute-start | bytes 835592 | tf_op jit(solution)/shard_map/ppermute | solution.py:19
  169.4 40.2 %collective-permute-start.14 = (f32[4,32,4,136]{3,2,1,0:T(4,128)}, f32[4,32,4,136]{3,2,1,0:T(4,128)}, u32[]{:S(2)}, u32[]{:S(2)}) collective-permute-start(f32[4,32,4,136]{3,2,1,0:T(4,128)} %get-tuple-element.27), channel_id=1, source_target_pairs={{1,0},{2,1},{3,2},{4,3},{5,4},{6,5},{7,6},{9,8},{10,9},{11,10},{12... | collective-permute-start | bytes 835592 | tf_op jit(solution)/shard_map/ppermute | solution.py:20
  171.3 36.3 %copy-start.8 = (f32[8,16,128]{2,1,0:T(8,128)}, f32[8,16,128]{2,1,0:T(8,128)S(1)}, u32[]{:S(2)}) copy-start(f32[8,16,128]{2,1,0:T(8,128)S(1)} %all-to-all-done.3) | copy-start | bytes 196612
  (18 other events, 92.8 us)
where the time goes:
time: 224 us; the launch traced here: 226 us
  waiting for transfers between devices  110 us (49%)
  other arithmetic  51.1 us (23%)
  starting transfers between devices  45.9 us (20%)
  local copies, waits for them, and re-layouts  14.3 us (6%)
  matrix products  2.88 us (1%)
    ppermute x3, waiting for transfers between devices, from_behind(): lax.ppermute(shard, axis, [(i, (i + by) % peers) for i in range(peers)])  78.2 us
    mul x8, other arithmetic, spread_inner(): scaled_lon = root_lon * field_state  36.1 us
    ppermute x6, starting transfers between devices, with_halo(): after = lax.ppermute(first, axis, down)  13.5 us
    ppermute x6, waiting for transfers between devices, with_halo(): after = lax.ppermute(first, axis, down)  13 us
    ppermute x6, waiting for transfers between devices, with_halo(): before = lax.ppermute(last, axis, up)  12.8 us
    ppermute x6, starting transfers between devices, with_halo(): before = lax.ppermute(last, axis, up)  10.3 us
    ppermute x3, starting transfers between devices, from_behind(): lax.ppermute(shard, axis, [(i, (i + by) % peers) for i in range(peers)])  6.08 us
    all_to_all x1, waiting for transfers between devices, local(): lax.all_to_all(obs_values, 'lat', split_axis=0, concat_axis=0, tiled=True)  4.81 us
  transfers between devices with their start and end apart: 19, of which 8 were waited for; matrix products, arithmetic and copies ran while one was open for 19% of the time, Pallas kernels for 0%

commit v1 on v0

v1 whole, which is shorter than its diff:
```python
import functools

import jax
import jax.numpy as jnp
from jax import lax
from jax.experimental import pallas as pl
from jax.experimental.pallas import tpu as pltpu
from jax.sharding import PartitionSpec as P

STEPS = 4
ROWS = 8
LANES = 128
PLANES = ROWS + 2 * STEPS
EDGE = 2 * STEPS
VMEM = pltpu.VMEM
MIB = 1 << 20


def lane_of(shape):
    return lax.broadcasted_iota(jnp.int32, shape, len(shape) - 1)


def turn(x, by):
    by = by % LANES if isinstance(by, int) else by
    return pltpu.roll(x, by, x.ndim - 1)


def position():
    lat, count = (lax.axis_index("lat"), lax.axis_size("lat"))
    even = lat % 2 == 0
    pole = jnp.logical_or(lat == 0, lat == count - 1)
    return even, pole


def split(x):
    high = x.astype(jnp.bfloat16)
    low = (x - high.astype(jnp.float32)).astype(jnp.bfloat16)
    return high, low


def matmul(a, b, dims):
    return lax.dot_general(a, b, (dims, ((), ())), preferred_element_type=jnp.float32)


def edges_of(plane_list, rows):
    slot = lane_of((rows, LANES)) // EDGE
    tile = jnp.zeros((rows, LANES), jnp.float32)
    for r, plane in enumerate(plane_list):
        p = STEPS + r
        tile = jnp.where(slot == p, turn(plane, EDGE * p - (LANES - STEPS)), tile)
    return tile


def pack_kernel(inc, cl, ct, b_out, a_out, g_out):
    width = inc.shape[0] // ROWS
    fields = cl.shape[0] // ROWS
    even, _ = position()
    a_row = jnp.where(even, STEPS, 0)
    b_row = STEPS - a_row
    for out, first in ((b_out, b_row), (a_out, a_row)):
        for k in range(STEPS):
            out[k, 0:width, :] = inc[pl.ds(first + k, width, stride=ROWS), :]
            out[k, width : width + fields, :] = cl[pl.ds(first + k, fields, stride=ROWS), :]
            out[k, width + fields : width + 2 * fields, :] = ct[pl.ds(first + k, fields, stride=ROWS), :]
    g_out[0:width, :] = edges_of([inc[pl.ds(r, width, stride=ROWS), :] for r in range(ROWS)], width)
    for n, ref in enumerate((cl, ct)):
        rows = [ref[pl.ds(r, fields, stride=ROWS), :] for r in range(ROWS)]
        g_out[width + n * fields : width + (n + 1) * fields, :] = edges_of(rows, fields)


def slots_kernel(counts, values, weights, columns, types, out):
    owners, bucket = (out.shape[0], values.shape[1])
    slots = columns.shape[1]
    lane = lane_of((1, slots))
    limit = jnp.zeros((1, slots), jnp.int32)
    for d in range(owners):
        limit = jnp.where(lane // bucket == d, counts[d], limit)
    code = jnp.where(lane % bucket < limit, columns[...] * 4 + types[...], -1).astype(jnp.float32)
    out[:, 0:bucket, :] = values[...]
    out[:, bucket : 2 * bucket, :] = weights[...]
    for d in range(owners):
        at = d * bucket
        window = code[:, at // LANES * LANES : at // LANES * LANES + LANES]
        out[d, 2 * bucket : 2 * bucket + 8, :] = jnp.broadcast_to(turn(window, -(at % LANES)), (8, LANES))


def spread_coefs(co, cb, fields):
    for p in range(PLANES + 1):
        for f in range(fields):
            a = jnp.broadcast_to(co[p, f : f + 1, :], (8, LANES))
            b = jnp.broadcast_to(co[p, fields + f : fields + f + 1, :], (8, LANES))
            cb[f, p, 0] = a
            cb[f, p, 1] = b
            cb[f, p, 2] = 1.0 - 2.0 * (a * a + b * b)


def diffuse(xt, ht, cb, store):
    width = xt.shape[1]
    fields = cb.shape[0]
    per_field = width // fields // 8
    lane = lane_of((8, LANES))

    def body(i, carry):
        rows = pl.ds(pl.multiple_of(i * 8, 8), 8)
        fld = i // per_field
        f = {p: xt[p, rows, :] for p in range(PLANES)}
        rim = ht[rows, :]
        for step in range(STEPS):
            low, high = (step, PLANES - 1 - step)
            last = step == STEPS - 1
            rim_l, rim_t, rim_c = (cb[fld, PLANES, n] for n in range(3))
            g_rim = rim_l * rim
            joined = g_rim
            h = {p: cb[fld, p, 1] * f[p] for p in range(low, high + 1)}
            new = {}
            for p in range(low + 1, high):
                a = cb[fld, p, 0]
                g = a * f[p]
                ends = turn(g_rim, LANES - 1 - (EDGE * p + STEPS - 1))
                east = turn(jnp.where(lane == 0, ends, g), -1)
                west = turn(jnp.where(lane == LANES - 1, ends, g), 1)
                new[p] = cb[fld, p, 2] * f[p] + a * (east + west) + cb[fld, p, 1] * (h[p + 1] + h[p - 1])
                if not last:
                    moved = turn(g, EDGE * p + STEPS - 1 - (LANES - 1))
                    joined = jnp.where(lane // EDGE == p, moved, joined)
            if not last:
                east = turn(jnp.where(lane % EDGE == STEPS, joined, g_rim), -1)
                west = turn(jnp.where(lane % EDGE == STEPS - 1, joined, g_rim), 1)
                h_rim = rim_t * rim
                rim = rim_c * rim + rim_l * (east + west) + rim_t * (turn(h_rim, EDGE) + turn(h_rim, -EDGE))
            f = new
        store(i, rows, [f[STEPS + r] for r in range(ROWS)])
        return carry

    lax.fori_loop(0, width // 8, body, 0)


def join_rim(own, from_a, from_b, signed_rows, even, pole):
    rows = own.shape[0]
    slot = lane_of((rows, LANES)) // EDGE
    a_base = jnp.where(even, PLANES - STEPS, 0)
    b_base = jnp.where(even, 0, PLANES - STEPS)
    tile = jnp.where(slot // STEPS == a_base // STEPS, turn(from_a, LANES // 2), own)
    row = lax.broadcasted_iota(jnp.int32, (rows, LANES), 0)
    winds = jnp.logical_and(row >= signed_rows[0], row < signed_rows[1])
    from_b = jnp.where(jnp.logical_and(winds, pole), -from_b, from_b)
    for k in range(STEPS):
        plain = jnp.where(even, ROWS + k, STEPS + k)
        mirrored = jnp.where(even, ROWS - 1 - k, PLANES - STEPS - 1 - k)
        source = jnp.where(pole, mirrored, plain)
        shift = (EDGE * (b_base + k - source) + 2 * LANES) % LANES
        tile = jnp.where(slot == b_base + k, turn(from_b, shift), tile)
    return tile


def side_select(west, east):
    return jnp.where(lane_of(west.shape) % EDGE < STEPS, west, east)


def codes_by_slot(code_rows):
    parts = [
        jnp.broadcast_to(code_rows[:, t * LANES : (t + 1) * LANES], (LANES, LANES)).T
        for t in range(code_rows.shape[1] // LANES)
    ]
    return jnp.concatenate(parts, 0).astype(jnp.int32)


def one_hot(code, rows):
    cell = jnp.where(code >= 0, code // 4, -1)
    lane = lane_of(code.shape)
    return jnp.concatenate([jnp.where(cell == r * LANES + lane, 1.0, 0.0).astype(jnp.bfloat16) for r in rows], 1)


def scatter(adjoint_t, hot):
    high, low = split(adjoint_t)
    return matmul(jnp.concatenate([high, low], 1), jnp.concatenate([hot, hot], 0), ((1,), (0,)))


def middle_kernel(
    inc, cl, ct, a_in, b_in, g_west, g_east, rim_a, rim_b, slots_in, operator,
    dep_out, adj_out, code_out, g_out, f_out, co_out, xt, ht, cb,
):
    width = inc.shape[0] // ROWS
    fields = cl.shape[0] // ROWS
    owners, bucket = (slots_in.shape[0], (slots_in.shape[1] - 8) // 2)
    slots = owners * bucket
    even, pole = position()
    a_base = jnp.where(even, PLANES - STEPS, 0)
    b_base = jnp.where(even, 0, PLANES - STEPS)
    sign = jnp.where(pole, -1.0, 1.0).astype(jnp.float32)
    half = width // 2
    for k in range(STEPS):
        kk = jnp.where(pole, STEPS - 1 - k, k)
        xt[a_base + k] = a_in[k, 0:width, :]
        xt[b_base + k, 0:half, :] = b_in[kk, 0:half, :]
        xt[b_base + k, half:width, :] = b_in[kk, half:width, :] * sign
        co_out[a_base + k] = a_in[k, width : width + 2 * fields, :]
        co_out[b_base + k] = b_in[kk, width : width + 2 * fields, :]
    for r in range(ROWS):
        xt[STEPS + r] = inc[pl.ds(r, width, stride=ROWS), :]
        co_out[STEPS + r, 0:fields, :] = cl[pl.ds(r, fields, stride=ROWS), :]
        co_out[STEPS + r, fields : 2 * fields, :] = ct[pl.ds(r, fields, stride=ROWS), :]
    own = side_select(g_west[...], g_east[...])
    rim = join_rim(own, rim_a[...], rim_b[...], (half, width), even, pole)
    ht[...] = rim[0:width]
    co_out[PLANES] = rim[width : width + 2 * fields]
    spread_coefs(co_out, cb, fields)

    def store(i, rows, planes):
        for r in range(ROWS):
            xt[STEPS + r, rows, :] = planes[r]

    diffuse(xt, ht, cb, store)

    lane = lane_of((1, LANES))
    per_tile = LANES // bucket
    code_parts = []
    for t in range(slots // LANES):
        part = jnp.full((1, LANES), -1.0, jnp.float32)
        for n in range(per_tile):
            d = t * per_tile + n
            got = slots_in[d, 2 * bucket : 2 * bucket + 1, :]
            part = jnp.where(lane // bucket == n, turn(got, n * bucket), part)
        code_parts.append(part)
    code_row = jnp.concatenate(code_parts, 1)
    code = codes_by_slot(code_row)
    hot = one_hot(code, range(ROWS))

    high, low = split(jnp.concatenate([xt[STEPS + r] for r in range(ROWS)], 1))
    both = matmul(hot, jnp.concatenate([high, low], 0), ((1,), (1,)))
    column = both[:, 0:width] + both[:, width:]

    kind = jnp.where(code >= 0, code % 4, -1)
    op_high, op_low = split(operator[...])
    masks = [kind == n for n in range(3)]

    def by_kind(x, dims):
        x_high, x_low = split(x)
        zero = jnp.zeros_like(x_high)
        total = None
        for n in range(3):
            m_high = jnp.where(masks[n], x_high, zero)
            m_low = jnp.where(masks[n], x_low, zero)
            part = matmul(m_high, op_high[n], dims) + matmul(m_high, op_low[n], dims) + matmul(m_low, op_high[n], dims)
            total = part if total is None else total + part
        return total

    model = by_kind(column, ((1,), (0,)))
    values = slots_in[:, 0:bucket, :].reshape(slots, LANES)
    weights = slots_in[:, bucket : 2 * bucket, :].reshape(slots, LANES)
    departures = jnp.where(code >= 0, values - model, 0.0)
    dep_out[...] = departures
    adjoint_t = by_kind(weights * departures, ((1,), (1,))).T
    for t in range(slots // LANES):
        adj_out[t] = adjoint_t[:, t * LANES : (t + 1) * LANES]
        code_out[t] = jnp.broadcast_to(code_row[:, t * LANES : (t + 1) * LANES], (8, LANES))
    forcing = scatter(adjoint_t, hot)
    planes = [forcing[:, r * LANES : (r + 1) * LANES] for r in range(ROWS)]
    for r in range(ROWS):
        f_out[r] = planes[r]
    g_out[...] = edges_of(planes, width)


def last_kernel(inc, f_in, co, g_west, g_east, a_in, b_in, out, xt, ht, cb):
    width = inc.shape[0] // ROWS
    fields = co.shape[1] // 2
    tiles = (a_in.shape[0] - width) // (width + 8)
    even, pole = position()
    half = width // 2
    sign = jnp.where(pole, -1.0, 1.0).astype(jnp.float32)

    def halo(ref, rows, base, flip):
        code = codes_by_slot(
            jnp.concatenate([ref[width * (1 + tiles) + 8 * t : width * (1 + tiles) + 8 * t + 1, :] for t in range(tiles)], 1)
        )
        adjoint_t = jnp.concatenate([ref[width * (1 + t) : width * (2 + t), :] for t in range(tiles)], 1)
        got = scatter(adjoint_t, one_hot(code, rows))
        for k in range(STEPS):
            plane = got[:, k * LANES : (k + 1) * LANES]
            if flip:
                xt[base + k, 0:half, :] = plane[0:half]
                xt[base + k, half:width, :] = plane[half:width] * sign
            else:
                xt[base + k] = plane

    a_first = jnp.where(even, 0, STEPS)
    halo(a_in, [a_first + k for k in range(STEPS)], jnp.where(even, PLANES - STEPS, 0), False)
    plain = [jnp.where(even, STEPS + k, k) for k in range(STEPS)]
    mirrored = [jnp.where(even, STEPS - 1 - k, ROWS - 1 - k) for k in range(STEPS)]
    b_rows = [jnp.where(pole, m, n) for m, n in zip(mirrored, plain)]
    halo(b_in, b_rows, jnp.where(even, 0, PLANES - STEPS), True)
    for r in range(ROWS):
        xt[STEPS + r] = f_in[r]
    own = side_select(g_west[...], g_east[...])
    ht[...] = join_rim(own, a_in[0:width, :], b_in[0:width, :], (half, width), even, pole)
    spread_coefs(co, cb, fields)

    def store(i, rows, planes):
        for r in range(ROWS):
            at = pl.ds(i * 8 * ROWS + r, 8, stride=ROWS)
            out[at, :] = inc[at, :] - planes[r]

    diffuse(xt, ht, cb, store)


def call(kernel, outs, args, scratch=(), smem=(), flops=0, limit=48):
    specs = [pl.BlockSpec(memory_space=pltpu.SMEM if n in smem else VMEM) for n in range(len(args))]
    size = 4 * sum(x.size for x in list(args) + list(outs))
    return pl.pallas_call(
        kernel,
        out_shape=outs,
        in_specs=specs,
        out_specs=[pl.BlockSpec(memory_space=VMEM) for _ in outs],
        scratch_shapes=list(scratch),
        compiler_params=pltpu.CompilerParams(vmem_limit_bytes=limit * MIB),
        cost_estimate=pl.CostEstimate(flops=flops, bytes_accessed=size, transcendentals=0),
    )(*args)


def routes():
    lons, lats = (lax.axis_size("lon"), lax.axis_size("lat"))
    at = lambda lon, lat: lon % lons * lats + lat
    cells = [(lon, lat) for lon in range(lons) for lat in range(lats)]
    inner = [(at(o, a), at(o, a ^ 1)) for o, a in cells]
    outer = []
    for o, a in cells:
        if a in (0, lats - 1):
            outer.append((at(o, a), at(o + lons // 2, a)))
        else:
            outer.append((at(o, a), at(o, a - 1 if a % 2 == 0 else a + 1)))
    east = [(at(o, a), at(o + 1, a)) for o, a in cells]
    west = [(at(o, a), at(o - 1, a)) for o, a in cells]
    return inner, outer, east, west


def local(
    increment, coef_lon, coef_lat, obs_values, obs_weight, obs_operator, obs_columns, obs_types, obs_counts
):
    f32 = jnp.float32
    shape = functools.partial(jax.ShapeDtypeStruct, dtype=f32)
    inner, outer, east, west = routes()
    send = lambda x, route: lax.ppermute(x, ("lon", "lat"), route)
    lats = lax.axis_size("lat")
    slots = obs_values.shape[0]
    bucket = slots // lats
    fields = increment.shape[0]
    width = fields * increment.shape[1]
    tall = width + 2 * fields
    inc = increment.reshape(width * ROWS, LANES)
    cl = coef_lon.reshape(fields * ROWS, LANES)
    ct = coef_lat.reshape(fields * ROWS, LANES)

    b_send, a_send, g_send = call(
        pack_kernel, [shape((STEPS, tall, LANES)), shape((STEPS, tall, LANES)), shape((tall, LANES))], [inc, cl, ct]
    )
    g_west = send(g_send, east)
    g_east = send(g_send, west)
    b_in = send(b_send, outer)
    a_in = send(a_send, inner)
    (slots_send,) = call(
        slots_kernel,
        [shape((lats, 2 * bucket + 8, LANES))],
        [
            obs_counts,
            obs_values.reshape(lats, bucket, LANES),
            obs_weight.reshape(lats, bucket, LANES),
            obs_columns.reshape(1, slots),
            obs_types.reshape(1, slots),
        ],
        smem=(0,),
    )
    slots_in = lax.all_to_all(slots_send, "lat", split_axis=0, concat_axis=0, tiled=True)
    rim_send = side_select(g_west, g_east)
    rim_a = send(rim_send, inner)
    rim_b = send(rim_send, outer)
    scratch = [
        VMEM((PLANES, width, LANES), f32),
        VMEM((width, LANES), f32),
        VMEM((fields, PLANES + 1, 3, 8, LANES), f32),
    ]
    tiles = slots // LANES
    departures, adjoint, code, g_send, forcing, co = call(
        middle_kernel,
        [
            shape((slots, LANES)),
            shape((tiles, width, LANES)),
            shape((tiles, 8, LANES)),
            shape((width, LANES)),
            shape((ROWS, width, LANES)),
            shape((PLANES + 1, 2 * fields, LANES)),
        ],
        [inc, cl, ct, a_in, b_in, g_west, g_east, rim_a, rim_b, slots_in, obs_operator],
        scratch,
        flops=10**8,
    )
    g_west = send(g_send, east)
    g_east = send(g_send, west)
    back = lax.all_to_all(
        departures.reshape(lats, bucket, LANES), "lat", split_axis=0, concat_axis=0, tiled=True
    )
    payload = jnp.concatenate(
        [side_select(g_west, g_east), adjoint.reshape(-1, LANES), code.reshape(-1, LANES)], 0
    )
    a_in = send(payload, inner)
    b_in = send(payload, outer)
    (gradient,) = call(
        last_kernel,
        [shape((width * ROWS, LANES))],
        [inc, forcing, co, g_west, g_east, a_in, b_in],
        scratch,
        flops=10**8,
    )
    return (gradient.reshape(increment.shape), back.reshape(slots, LANES))


def solution(mesh):
    return jax.shard_map(
        local,
        mesh=mesh,
        in_specs=(
            P(None, None, "lat", "lon"),
            P(None, "lat", "lon"),
            P(None, "lat", "lon"),
            P(("lon", "lat"), None),
            P(("lon", "lat"), None),
            P(),
            P(("lon", "lat")),
            P(("lon", "lat")),
            P(("lon", "lat")),
        ),
        out_specs=(P(None, None, "lat", "lon"), P(("lon", "lat"), None)),
        check_vma=False,
    )
```

time: 224 us -> 68.9 us (0.31); the launches traced: 226 us -> 68.5 us
  waiting for transfers between devices: 110 us -> 15.1 us
  other arithmetic: 51.1 us -> 0.05 us
  starting transfers between devices: 45.9 us -> 16.2 us
  Pallas kernels: 0 us -> 24.5 us
  local copies, waits for them, and re-layouts: 14.3 us -> 3.14 us
  blocking collectives: 0 us -> 8.77 us
  matrix products: 2.88 us -> 0 us
    ppermute x15 -> x10, waiting for transfers between devices: 104 us -> 15.1 us  [local(): send = lambda x, route: lax.ppermute(x, ('lon', 'lat'), route)]
    mul x18 -> x0, other arithmetic: 38.5 us -> none  [the longest x8 36.1 us: spread_inner(): scaled_lon = root_lon * field_state]
    pallas_call x0 -> x4, Pallas kernels: none -> 24.5 us  [call(): pl.pallas_call(kernel, out_shape=outs, in_specs=specs, out_specs=[pl.Bloc...]
    ppermute x15 -> x10, starting transfers between devices: 29.9 us -> 12.3 us  [local(): send = lambda x, route: lax.ppermute(x, ('lon', 'lat'), route)]
    all_to_all x4 -> x1, starting transfers between devices: 16 us -> 3.85 us  [local(): lax.all_to_all(slots_send, 'lat', split_axis=0, concat_axis=0, tiled=True)]
    all_to_all x0 -> x1, blocking collectives: none -> 8.77 us  [local(): lax.all_to_all(departures.reshape(lats, bucket, LANES), 'lat', split_axis...]
    slice x14 -> x0, local copies, waits for them, and re-layouts: 7.91 us -> none  [the longest x3 2.55 us: extend(): edge_rows = jnp.stack((wide[:, :, :depth, :], wide[:, :, -depth:, :]))]
    all_to_all x4 -> x1, waiting for transfers between devices: 6.16 us -> 0.01 us  [local(): lax.all_to_all(slots_send, 'lat', split_axis=0, concat_axis=0, tiled=True)]
  transfers between devices with their start and end apart: 19 -> 11, of which waited for: 8 -> 3; matrix products, arithmetic and copies ran while one was open for 19% -> 0% of each run, Pallas kernels for 0% -> 2%
where the time goes in v1:
time: 68.9 us; the launch traced here: 68.5 us
  Pallas kernels  24.5 us (36%)
  starting transfers between devices  16.2 us (24%)
  waiting for transfers between devices  15.1 us (22%)
  blocking collectives  8.77 us (13%)
  local copies, waits for them, and re-layouts  3.14 us (5%)
  between operations  0.8 us (1%)
    pallas_call x4, Pallas kernels, call(): pl.pallas_call(kernel, out_shape=outs, in_specs=specs, out_specs=[pl.Bloc...  24.5 us
    ppermute x10, waiting for transfers between devices, local(): send = lambda x, route: lax.ppermute(x, ('lon', 'lat'), route)  15.1 us
    ppermute x10, starting transfers between devices, local(): send = lambda x, route: lax.ppermute(x, ('lon', 'lat'), route)  12.3 us
    all_to_all x1, blocking collectives, local(): lax.all_to_all(departures.reshape(lats, bucket, LANES), 'lat', split_axis...  8.77 us
    all_to_all x1, starting transfers between devices, local(): lax.all_to_all(slots_send, 'lat', split_axis=0, concat_axis=0, tiled=True)  3.85 us
    unnamed x25, local copies, waits for them, and re-layouts  3.14 us
  transfers between devices with their start and end apart: 11, of which 3 were waited for; matrix products, arithmetic and copies ran while one was open for 0% of the time, Pallas kernels for 2%

profile of v1, /device:TPU:0, one launch (start us, length us, event | category | flops | bytes accessed | tf_op | source)
XLA Modules:
  0.0 68.5 jit_solution(7025112261745285217)
XLA Ops:
  0.6 0.0 copy-start
  0.6 1.0 %copy-done = f32[4,32,8,128]{3,2,1,0:T(8,128)S(1)} copy-done((f32[4,32,8,128]{3,2,1,0:T(8,128)S(1)}, f32[4,32,8,128]{3,2,1,0:T(8,128)}, u32[]{:S(2)}) %copy-start) | copy-done | bytes 524312
  1.7 0.7 %copy-done.3 = f32[4,8,128]{2,1,0:T(8,128)S(1)} copy-done((f32[4,8,128]{2,1,0:T(8,128)S(1)}, f32[4,8,128]{2,1,0:T(8,128)}, u32[]{:S(2)}) %copy-start.3) | copy-done | bytes 16408
  2.4 0.7 %copy-done.5 = f32[4,8,128]{2,1,0:T(8,128)S(1)} copy-done((f32[4,8,128]{2,1,0:T(8,128)S(1)}, f32[4,8,128]{2,1,0:T(8,128)}, u32[]{:S(2)}) %copy-start.5) | copy-done | bytes 16408
  3.1 0.3 shard_map.104
  3.4 0.0 copy-start.1
  3.4 5.1 %collective-permute-start.3 = (f32[136,128]{1,0:T(8,128)S(1)}, f32[136,128]{1,0:T(8,128)S(1)}, u32[]{:S(2)}, u32[]{:S(2)}) collective-permute-start(f32[136,128]{1,0:T(8,128)S(1)} %get-tuple-element.13), channel_id=1, source_target_pairs={{0,24},{1,25},{2,26},{3,27},{4,28},{5,29},{6,30},{7,31},{8,0},{9,1... | collective-permute-start | bytes 208904 | tf_op jit(solution)/shard_map/ppermute | solution.py:342
  8.6 1.3 %shard_map.105 = f32[8,40,128]{2,1,0:T(8,128)} custom-call(s32[8]{0:T(128)S(1)} %copy-done.9, f32[8,16,128]{2,1,0:T(8,128)S(1)} %bitcast.20, f32[8,16,128]{2,1,0:T(8,128)S(1)} %bitcast.21, s32[1,128]{1,0:T(1,128)S(1)} %bitcast.24, s32[1,128]{1,0:T(1,128)S(1)} %bitcast.25), custom_call_target="tpu_custom_call" | custom-call | bytes 295968 | tf_op jit(solution)/shard_map/pallas_call | solution.py:309
  9.9 3.9 %all-to-all-start = ((f32[8,40,128]{2,1,0:T(8,128)}), f32[8,40,128]{2,1,0:T(8,128)S(1)}, u32[]{:S(2)}, u32[]{:S(2)}) async-start(f32[8,40,128]{2,1,0:T(8,128)} %shard_map.105), calls=%async_computation | async-start | bytes 327680 | tf_op jit(solution)/shard_map/all_to_all | solution.py:372
  13.7 0.5 collective-permute-start
  14.2 1.0 %collective-permute-start.1 = (f32[4,136,128]{2,1,0:T(8,128)S(1)}, f32[4,136,128]{2,1,0:T(8,128)S(1)}, u32[]{:S(2)}, u32[]{:S(2)}) collective-permute-start(f32[4,136,128]{2,1,0:T(8,128)S(1)} %get-tuple-element.12), channel_id=1, source_target_pairs={{0,16},{1,2},{2,1},{3,4},{4,3},{5,6},{6,5},{7,23},{8,24},{9,10},{1... | collective-permute-start | bytes 835592 | tf_op jit(solution)/shard_map/ppermute | solution.py:342
  15.3 0.0 copy-start.4
  15.3 2.0 %collective-permute-start.5 = (f32[136,128]{1,0:T(8,128)S(1)}, f32[136,128]{1,0:T(8,128)S(1)}, u32[]{:S(2)}, u32[]{:S(2)}) collective-permute-start(f32[136,128]{1,0:T(8,128)S(1)} %fusion), channel_id=1, source_target_pairs={{0,16},{1,2},{2,1},{3,4},{4,3},{5,6},{6,5},{7,23},{8,24},{9,10},{1... | collective-permute-start | bytes 208904 | tf_op jit(solution)/shard_map/ppermute | solution.py:342
  17.3 8.9 %collective-permute-done.5.rim_b = f32[136,128]{1,0:T(8,128)S(1)} collective-permute-done((f32[136,128]{1,0:T(8,128)S(1)}, f32[136,128]{1,0:T(8,128)S(1)}, u32[]{:S(2)}, u32[]{:S(2)}) %collective-permute-start.5) | collective-permute-done | bytes 69664 | tf_op jit(solution)/shard_map/ppermute | solution.py:342
  26.2 11.7 %shard_map.106 = (f32[128,128]{1,0:T(8,128)S(1)}, f32[1,128,128]{2,1,0:T(8,128)S(1)}, f32[1,8,128]{2,1,0:T(8,128)S(1)}, f32[128,128]{1,0:T(8,128)S(1)}, f32[8,12...) custom-call(f32[1024,128]{1,0:T(8,128)S(1)} %bitcast.13, f32[32,128]{1,0:T(8,128)S(1)} %bitcast.16, f32[32,128]{1,0:T(8,128)S(1)} %bitcast.18, ...), custom_call_target="tpu_custom_call" | custom-call | flops 100000000 | bytes 2547712 | tf_op jit(solution)/shard_map/pallas_call | solution.py:309
  38.0 1.9 %collective-permute-start.7 = (f32[128,128]{1,0:T(8,128)S(1)}, f32[128,128]{1,0:T(8,128)S(1)}, u32[]{:S(2)}, u32[]{:S(2)}) collective-permute-start(f32[128,128]{1,0:T(8,128)S(1)} %get-tuple-element.16), channel_id=1, source_target_pairs={{0,24},{1,25},{2,26},{3,27},{4,28},{5,29},{6,30},{7,31},{8,0},{9,1... | collective-permute-start | bytes 196616 | tf_op jit(solution)/shard_map/ppermute | solution.py:342
  39.9 0.1 collective-permute-start.6
  40.0 2.2 %collective-permute-done.7.g_east = f32[128,128]{1,0:T(8,128)S(1)} collective-permute-done((f32[128,128]{1,0:T(8,128)S(1)}, f32[128,128]{1,0:T(8,128)S(1)}, u32[]{:S(2)}, u32[]{:S(2)}) %collective-permute-start.7) | collective-permute-done | bytes 65568 | tf_op jit(solution)/shard_map/ppermute | solution.py:342
  42.3 4.0 %collective-permute-done.6.g_west = f32[128,128]{1,0:T(8,128)S(1)} collective-permute-done((f32[128,128]{1,0:T(8,128)S(1)}, f32[128,128]{1,0:T(8,128)S(1)}, u32[]{:S(2)}, u32[]{:S(2)}) %collective-permute-start.6) | collective-permute-done | bytes 65568 | tf_op jit(solution)/shard_map/ppermute | solution.py:342
  46.3 0.1 collective-permute-start.9
  46.4 1.6 %collective-permute-start.8 = (f32[264,128]{1,0:T(8,128)S(1)}, f32[264,128]{1,0:T(8,128)S(1)}, u32[]{:S(2)}, u32[]{:S(2)}) collective-permute-start(f32[264,128]{1,0:T(8,128)S(1)} %pad_maximum_fusion), channel_id=1, source_target_pairs={{0,1},{1,0},{2,3},{3,2},{4,5},{5,4},{6,7},{7,6},{8,9},{9,8},{10,11... | collective-permute-start | bytes 405512 | tf_op jit(solution)/shard_map/ppermute | solution.py:342
  47.9 8.8 %all_to_all.10 = f32[8,16,128]{2,1,0:T(8,128)S(1)} all-to-all(f32[8,16,128]{2,1,0:T(8,128)S(1)} %bitcast.19), channel_id=1, replica_groups=mesh['lon'=4,'lat'=8] {'lat'}, dimensions={0} | all-to-all | bytes 131072 | tf_op jit(solution)/shard_map/all_to_all | solution.py:398
  56.7 11.2 %shard_map.107 = f32[1024,128]{1,0:T(8,128)} custom-call(f32[1024,128]{1,0:T(8,128)S(1)} %bitcast.14, f32[8,128,128]{2,1,0:T(8,128)S(1)} %get-tuple-element.14.f_in, f32[17,8,128]{2,1,0:T(8,128)S(1)} %get-tuple-element.15.co, f32[128,128]{1,0:T(8,128)S(1)} %collective-permute-done.6.g_west, f32[128,128]{1,0:T(8,128)S(1)} %collective-permute-done.7.g_east, ...), custom_call_target="tpu_custom_call" | custom-call | flops 100000000 | bytes 2043904 | tf_op jit(solution)/shard_map/pallas_call | solution.py:309
  67.9 0.6 copy.12
  (33 shorter events, 0.1 us)
Async XLA Ops:
  0.6 1.0 %copy-start = (f32[4,32,8,128]{3,2,1,0:T(8,128)S(1)}, f32[4,32,8,128]{3,2,1,0:T(8,128)}, u32[]{:S(2)}) copy-start(f32[4,32,8,128]{3,2,1,0:T(8,128)} %param.9) | copy-start | bytes 1572868
  1.7 0.7 %copy-start.3 = (f32[4,8,128]{2,1,0:T(8,128)S(1)}, f32[4,8,128]{2,1,0:T(8,128)}, u32[]{:S(2)}) copy-start(f32[4,8,128]{2,1,0:T(8,128)} %param.10) | copy-start | bytes 49156
  2.4 0.7 %copy-start.5 = (f32[4,8,128]{2,1,0:T(8,128)S(1)}, f32[4,8,128]{2,1,0:T(8,128)}, u32[]{:S(2)}) copy-start(f32[4,8,128]{2,1,0:T(8,128)} %param.11) | copy-start | bytes 49156
  3.1 5.4 %copy-start.7 = (f32[128,128]{1,0:T(8,128)S(1)}, f32[128,128]{1,0:T(8,128)}, u32[]{:S(2)}) copy-start(f32[128,128]{1,0:T(8,128)} %param.12) | copy-start | bytes 196612
  3.1 5.4 %copy-start.8 = (f32[128,128]{1,0:T(8,128)S(1)}, f32[128,128]{1,0:T(8,128)}, u32[]{:S(2)}) copy-start(f32[128,128]{1,0:T(8,128)} %param.13) | copy-start | bytes 196612
  3.1 5.4 %copy-start.9 = (s32[8]{0:T(128)S(1)}, s32[8]{0:T(128)}, u32[]{:S(2)}) copy-start(s32[8]{0:T(128)} %counts.1) | copy-start | bytes 100
  3.1 5.4 %copy-start.10 = (s32[128]{0:T(128)S(1)}, s32[128]{0:T(128)}, u32[]{:S(2)}) copy-start(s32[128]{0:T(128)} %param.15) | copy-start | bytes 1540
  3.1 5.4 %copy-start.11 = (s32[128]{0:T(128)S(1)}, s32[128]{0:T(128)}, u32[]{:S(2)}) copy-start(s32[128]{0:T(128)} %param.16) | copy-start | bytes 1540
  3.4 22.8 %copy-start.1 = (f32[4,32,8,128]{3,2,1,0:T(8,128)S(1)}, f32[4,32,8,128]{3,2,1,0:T(8,128)}, u32[]{:S(2)}) copy-start(f32[4,32,8,128]{3,2,1,0:T(8,128)} %param.9) | copy-start | bytes 1572868
  3.4 11.8 %collective-permute-start.3 = (f32[136,128]{1,0:T(8,128)S(1)}, f32[136,128]{1,0:T(8,128)S(1)}, u32[]{:S(2)}, u32[]{:S(2)}) collective-permute-start(f32[136,128]{1,0:T(8,128)S(1)} %get-tuple-element.13), channel_id=1, source_target_pairs={{0,24},{1,25},{2,26},{3,27},{4,28},{5,29},{6,30},{7,31},{8,0},{9,1... | collective-permute-start | bytes 208904 | tf_op jit(solution)/shard_map/ppermute | solution.py:342
  8.5 6.7 %collective-permute-start.2 = (f32[136,128]{1,0:T(8,128)S(1)}, f32[136,128]{1,0:T(8,128)S(1)}, u32[]{:S(2)}, u32[]{:S(2)}) collective-permute-start(f32[136,128]{1,0:T(8,128)S(1)} %get-tuple-element.13), channel_id=1, source_target_pairs={{0,8},{1,9},{2,10},{3,11},{4,12},{5,13},{6,14},{7,15},{8,16},{9,17... | collective-permute-start | bytes 208904 | tf_op jit(solution)/shard_map/ppermute | solution.py:342
  9.9 16.3 %copy-start.2 = (f32[3,128,128]{2,1,0:T(8,128)S(1)}, f32[3,128,128]{2,1,0:T(8,128)}, u32[]{:S(2)}) copy-start(f32[3,128,128]{2,1,0:T(8,128)} %operator.1) | copy-start | bytes 589828
  9.9 16.3 %all-to-all-start = ((f32[8,40,128]{2,1,0:T(8,128)}), f32[8,40,128]{2,1,0:T(8,128)S(1)}, u32[]{:S(2)}, u32[]{:S(2)}) async-start(f32[8,40,128]{2,1,0:T(8,128)} %shard_map.105), calls=%async_computation | async-start | bytes 327680 | tf_op jit(solution)/shard_map/all_to_all | solution.py:372
  13.7 12.4 %collective-permute-start = (f32[4,136,128]{2,1,0:T(8,128)S(1)}, f32[4,136,128]{2,1,0:T(8,128)S(1)}, u32[]{:S(2)}, u32[]{:S(2)}) collective-permute-start(f32[4,136,128]{2,1,0:T(8,128)S(1)} %get-tuple-element.11), channel_id=1, source_target_pairs={{0,1},{1,0},{2,3},{3,2},{4,5},{5,4},{6,7},{7,6},{8,9},{9,8},{10,11... | collective-permute-start | bytes 835592 | tf_op jit(solution)/shard_map/ppermute | solution.py:342
  14.2 11.9 %collective-permute-start.1 = (f32[4,136,128]{2,1,0:T(8,128)S(1)}, f32[4,136,128]{2,1,0:T(8,128)S(1)}, u32[]{:S(2)}, u32[]{:S(2)}) collective-permute-start(f32[4,136,128]{2,1,0:T(8,128)S(1)} %get-tuple-element.12), channel_id=1, source_target_pairs={{0,16},{1,2},{2,1},{3,4},{4,3},{5,6},{6,5},{7,23},{8,24},{9,10},{1... | collective-permute-start | bytes 835592 | tf_op jit(solution)/shard_map/ppermute | solution.py:342
  15.3 11.0 %copy-start.4 = (f32[4,8,128]{2,1,0:T(8,128)S(1)}, f32[4,8,128]{2,1,0:T(8,128)}, u32[]{:S(2)}) copy-start(f32[4,8,128]{2,1,0:T(8,128)} %param.10) | copy-start | bytes 49156
  15.3 10.9 %copy-start.6 = (f32[4,8,128]{2,1,0:T(8,128)S(1)}, f32[4,8,128]{2,1,0:T(8,128)}, u32[]{:S(2)}) copy-start(f32[4,8,128]{2,1,0:T(8,128)} %param.11) | copy-start | bytes 49156
  15.3 10.9 %collective-permute-start.5 = (f32[136,128]{1,0:T(8,128)S(1)}, f32[136,128]{1,0:T(8,128)S(1)}, u32[]{:S(2)}, u32[]{:S(2)}) collective-permute-start(f32[136,128]{1,0:T(8,128)S(1)} %fusion), channel_id=1, source_target_pairs={{0,16},{1,2},{2,1},{3,4},{4,3},{5,6},{6,5},{7,23},{8,24},{9,10},{1... | collective-permute-start | bytes 208904 | tf_op jit(solution)/shard_map/ppermute | solution.py:342
  17.3 8.9 %collective-permute-start.4 = (f32[136,128]{1,0:T(8,128)S(1)}, f32[136,128]{1,0:T(8,128)S(1)}, u32[]{:S(2)}, u32[]{:S(2)}) collective-permute-start(f32[136,128]{1,0:T(8,128)S(1)} %fusion), channel_id=1, source_target_pairs={{0,1},{1,0},{2,3},{3,2},{4,5},{5,4},{6,7},{7,6},{8,9},{9,8},{10,11... | collective-permute-start | bytes 208904 | tf_op jit(solution)/shard_map/ppermute | solution.py:342
  38.0 4.3 %collective-permute-start.7 = (f32[128,128]{1,0:T(8,128)S(1)}, f32[128,128]{1,0:T(8,128)S(1)}, u32[]{:S(2)}, u32[]{:S(2)}) collective-permute-start(f32[128,128]{1,0:T(8,128)S(1)} %get-tuple-element.16), channel_id=1, source_target_pairs={{0,24},{1,25},{2,26},{3,27},{4,28},{5,29},{6,30},{7,31},{8,0},{9,1... | collective-permute-start | bytes 196616 | tf_op jit(solution)/shard_map/ppermute | solution.py:342
  39.9 6.3 %collective-permute-start.6 = (f32[128,128]{1,0:T(8,128)S(1)}, f32[128,128]{1,0:T(8,128)S(1)}, u32[]{:S(2)}, u32[]{:S(2)}) collective-permute-start(f32[128,128]{1,0:T(8,128)S(1)} %get-tuple-element.16), channel_id=1, source_target_pairs={{0,8},{1,9},{2,10},{3,11},{4,12},{5,13},{6,14},{7,15},{8,16},{9,17... | collective-permute-start | bytes 196616 | tf_op jit(solution)/shard_map/ppermute | solution.py:342
  46.3 10.4 %collective-permute-start.9 = (f32[264,128]{1,0:T(8,128)S(1)}, f32[264,128]{1,0:T(8,128)S(1)}, u32[]{:S(2)}, u32[]{:S(2)}) collective-permute-start(f32[264,128]{1,0:T(8,128)S(1)} %pad_maximum_fusion), channel_id=1, source_target_pairs={{0,16},{1,2},{2,1},{3,4},{4,3},{5,6},{6,5},{7,23},{8,24},{9,10},{1... | collective-permute-start | bytes 405512 | tf_op jit(solution)/shard_map/ppermute | solution.py:342
  46.4 10.4 %collective-permute-start.8 = (f32[264,128]{1,0:T(8,128)S(1)}, f32[264,128]{1,0:T(8,128)S(1)}, u32[]{:S(2)}, u32[]{:S(2)}) collective-permute-start(f32[264,128]{1,0:T(8,128)S(1)} %pad_maximum_fusion), channel_id=1, source_target_pairs={{0,1},{1,0},{2,3},{3,2},{4,5},{5,4},{6,7},{7,6},{8,9},{9,8},{10,11... | collective-permute-start | bytes 405512 | tf_op jit(solution)/shard_map/ppermute | solution.py:342

commit v2 on v0

v2 whole, which is shorter than its diff:
```python
import functools

import jax
import jax.numpy as jnp
from jax import lax
from jax.experimental import pallas as pl
from jax.experimental.pallas import tpu as pltpu
from jax.sharding import PartitionSpec as P

STEPS = 4
ROWS = 8
LANES = 128
PLANES = ROWS + 2 * STEPS
WIDE = LANES + 2 * STEPS
REGS = WIDE // 8
PADDED = LANES + 16
VMEM = pltpu.VMEM
HBM = pltpu.HBM
MIB = 1 << 20
F32 = jnp.float32


def iota(shape, axis):
    return lax.broadcasted_iota(jnp.int32, shape, axis)


def position():
    lat, count = (lax.axis_index("lat"), lax.axis_size("lat"))
    return lat % 2 == 0, jnp.logical_or(lat == 0, lat == count - 1)


def halo_places(even, pole):
    a_base = jnp.where(even, PLANES - STEPS, 0)
    b_base = jnp.where(even, 0, PLANES - STEPS)
    a_rows = [jnp.where(even, k, STEPS + k) for k in range(STEPS)]
    b_rows = [
        jnp.where(
            pole,
            jnp.where(even, STEPS - 1 - k, ROWS - 1 - k),
            jnp.where(even, STEPS + k, k),
        )
        for k in range(STEPS)
    ]
    return a_base, b_base, a_rows, b_rows


def wind_sign(pole, shape):
    flipped = jnp.logical_and(iota(shape, len(shape) - 1) >= LANES // 2, pole)
    return jnp.where(flipped, -1.0, 1.0).astype(F32)


def split(x):
    high = x.astype(jnp.bfloat16)
    low = (x - high.astype(F32)).astype(jnp.bfloat16)
    return high, low


def matmul(a, b, dims=((1,), (0,))):
    return lax.dot_general(a, b, (dims, ((), ())), preferred_element_type=F32)


def halves(x):
    return x[:, :LANES] + x[:, LANES:]


def pack_kernel(inc_hbm, cl_hbm, ct_hbm, own, coef, b_out, a_out, w_out, e_out, inc, cl, ct, raw, sems):
    copies = [
        pltpu.make_async_copy(src, dst, sems.at[n])
        for n, (src, dst) in enumerate(((inc_hbm, inc), (cl_hbm, cl), (ct_hbm, ct)))
    ]
    for copy in copies:
        copy.start()
    for copy in copies:
        copy.wait()
    fields = cl.shape[0] // ROWS
    even, _ = position()
    raw[...] = jnp.zeros(raw.shape, F32)
    for r in range(ROWS):
        own[r] = inc[pl.ds(r, LANES, stride=ROWS), :].T
        at = 8 * (STEPS + r)
        raw[at : at + fields, :] = cl[pl.ds(r, fields, stride=ROWS), :]
        raw[at + fields : at + 2 * fields, :] = ct[pl.ds(r, fields, stride=ROWS), :]
        w_out[r] = own[r, 0:STEPS, :]
        e_out[r] = own[r, LANES - STEPS : LANES, :]
    coef[...] = raw[...].T
    w_out[ROWS] = coef[0:STEPS, :]
    e_out[ROWS] = coef[LANES - STEPS : LANES, :]
    a_row = jnp.where(even, STEPS, 0)
    b_row = STEPS - a_row
    for out, first in ((b_out, b_row), (a_out, a_row)):
        for k in range(STEPS):
            out[k * LANES : (k + 1) * LANES, :] = own[first + k]
            at = STEPS * LANES + 8 * k
            out[at : at + 8, :] = raw[pl.ds(pl.multiple_of(8 * (STEPS + first + k), 8), 8), :]


def slots_kernel(counts, values, weights, columns, types, out):
    owners, bucket = (out.shape[0], values.shape[1])
    slots = columns.shape[1]
    lane = iota((1, slots), 1)
    limit = jnp.zeros((1, slots), jnp.int32)
    for d in range(owners):
        limit = jnp.where(lane // bucket == d, counts[d], limit)
    code = jnp.where(lane % bucket < limit, columns[...] * 4 + types[...], -1).astype(F32)
    out[:, 0:bucket, :] = values[...]
    out[:, bucket : 2 * bucket, :] = weights[...]
    for d in range(owners):
        at = d * bucket
        window = code[:, at // LANES * LANES : at // LANES * LANES + LANES]
        moved = pltpu.roll(window, (-at) % LANES, 1)
        out[d, 2 * bucket : 2 * bucket + 8, :] = jnp.broadcast_to(moved, (8, LANES))


def coefs_wide(coef, a_in, b_in, from_west, from_east, rim_a, rim_b, raw, co_out, even, pole):
    a_base, b_base, _, b_rows = halo_places(even, pole)
    raw[...] = jnp.zeros(raw.shape, F32)
    for k in range(STEPS):
        kk = jnp.where(pole, STEPS - 1 - k, k)
        at = STEPS * LANES
        raw[pl.ds(pl.multiple_of(8 * (a_base + k), 8), 8), :] = a_in[at + 8 * k : at + 8 * k + 8, :]
        raw[pl.ds(pl.multiple_of(8 * (b_base + k), 8), 8), :] = b_in[pl.ds(pl.multiple_of(at + 8 * kk, 8), 8), :]
    co_out[8 : 8 + LANES, :] = raw[...].T + coef[...]
    tile = jnp.concatenate([from_west[ROWS], from_east[ROWS]], 0)
    plane = iota((8, LANES), 1) // 8
    tile = jnp.where(plane // STEPS == a_base // STEPS, pltpu.roll(rim_a[ROWS], LANES // 2, 1), tile)
    for k in range(STEPS):
        shift = (8 * (b_base + k - STEPS - b_rows[k]) + 2 * LANES) % LANES
        tile = jnp.where(plane == b_base + k, pltpu.roll(rim_b[ROWS], shift, 1), tile)
    co_out[8 - STEPS : 8, :] = tile[0:STEPS]
    co_out[8 + LANES : 8 + LANES + STEPS, :] = tile[STEPS : 2 * STEPS]


def expand(co, cl, ct, cc):
    wide = jnp.concatenate([co[pl.ds(8 - STEPS + q, 8, stride=REGS), :] for q in range(REGS)], 0)
    high, low = split(wide)
    tall = 2 * LANES - 16
    row, col = (iota((tall, 2 * LANES), 0), iota((tall, 2 * LANES), 1))
    wanted = LANES - 16 + col // LANES * 4 + col % LANES // (LANES // 4)
    picks = [jnp.where(row == wanted + 8 * odd, 1.0, 0.0).astype(jnp.bfloat16) for odd in range(2)]
    for p in range(PLANES):
        first = LANES - 16 - p // 2 * 16
        pick = picks[p % 2][first : first + LANES, :]
        both = matmul(high, pick) + matmul(low, pick)
        a, b = (both[:, :LANES], both[:, LANES:])
        cl[p] = a
        ct[p] = b
        cc[p] = 1.0 - 2.0 * (a * a + b * b)


def diffuse(f, spare, cl, ct, cc, store=None):
    for step in range(STEPS):
        last = step == STEPS - 1 and store is not None

        def row(p, carry, f=f, spare=spare, last=last):
            regs = [pl.ds(8 * q, 8) for q in range(REGS)]
            here = [f[p, at, :] for at in regs]
            g = [cl[p, at, :] * x for at, x in zip(regs, here)]
            g = [pltpu.roll(g[-1], 1, 0)] + g + [pltpu.roll(g[0], 7, 0)]
            for q, at in enumerate(regs):
                sides = ct[p + 1, at, :] * f[p + 1, at, :] + ct[p - 1, at, :] * f[p - 1, at, :]
                new = cc[p, at, :] * here[q] + cl[p, at, :] * (g[q] + g[q + 2]) + ct[p, at, :] * sides
                if last:
                    store(p - STEPS, q, new)
                else:
                    spare[p, at, :] = new
            return carry

        lax.fori_loop(step + 1, PLANES - 1 - step, row, 0)
        f, spare = (spare, f)


def cell_of(n, rows):
    plane = (n * 482) >> 16
    rest = n - WIDE * plane
    column = (rest % 8) * REGS + rest // 8 - STEPS
    row = jnp.full(n.shape, -1, jnp.int32)
    for k, r in enumerate(rows):
        row = jnp.where(plane == k, r, row)
    inside = jnp.logical_and(jnp.logical_and(column >= 0, column < LANES), row >= 0)
    return jnp.where(inside, row * LANES + column, -2)


def scatter(adjoint, code_row, rows):
    high, low = split(adjoint)
    code = code_row.astype(jnp.int32)
    cell = jnp.where(code >= 0, code >> 2, -1)
    places = cell_of(iota((len(rows) * WIDE, LANES), 0), rows)
    hot = jnp.concatenate(
        [
            jnp.where(places == cell[:, t * LANES : (t + 1) * LANES], 1.0, 0.0).astype(jnp.bfloat16)
            for t in range(cell.shape[1] // LANES)
        ],
        1,
    )
    return halves(matmul(hot, jnp.concatenate([high, low], 1)))


def middle_kernel(
    own, coef, a_in, b_in, from_west, from_east, rim_a, rim_b, slots_in, operator,
    dep_out, adj_out, code_out, w_out, e_out, f_out, co_out,
    wide, raw, f, spare, cl, ct, cc,
):
    owners, bucket = (slots_in.shape[0], (slots_in.shape[1] - 8) // 2)
    slots = owners * bucket
    even, pole = position()
    a_base, b_base, a_rows, b_rows = halo_places(even, pole)
    sign = wind_sign(pole, (1, LANES))
    inner = slice(8, 8 + LANES)
    west, east = (slice(8 - STEPS, 8), slice(8 + LANES, 8 + LANES + STEPS))
    coefs_wide(coef, a_in, b_in, from_west, from_east, rim_a, rim_b, raw, co_out, even, pole)
    expand(co_out, cl, ct, cc)
    for k in range(STEPS):
        wide[a_base + k, inner, :] = a_in[k * LANES : (k + 1) * LANES, :]
        wide[a_base + k, west, :] = rim_a[a_rows[k], 0:STEPS, :]
        wide[a_base + k, east, :] = rim_a[a_rows[k], STEPS : 2 * STEPS, :]
        at = pl.multiple_of(jnp.where(pole, STEPS - 1 - k, k) * LANES, LANES)
        wide[b_base + k, inner, :] = b_in[pl.ds(at, LANES), :] * sign
        wide[b_base + k, west, :] = rim_b[b_rows[k], 0:STEPS, :] * sign
        wide[b_base + k, east, :] = rim_b[b_rows[k], STEPS : 2 * STEPS, :] * sign
    for r in range(ROWS):
        wide[STEPS + r, inner, :] = own[r]
        wide[STEPS + r, west, :] = from_west[r]
        wide[STEPS + r, east, :] = from_east[r]

    def interleave(p, carry):
        for q in range(REGS):
            f[p, pl.ds(8 * q, 8), :] = wide[p, pl.ds(8 - STEPS + q, 8, stride=REGS), :]
        return carry

    lax.fori_loop(0, PLANES, interleave, 0)
    diffuse(f, spare, cl, ct, cc)

    lane = iota((1, LANES), 1)
    per_tile = LANES // bucket
    code_parts = []
    for t in range(slots // LANES):
        part = jnp.full((1, LANES), -1.0, F32)
        for n in range(per_tile):
            got = slots_in[t * per_tile + n, 2 * bucket : 2 * bucket + 1, :]
            part = jnp.where(lane // bucket == n, pltpu.roll(got, n * bucket, 1), part)
        code_parts.append(part)
        code_out[8 * t : 8 * t + 8, :] = jnp.broadcast_to(part, (8, LANES))
    code_row = jnp.concatenate(code_parts, 1)
    code = jnp.concatenate([jnp.broadcast_to(part, (LANES, LANES)).T for part in code_parts], 0)
    code = code.astype(jnp.int32)
    cell = jnp.where(code >= 0, code >> 2, -1)
    kind = jnp.where(code >= 0, code & 3, -1)

    depth = ROWS * WIDE
    padded = (depth + LANES - 1) // LANES * LANES
    places = cell_of(iota((1, padded), 1), range(ROWS))
    hot = jnp.concatenate(
        [
            jnp.where(places[:, t : t + LANES] == cell, 1.0, 0.0).astype(jnp.bfloat16)
            for t in range(0, padded, LANES)
        ],
        1,
    )
    state = jnp.concatenate(split(f[STEPS : STEPS + ROWS].reshape(depth, LANES)), 1)
    state = jnp.concatenate([state, jnp.zeros((padded - depth, 2 * LANES), jnp.bfloat16)], 0)
    column = halves(matmul(hot, state))

    masks = [kind == n for n in range(3)]
    op_high, op_low = split(operator[...])
    zero = jnp.zeros((LANES, LANES), jnp.bfloat16)

    def by_kind(x):
        return jnp.concatenate([jnp.where(m, part, jnp.zeros_like(part)) for part in split(x) for m in masks], 1)

    forward = jnp.concatenate(
        [jnp.concatenate([op_high[n], op_low[n]], 1) for n in range(3)]
        + [jnp.concatenate([op_high[n], zero], 1) for n in range(3)],
        0,
    )
    model = halves(matmul(by_kind(column), forward))
    values = slots_in[:, 0:bucket, :].reshape(slots, LANES)
    weights = slots_in[:, bucket : 2 * bucket, :].reshape(slots, LANES)
    departures = jnp.where(code >= 0, values - model, 0.0)
    dep_out[...] = departures
    backward = jnp.concatenate(
        [
            jnp.concatenate([op_high[0], op_high[1], op_high[2]] * 2, 1),
            jnp.concatenate([op_low[0], op_low[1], op_low[2], zero, zero, zero], 1),
        ],
        0,
    )
    adjoint = halves(matmul(by_kind(weights * departures), backward, ((1,), (1,))))
    adj_out[...] = adjoint
    forcing = scatter(adjoint, code_row, range(ROWS))
    for r in range(ROWS):
        f_out[r] = forcing[r * WIDE : (r + 1) * WIDE]
    for r in range(ROWS):
        w_out[r] = f_out[r, pl.ds(8 * STEPS, STEPS, stride=8), :]
        e_out[r] = f_out[r, pl.ds(8 * (LANES - 7 * REGS) + 7, STEPS, stride=8), :]


def last_kernel(inc, f_in, co, from_west, from_east, a_in, b_in, out, f, spare, cl, ct, cc, wide):
    rims = 8 * ROWS
    slots = (a_in.shape[0] - rims) * LANES // (LANES + 8)
    even, pole = position()
    a_base, b_base, a_rows, b_rows = halo_places(even, pole)
    sign = wind_sign(pole, (1, LANES))
    west, east = (pl.ds(0, STEPS, stride=8), pl.ds(8 * (REGS - STEPS) + 7, STEPS, stride=8))

    def halo(ref, rows, base, scale):
        codes = [ref[rims + slots + 8 * t : rims + slots + 8 * t + 1, :] for t in range(slots // LANES)]
        got = scatter(ref[rims : rims + slots, :], jnp.concatenate(codes, 1), rows)
        for k in range(STEPS):
            f[base + k] = got[k * WIDE : (k + 1) * WIDE] * scale
            rim = ref[pl.ds(pl.multiple_of(8 * rows[k], 8), 8), :] * scale
            f[base + k, west, :] = rim[0:STEPS]
            f[base + k, east, :] = rim[STEPS : 2 * STEPS]

    halo(a_in, a_rows, a_base, 1.0)
    halo(b_in, b_rows, b_base, sign)
    for r in range(ROWS):
        f[STEPS + r] = f_in[r]
        f[STEPS + r, west, :] = from_west[r]
        f[STEPS + r, east, :] = from_east[r]
    expand(co, cl, ct, cc)

    def store(r, q, value):
        wide[r, pl.ds(8 - STEPS + q, 8, stride=REGS), :] = value

    diffuse(f, spare, cl, ct, cc, store)
    for r in range(ROWS):
        at = pl.ds(r, LANES, stride=ROWS)
        out[at, :] = inc[at, :] - wide[r, 8 : 8 + LANES, :].T


def call(kernel, outs, args, scratch=(), spaces=None, flops=0, limit=48):
    spaces = spaces or {}
    specs = [pl.BlockSpec(memory_space=spaces.get(n, VMEM)) for n in range(len(args))]
    size = 4 * sum(x.size for x in list(args) + list(outs))
    return pl.pallas_call(
        kernel,
        out_shape=outs,
        in_specs=specs,
        out_specs=[pl.BlockSpec(memory_space=VMEM) for _ in outs],
        scratch_shapes=list(scratch),
        compiler_params=pltpu.CompilerParams(vmem_limit_bytes=limit * MIB),
        cost_estimate=pl.CostEstimate(flops=flops, bytes_accessed=size, transcendentals=0),
    )(*args)


def routes():
    lons, lats = (lax.axis_size("lon"), lax.axis_size("lat"))
    at = lambda lon, lat: lon % lons * lats + lat
    cells = [(lon, lat) for lon in range(lons) for lat in range(lats)]
    inner = [(at(o, a), at(o, a ^ 1)) for o, a in cells]
    outer = []
    for o, a in cells:
        if a in (0, lats - 1):
            outer.append((at(o, a), at(o + lons // 2, a)))
        else:
            outer.append((at(o, a), at(o, a - 1 if a % 2 == 0 else a + 1)))
    east = [(at(o, a), at(o + 1, a)) for o, a in cells]
    west = [(at(o, a), at(o - 1, a)) for o, a in cells]
    return inner, outer, east, west


def local(
    increment, coef_lon, coef_lat, obs_values, obs_weight, obs_operator, obs_columns, obs_types, obs_counts
):
    shape = lambda *dims: jax.ShapeDtypeStruct(dims, F32)
    inner, outer, east, west = routes()
    send = lambda x, route: lax.ppermute(x, ("lon", "lat"), route)
    lats = lax.axis_size("lat")
    slots = obs_values.shape[0]
    bucket = slots // lats
    tiles = slots // LANES
    fields = increment.shape[0]
    inc = increment.reshape(-1, LANES)
    cl = coef_lon.reshape(fields * ROWS, LANES)
    ct = coef_lat.reshape(fields * ROWS, LANES)

    own, coef, b_send, a_send, w_send, e_send = call(
        pack_kernel,
        [
            shape(ROWS, LANES, LANES),
            shape(LANES, LANES),
            shape(STEPS * (LANES + 8), LANES),
            shape(STEPS * (LANES + 8), LANES),
            shape(ROWS + 1, STEPS, LANES),
            shape(ROWS + 1, STEPS, LANES),
        ],
        [inc, cl, ct],
        [
            VMEM(inc.shape, F32),
            VMEM(cl.shape, F32),
            VMEM(ct.shape, F32),
            VMEM((LANES, LANES), F32),
            pltpu.SemaphoreType.DMA((3,)),
        ],
        spaces={0: HBM, 1: HBM, 2: HBM},
    )
    b_in = send(b_send, outer)
    from_west = send(e_send, east)
    from_east = send(w_send, west)
    a_in = send(a_send, inner)
    (slots_send,) = call(
        slots_kernel,
        [shape(lats, 2 * bucket + 8, LANES)],
        [
            obs_counts,
            obs_values.reshape(lats, bucket, LANES),
            obs_weight.reshape(lats, bucket, LANES),
            obs_columns.reshape(1, slots),
            obs_types.reshape(1, slots),
        ],
        spaces={0: pltpu.SMEM},
    )
    slots_in = lax.all_to_all(slots_send, "lat", split_axis=0, concat_axis=0, tiled=True)
    rim_send = jnp.concatenate([from_west, from_east], 1)
    rim_a = send(rim_send, inner)
    rim_b = send(rim_send, outer)
    grid = VMEM((PLANES, WIDE, LANES), F32)
    departures, adjoint, code, w_send, e_send, forcing, co = call(
        middle_kernel,
        [
            shape(slots, LANES),
            shape(slots, LANES),
            shape(8 * tiles, LANES),
            shape(ROWS, STEPS, LANES),
            shape(ROWS, STEPS, LANES),
            shape(ROWS, WIDE, LANES),
            shape(PADDED, LANES),
        ],
        [own, coef, a_in, b_in, from_west, from_east, rim_a, rim_b, slots_in, obs_operator],
        [VMEM((PLANES, PADDED, LANES), F32), VMEM((LANES, LANES), F32)] + [grid] * 5,
        flops=10**8,
    )
    from_west = send(e_send, east)
    from_east = send(w_send, west)
    back = lax.all_to_all(
        departures.reshape(lats, bucket, LANES), "lat", split_axis=0, concat_axis=0, tiled=True
    )
    rims = jnp.concatenate([from_west, from_east], 1).reshape(8 * ROWS, LANES)
    payload = jnp.concatenate([rims, adjoint, code], 0)
    a_in = send(payload, inner)
    b_in = send(payload, outer)
    (gradient,) = call(
        last_kernel,
        [shape(*inc.shape)],
        [inc, forcing, co, from_west, from_east, a_in, b_in],
        [grid] * 5 + [VMEM((ROWS, PADDED, LANES), F32)],
        flops=10**8,
    )
    return (gradient.reshape(increment.shape), back.reshape(slots, LANES))


def solution(mesh):
    return jax.shard_map(
        local,
        mesh=mesh,
        in_specs=(
            P(None, None, "lat", "lon"),
            P(None, "lat", "lon"),
            P(None, "lat", "lon"),
            P(("lon", "lat"), None),
            P(("lon", "lat"), None),
            P(),
            P(("lon", "lat")),
            P(("lon", "lat")),
            P(("lon", "lat")),
        ),
        out_specs=(P(None, None, "lat", "lon"), P(("lon", "lat"), None)),
        check_vma=False,
    )
```

time: 224 us -> 46.1 us (0.21); the launches traced: 226 us -> 45.5 us
  waiting for transfers between devices: 110 us -> 5.41 us
  other arithmetic: 51.1 us -> 0.03 us
  starting transfers between devices: 45.9 us -> 18.3 us
  local copies, waits for them, and re-layouts: 14.3 us -> 3.79 us
  Pallas kernels: 0 us -> 9.42 us
  blocking collectives: 0 us -> 7.85 us
  matrix products: 2.88 us -> 0 us
    ppermute x15 -> x10, waiting for transfers between devices: 104 us -> 4.56 us  [local(): send = lambda x, route: lax.ppermute(x, ('lon', 'lat'), route)]
    mul x18 -> x0, other arithmetic: 38.5 us -> none  [the longest x8 36.1 us: spread_inner(): scaled_lon = root_lon * field_state]
    ppermute x15 -> x10, starting transfers between devices: 29.9 us -> 14.8 us  [local(): send = lambda x, route: lax.ppermute(x, ('lon', 'lat'), route)]
    all_to_all x4 -> x1, starting transfers between devices: 16 us -> 3.51 us  [local(): lax.all_to_all(slots_send, 'lat', split_axis=0, concat_axis=0, tiled=True)]
    pallas_call x0 -> x4, Pallas kernels: none -> 9.42 us  [call(): pl.pallas_call(kernel, out_shape=outs, in_specs=specs, out_specs=[pl.Bloc...]
    slice x14 -> x0, local copies, waits for them, and re-layouts: 7.91 us -> none  [the longest x3 2.55 us: extend(): edge_rows = jnp.stack((wide[:, :, :depth, :], wide[:, :, -depth:, :]))]
    all_to_all x0 -> x1, blocking collectives: none -> 7.85 us  [local(): lax.all_to_all(departures.reshape(lats, bucket, LANES), 'lat', split_axis...]
    all_to_all x4 -> x1, waiting for transfers between devices: 6.16 us -> 0.85 us  [local(): lax.all_to_all(slots_send, 'lat', split_axis=0, concat_axis=0, tiled=True)]
  transfers between devices with their start and end apart: 19 -> 11, of which waited for: 8 -> 3; matrix products, arithmetic and copies ran while one was open for 19% -> 0% of each run, Pallas kernels for 0% -> 3%
where the time goes in v2:
time: 46.1 us; the launch traced here: 45.5 us
  starting transfers between devices  18.3 us (40%)
  Pallas kernels  9.42 us (20%)
  blocking collectives  7.85 us (17%)
  waiting for transfers between devices  5.41 us (12%)
  local copies, waits for them, and re-layouts  3.79 us (8%)
  between operations  0.74 us (2%)
    ppermute x10, starting transfers between devices, local(): send = lambda x, route: lax.ppermute(x, ('lon', 'lat'), route)  14.8 us
    pallas_call x4, Pallas kernels, call(): pl.pallas_call(kernel, out_shape=outs, in_specs=specs, out_specs=[pl.Bloc...  9.42 us
    all_to_all x1, blocking collectives, local(): lax.all_to_all(departures.reshape(lats, bucket, LANES), 'lat', split_axis...  7.85 us
    ppermute x10, waiting for transfers between devices, local(): send = lambda x, route: lax.ppermute(x, ('lon', 'lat'), route)  4.56 us
    unnamed x21, local copies, waits for them, and re-layouts  3.79 us
    all_to_all x1, starting transfers between devices, local(): lax.all_to_all(slots_send, 'lat', split_axis=0, concat_axis=0, tiled=True)  3.51 us
  transfers between devices with their start and end apart: 11, of which 3 were waited for; matrix products, arithmetic and copies ran while one was open for 0% of the time, Pallas kernels for 3%

profile of v2, /device:TPU:0, one launch (start us, length us, event | category | flops | bytes accessed | tf_op | source)
XLA Modules:
  0.0 45.5 jit_solution(14859554618363573761)
XLA Ops:
  0.6 1.0 %copy-done = f32[4,32,8,128]{3,2,1,0:T(8,128)S(1)} copy-done((f32[4,32,8,128]{3,2,1,0:T(8,128)S(1)}, f32[4,32,8,128]{3,2,1,0:T(8,128)}, u32[]{:S(2)}) %copy-start) | copy-done | bytes 524312
  1.7 0.7 %copy-done.5 = f32[4,8,128]{2,1,0:T(8,128)S(1)} copy-done((f32[4,8,128]{2,1,0:T(8,128)S(1)}, f32[4,8,128]{2,1,0:T(8,128)}, u32[]{:S(2)}) %copy-start.5) | copy-done | bytes 16408
  2.4 0.7 %copy-done.6 = f32[4,8,128]{2,1,0:T(8,128)S(1)} copy-done((f32[4,8,128]{2,1,0:T(8,128)S(1)}, f32[4,8,128]{2,1,0:T(8,128)}, u32[]{:S(2)}) %copy-start.6) | copy-done | bytes 16408
  3.1 0.4 shard_map.104
  3.5 0.5 %collective-permute-start = (f32[544,128]{1,0:T(8,128)S(1)}, f32[544,128]{1,0:T(8,128)S(1)}, u32[]{:S(2)}, u32[]{:S(2)}) collective-permute-start(f32[544,128]{1,0:T(8,128)S(1)} %get-tuple-element.17), channel_id=1, source_target_pairs={{0,1},{1,0},{2,3},{3,2},{4,5},{5,4},{6,7},{7,6},{8,9},{9,8},{10,11... | collective-permute-start | bytes 835592 | tf_op jit(solution)/shard_map/ppermute | solution.py:367
  4.0 3.7 %collective-permute-start.1 = (f32[544,128]{1,0:T(8,128)S(1)}, f32[544,128]{1,0:T(8,128)S(1)}, u32[]{:S(2)}, u32[]{:S(2)}) collective-permute-start(f32[544,128]{1,0:T(8,128)S(1)} %get-tuple-element.18), channel_id=1, source_target_pairs={{0,16},{1,2},{2,1},{3,4},{4,3},{5,6},{6,5},{7,23},{8,24},{9,10},{1... | collective-permute-start | bytes 835592 | tf_op jit(solution)/shard_map/ppermute | solution.py:367
  7.7 1.6 %collective-permute-start.2 = (f32[9,4,128]{2,1,0:T(4,128)S(1)}, f32[9,4,128]{2,1,0:T(4,128)S(1)}, u32[]{:S(2)}, u32[]{:S(2)}) collective-permute-start(f32[9,4,128]{2,1,0:T(4,128)S(1)} %get-tuple-element.19), channel_id=1, source_target_pairs={{0,8},{1,9},{2,10},{3,11},{4,12},{5,13},{6,14},{7,15},{8,16},{9,17... | collective-permute-start | bytes 55304 | tf_op jit(solution)/shard_map/ppermute | solution.py:367
  9.3 2.2 %collective-permute-start.3 = (f32[9,4,128]{2,1,0:T(4,128)S(1)}, f32[9,4,128]{2,1,0:T(4,128)S(1)}, u32[]{:S(2)}, u32[]{:S(2)}) collective-permute-start(f32[9,4,128]{2,1,0:T(4,128)S(1)} %get-tuple-element.20), channel_id=1, source_target_pairs={{0,24},{1,25},{2,26},{3,27},{4,28},{5,29},{6,30},{7,31},{8,0},{9,1... | collective-permute-start | bytes 55304 | tf_op jit(solution)/shard_map/ppermute | solution.py:367
  11.6 0.6 %copy-done.7 = s32[8]{0:T(128)S(1)} copy-done((s32[8]{0:T(128)S(1)}, s32[8]{0:T(128)}, u32[]{:S(2)}) %copy-start.7) | copy-done | bytes 56
  12.2 0.0 copy-done.9
  12.2 1.3 %shard_map.105 = f32[8,40,128]{2,1,0:T(8,128)} custom-call(s32[8]{0:T(128)S(1)} %copy-done.7, f32[8,16,128]{2,1,0:T(8,128)S(1)} %bitcast.15, f32[8,16,128]{2,1,0:T(8,128)S(1)} %bitcast.16, s32[1,128]{1,0:T(1,128)S(1)} %bitcast.19, s32[1,128]{1,0:T(1,128)S(1)} %bitcast.20), custom_call_target="tpu_custom_call" | custom-call | bytes 295968 | tf_op jit(solution)/shard_map/pallas_call | solution.py:335
  13.5 3.5 %all-to-all-start = ((f32[8,40,128]{2,1,0:T(8,128)}), f32[8,40,128]{2,1,0:T(8,128)S(1)}, u32[]{:S(2)}, u32[]{:S(2)}) async-start(f32[8,40,128]{2,1,0:T(8,128)} %shard_map.105), calls=%async_computation | async-start | bytes 327680 | tf_op jit(solution)/shard_map/all_to_all | solution.py:413
  17.1 1.7 %collective-permute-start.5 = (f32[9,8,128]{2,1,0:T(8,128)S(1)}, f32[9,8,128]{2,1,0:T(8,128)S(1)}, u32[]{:S(2)}, u32[]{:S(2)}) collective-permute-start(f32[9,8,128]{2,1,0:T(8,128)S(1)} %pad_maximum_fusion.1), channel_id=1, source_target_pairs={{0,16},{1,2},{2,1},{3,4},{4,3},{5,6},{6,5},{7,23},{8,24},{9,10},{1... | collective-permute-start | bytes 110600 | tf_op jit(solution)/shard_map/ppermute | solution.py:367
  18.8 0.4 collective-permute-start.4
  19.2 2.8 %collective-permute-done.5.rim_b = f32[9,8,128]{2,1,0:T(8,128)S(1)} collective-permute-done((f32[9,8,128]{2,1,0:T(8,128)S(1)}, f32[9,8,128]{2,1,0:T(8,128)S(1)}, u32[]{:S(2)}, u32[]{:S(2)}) %collective-permute-start.5) | collective-permute-done | bytes 36896 | tf_op jit(solution)/shard_map/ppermute | solution.py:367
  22.0 0.8 %all-to-all-done.slots_in = f32[8,40,128]{2,1,0:T(8,128)S(1)} async-done(((f32[8,40,128]{2,1,0:T(8,128)}), f32[8,40,128]{2,1,0:T(8,128)S(1)}, u32[]{:S(2)}, u32[]{:S(2)}) %all-to-all-start) | async-done | bytes 163872 | tf_op jit(solution)/shard_map/all_to_all | solution.py:413
  22.9 4.0 %shard_map.106 = (f32[128,128]{1,0:T(8,128)S(1)}, f32[128,128]{1,0:T(8,128)S(1)}, f32[8,128]{1,0:T(8,128)S(1)}, f32[8,4,128]{2,1,0:T(4,128)S(1)}, f32[8,4,128]{2...) custom-call(f32[8,128,128]{2,1,0:T(8,128)S(1)} %get-tuple-element.15.own, ...), custom_call_target="tpu_custom_call" | custom-call | flops 100000000 | bytes 2416640 | tf_op jit(solution)/shard_map/pallas_call | solution.py:335
  26.9 0.0 collective-permute-start.6
  26.9 3.8 %collective-permute-start.7 = (f32[8,4,128]{2,1,0:T(4,128)S(1)}, f32[8,4,128]{2,1,0:T(4,128)S(1)}, u32[]{:S(2)}, u32[]{:S(2)}) collective-permute-start(f32[8,4,128]{2,1,0:T(4,128)S(1)} %get-tuple-element.24), channel_id=1, source_target_pairs={{0,24},{1,25},{2,26},{3,27},{4,28},{5,29},{6,30},{7,31},{8,0},{9,1... | collective-permute-start | bytes 49160 | tf_op jit(solution)/shard_map/ppermute | solution.py:367
  30.7 1.7 %collective-permute-done.6.from_west = f32[8,4,128]{2,1,0:T(4,128)S(1)} collective-permute-done((f32[8,4,128]{2,1,0:T(4,128)S(1)}, f32[8,4,128]{2,1,0:T(4,128)S(1)}, u32[]{:S(2)}, u32[]{:S(2)}) %collective-permute-start.6) | collective-permute-done | bytes 16416 | tf_op jit(solution)/shard_map/ppermute | solution.py:367
  32.5 0.8 %collective-permute-start.9 = (f32[200,128]{1,0:T(8,128)S(1)}, f32[200,128]{1,0:T(8,128)S(1)}, u32[]{:S(2)}, u32[]{:S(2)}) collective-permute-start(f32[200,128]{1,0:T(8,128)S(1)} %pad_maximum_fusion), channel_id=1, source_target_pairs={{0,16},{1,2},{2,1},{3,4},{4,3},{5,6},{6,5},{7,23},{8,24},{9,10},{1... | collective-permute-start | bytes 307208 | tf_op jit(solution)/shard_map/ppermute | solution.py:367
  33.3 7.8 %all_to_all.10 = f32[8,16,128]{2,1,0:T(8,128)S(1)} all-to-all(f32[8,16,128]{2,1,0:T(8,128)S(1)} %bitcast.14), channel_id=1, replica_groups=mesh['lon'=4,'lat'=8] {'lat'}, dimensions={0} | all-to-all | bytes 131072 | tf_op jit(solution)/shard_map/all_to_all | solution.py:435
  41.1 3.7 %shard_map.107 = f32[1024,128]{1,0:T(8,128)} custom-call(f32[1024,128]{1,0:T(8,128)S(1)} %bitcast.13, f32[8,136,128]{2,1,0:T(8,128)S(1)} %get-tuple-element.21.f_in, f32[144,128]{1,0:T(8,128)S(1)} %get-tuple-element.22.co, f32[8,4,128]{2,1,0:T(4,128)S(1)} %collective-permute-done.6.from_west, f32[8,4,128]{2,1,0:T(4,128)S(1)} %collective-permute-done.7.from_east, ...), custom_call_target="tpu_custom_call" | custom-call | flops 100000000 | bytes 1916928 | tf_op jit(solution)/shard_map/pallas_call | solution.py:335
  44.9 0.6 %copy.12 = f32[128,128]{1,0:T(8,128)} copy(f32[128,128]{1,0:T(8,128)S(1)} %bitcast.22) | data formatting | bytes 131072
  (27 shorter events, 0.1 us)
Async XLA Ops:
  0.6 1.0 %copy-start = (f32[4,32,8,128]{3,2,1,0:T(8,128)S(1)}, f32[4,32,8,128]{3,2,1,0:T(8,128)}, u32[]{:S(2)}) copy-start(f32[4,32,8,128]{3,2,1,0:T(8,128)} %param.9) | copy-start | bytes 1572868
  1.7 0.7 %copy-start.5 = (f32[4,8,128]{2,1,0:T(8,128)S(1)}, f32[4,8,128]{2,1,0:T(8,128)}, u32[]{:S(2)}) copy-start(f32[4,8,128]{2,1,0:T(8,128)} %param.10) | copy-start | bytes 49156
  2.4 0.7 %copy-start.6 = (f32[4,8,128]{2,1,0:T(8,128)S(1)}, f32[4,8,128]{2,1,0:T(8,128)}, u32[]{:S(2)}) copy-start(f32[4,8,128]{2,1,0:T(8,128)} %param.11) | copy-start | bytes 49156
  3.1 8.4 %copy-start.3 = (f32[128,128]{1,0:T(8,128)S(1)}, f32[128,128]{1,0:T(8,128)}, u32[]{:S(2)}) copy-start(f32[128,128]{1,0:T(8,128)} %param.12) | copy-start | bytes 196612
  3.1 8.4 %copy-start.4 = (f32[128,128]{1,0:T(8,128)S(1)}, f32[128,128]{1,0:T(8,128)}, u32[]{:S(2)}) copy-start(f32[128,128]{1,0:T(8,128)} %param.13) | copy-start | bytes 196612
  3.5 19.3 %collective-permute-start = (f32[544,128]{1,0:T(8,128)S(1)}, f32[544,128]{1,0:T(8,128)S(1)}, u32[]{:S(2)}, u32[]{:S(2)}) collective-permute-start(f32[544,128]{1,0:T(8,128)S(1)} %get-tuple-element.17), channel_id=1, source_target_pairs={{0,1},{1,0},{2,3},{3,2},{4,5},{5,4},{6,7},{7,6},{8,9},{9,8},{10,11... | collective-permute-start | bytes 835592 | tf_op jit(solution)/shard_map/ppermute | solution.py:367
  4.0 18.8 %collective-permute-start.1 = (f32[544,128]{1,0:T(8,128)S(1)}, f32[544,128]{1,0:T(8,128)S(1)}, u32[]{:S(2)}, u32[]{:S(2)}) collective-permute-start(f32[544,128]{1,0:T(8,128)S(1)} %get-tuple-element.18), channel_id=1, source_target_pairs={{0,16},{1,2},{2,1},{3,4},{4,3},{5,6},{6,5},{7,23},{8,24},{9,10},{1... | collective-permute-start | bytes 835592 | tf_op jit(solution)/shard_map/ppermute | solution.py:367
  7.7 9.3 %collective-permute-start.2 = (f32[9,4,128]{2,1,0:T(4,128)S(1)}, f32[9,4,128]{2,1,0:T(4,128)S(1)}, u32[]{:S(2)}, u32[]{:S(2)}) collective-permute-start(f32[9,4,128]{2,1,0:T(4,128)S(1)} %get-tuple-element.19), channel_id=1, source_target_pairs={{0,8},{1,9},{2,10},{3,11},{4,12},{5,13},{6,14},{7,15},{8,16},{9,17... | collective-permute-start | bytes 55304 | tf_op jit(solution)/shard_map/ppermute | solution.py:367
  9.3 7.8 %collective-permute-start.3 = (f32[9,4,128]{2,1,0:T(4,128)S(1)}, f32[9,4,128]{2,1,0:T(4,128)S(1)}, u32[]{:S(2)}, u32[]{:S(2)}) collective-permute-start(f32[9,4,128]{2,1,0:T(4,128)S(1)} %get-tuple-element.20), channel_id=1, source_target_pairs={{0,24},{1,25},{2,26},{3,27},{4,28},{5,29},{6,30},{7,31},{8,0},{9,1... | collective-permute-start | bytes 55304 | tf_op jit(solution)/shard_map/ppermute | solution.py:367
  11.5 0.7 %copy-start.7 = (s32[8]{0:T(128)S(1)}, s32[8]{0:T(128)}, u32[]{:S(2)}) copy-start(s32[8]{0:T(128)} %counts.1) | copy-start | bytes 100
  11.5 0.7 %copy-start.8 = (s32[128]{0:T(128)S(1)}, s32[128]{0:T(128)}, u32[]{:S(2)}) copy-start(s32[128]{0:T(128)} %param.15) | copy-start | bytes 1540
  11.5 0.7 %copy-start.9 = (s32[128]{0:T(128)S(1)}, s32[128]{0:T(128)}, u32[]{:S(2)}) copy-start(s32[128]{0:T(128)} %param.16) | copy-start | bytes 1540
  13.5 9.3 %copy-start.2 = (f32[3,128,128]{2,1,0:T(8,128)S(1)}, f32[3,128,128]{2,1,0:T(8,128)}, u32[]{:S(2)}) copy-start(f32[3,128,128]{2,1,0:T(8,128)} %operator.1) | copy-start | bytes 589828
  13.5 9.3 %all-to-all-start = ((f32[8,40,128]{2,1,0:T(8,128)}), f32[8,40,128]{2,1,0:T(8,128)S(1)}, u32[]{:S(2)}, u32[]{:S(2)}) async-start(f32[8,40,128]{2,1,0:T(8,128)} %shard_map.105), calls=%async_computation | async-start | bytes 327680 | tf_op jit(solution)/shard_map/all_to_all | solution.py:413
  17.1 4.9 %collective-permute-start.5 = (f32[9,8,128]{2,1,0:T(8,128)S(1)}, f32[9,8,128]{2,1,0:T(8,128)S(1)}, u32[]{:S(2)}, u32[]{:S(2)}) collective-permute-start(f32[9,8,128]{2,1,0:T(8,128)S(1)} %pad_maximum_fusion.1), channel_id=1, source_target_pairs={{0,16},{1,2},{2,1},{3,4},{4,3},{5,6},{6,5},{7,23},{8,24},{9,10},{1... | collective-permute-start | bytes 110600 | tf_op jit(solution)/shard_map/ppermute | solution.py:367
  18.8 3.2 %collective-permute-start.4 = (f32[9,8,128]{2,1,0:T(8,128)S(1)}, f32[9,8,128]{2,1,0:T(8,128)S(1)}, u32[]{:S(2)}, u32[]{:S(2)}) collective-permute-start(f32[9,8,128]{2,1,0:T(8,128)S(1)} %pad_maximum_fusion.1), channel_id=1, source_target_pairs={{0,1},{1,0},{2,3},{3,2},{4,5},{5,4},{6,7},{7,6},{8,9},{9,8},{10,11... | collective-permute-start | bytes 110600 | tf_op jit(solution)/shard_map/ppermute | solution.py:367
  22.9 18.3 %copy-start.1 = (f32[4,32,8,128]{3,2,1,0:T(8,128)S(1)}, f32[4,32,8,128]{3,2,1,0:T(8,128)}, u32[]{:S(2)}) copy-start(f32[4,32,8,128]{3,2,1,0:T(8,128)} %param.9) | copy-start | bytes 1572868
  26.9 5.6 %collective-permute-start.6 = (f32[8,4,128]{2,1,0:T(4,128)S(1)}, f32[8,4,128]{2,1,0:T(4,128)S(1)}, u32[]{:S(2)}, u32[]{:S(2)}) collective-permute-start(f32[8,4,128]{2,1,0:T(4,128)S(1)} %get-tuple-element.23), channel_id=1, source_target_pairs={{0,8},{1,9},{2,10},{3,11},{4,12},{5,13},{6,14},{7,15},{8,16},{9,17... | collective-permute-start | bytes 49160 | tf_op jit(solution)/shard_map/ppermute | solution.py:367
  26.9 5.5 %collective-permute-start.7 = (f32[8,4,128]{2,1,0:T(4,128)S(1)}, f32[8,4,128]{2,1,0:T(4,128)S(1)}, u32[]{:S(2)}, u32[]{:S(2)}) collective-permute-start(f32[8,4,128]{2,1,0:T(4,128)S(1)} %get-tuple-element.24), channel_id=1, source_target_pairs={{0,24},{1,25},{2,26},{3,27},{4,28},{5,29},{6,30},{7,31},{8,0},{9,1... | collective-permute-start | bytes 49160 | tf_op jit(solution)/shard_map/ppermute | solution.py:367
  32.5 8.7 %collective-permute-start.9 = (f32[200,128]{1,0:T(8,128)S(1)}, f32[200,128]{1,0:T(8,128)S(1)}, u32[]{:S(2)}, u32[]{:S(2)}) collective-permute-start(f32[200,128]{1,0:T(8,128)S(1)} %pad_maximum_fusion), channel_id=1, source_target_pairs={{0,16},{1,2},{2,1},{3,4},{4,3},{5,6},{6,5},{7,23},{8,24},{9,10},{1... | collective-permute-start | bytes 307208 | tf_op jit(solution)/shard_map/ppermute | solution.py:367
  33.3 7.9 %collective-permute-start.8 = (f32[200,128]{1,0:T(8,128)S(1)}, f32[200,128]{1,0:T(8,128)S(1)}, u32[]{:S(2)}, u32[]{:S(2)}) collective-permute-start(f32[200,128]{1,0:T(8,128)S(1)} %pad_maximum_fusion), channel_id=1, source_target_pairs={{0,1},{1,0},{2,3},{3,2},{4,5},{5,4},{6,7},{7,6},{8,9},{9,8},{10,11... | collective-permute-start | bytes 307208 | tf_op jit(solution)/shard_map/ppermute | solution.py:367

commit v3 on v2

--- a/solution.py
+++ b/solution.py
@@ -17,6 +17,7 @@
 VMEM = pltpu.VMEM
 HBM = pltpu.HBM
 MIB = 1 << 20
+LONG = 10**10
 F32 = jnp.float32
 
 
@@ -63,14 +64,26 @@
     return x[:, :LANES] + x[:, LANES:]
 
 
-def pack_kernel(inc_hbm, cl_hbm, ct_hbm, own, coef, b_out, a_out, w_out, e_out, inc, cl, ct, raw, sems):
-    copies = [
-        pltpu.make_async_copy(src, dst, sems.at[n])
-        for n, (src, dst) in enumerate(((inc_hbm, inc), (cl_hbm, cl), (ct_hbm, ct)))
-    ]
+def pack_kernel(
+    inc_hbm, cl_hbm, ct_hbm, values, weights, columns_hbm, types_hbm, counts_hbm,
+    own, coef, b_out, a_out, rim_out, w_out, e_out, slots_out,
+    inc, cl, ct, raw, columns, types, counts, sems,
+):
+    owners, bucket = (slots_out.shape[0], values.shape[1])
+    moves = (
+        (inc_hbm, inc),
+        (cl_hbm, cl),
+        (ct_hbm, ct),
+        (columns_hbm, columns),
+        (types_hbm, types),
+        (counts_hbm, counts),
+        (values, slots_out.at[:, pl.ds(0, bucket), :]),
+        (weights, slots_out.at[:, pl.ds(bucket, bucket), :]),
+    )
+    copies = [pltpu.make_async_copy(src, dst, sems.at[n]) for n, (src, dst) in enumerate(moves)]
     for copy in copies:
         copy.start()
-    for copy in copies:
+    for copy in copies[:3]:
         copy.wait()
     fields = cl.shape[0] // ROWS
     even, _ = position()
@@ -92,27 +105,59 @@
             out[k * LANES : (k + 1) * LANES, :] = own[first + k]
             at = STEPS * LANES + 8 * k
             out[at : at + 8, :] = raw[pl.ds(pl.multiple_of(8 * (STEPS + first + k), 8), 8), :]
-
-
-def slots_kernel(counts, values, weights, columns, types, out):
-    owners, bucket = (out.shape[0], values.shape[1])
+    rim = jnp.concatenate([coef[0:STEPS, :], coef[LANES - STEPS : LANES, :]], 0)
+    rim_out[STEPS] = rim
+    a_out[STEPS * (LANES + 16) : STEPS * (LANES + 16) + 8, :] = rim
+    for k in range(STEPS):
+        rim_out[k, 0:STEPS, :] = own[b_row + k, 0:STEPS, :]
+        rim_out[k, STEPS : 2 * STEPS, :] = own[b_row + k, LANES - STEPS : LANES, :]
+        at = STEPS * (LANES + 8) + 8 * k
+        a_out[at : at + STEPS, :] = own[a_row + k, 0:STEPS, :]
+        a_out[at + STEPS : at + 2 * STEPS, :] = own[a_row + k, LANES - STEPS : LANES, :]
+    for copy in copies[3:]:
+        copy.wait()
     slots = columns.shape[1]
     lane = iota((1, slots), 1)
     limit = jnp.zeros((1, slots), jnp.int32)
     for d in range(owners):
         limit = jnp.where(lane // bucket == d, counts[d], limit)
     code = jnp.where(lane % bucket < limit, columns[...] * 4 + types[...], -1).astype(F32)
-    out[:, 0:bucket, :] = values[...]
-    out[:, bucket : 2 * bucket, :] = weights[...]
     for d in range(owners):
         at = d * bucket
         window = code[:, at // LANES * LANES : at // LANES * LANES + LANES]
         moved = pltpu.roll(window, (-at) % LANES, 1)
-        out[d, 2 * bucket : 2 * bucket + 8, :] = jnp.broadcast_to(moved, (8, LANES))
-
-
-def coefs_wide(coef, a_in, b_in, from_west, from_east, rim_a, rim_b, raw, co_out, even, pole):
+        slots_out[d, 2 * bucket : 2 * bucket + 8, :] = jnp.broadcast_to(moved, (8, LANES))
+
+
+def edge_kernel(w_own, e_own, a_in, rim_b, w_out, e_out):
+    even, pole = position()
     a_base, b_base, _, b_rows = halo_places(even, pole)
+    sign = wind_sign(pole, (1, LANES))
+    at = STEPS * (LANES + 8)
+    for k in range(STEPS):
+        rim = a_in[at + 8 * k : at + 8 * k + 8, :]
+        w_out[a_base + k] = rim[0:STEPS]
+        e_out[a_base + k] = rim[STEPS : 2 * STEPS]
+        rim = rim_b[jnp.where(pole, STEPS - 1 - k, k)] * sign
+        w_out[b_base + k] = rim[0:STEPS]
+        e_out[b_base + k] = rim[STEPS : 2 * STEPS]
+    for r in range(ROWS):
+        w_out[STEPS + r] = w_own[r]
+        e_out[STEPS + r] = e_own[r]
+    at += 8 * STEPS
+    plane = iota((8, LANES), 1) // 8
+    tile = jnp.concatenate([w_own[ROWS], e_own[ROWS]], 0)
+    from_a = pltpu.roll(a_in[at : at + 8, :], LANES // 2, 1)
+    tile = jnp.where(plane // STEPS == a_base // STEPS, from_a, tile)
+    for k in range(STEPS):
+        shift = (8 * (b_base + k - STEPS - b_rows[k]) + 2 * LANES) % LANES
+        tile = jnp.where(plane == b_base + k, pltpu.roll(rim_b[STEPS], shift, 1), tile)
+    w_out[PLANES] = tile[0:STEPS]
+    e_out[PLANES] = tile[STEPS : 2 * STEPS]
+
+
+def coefs_wide(coef, a_in, b_in, from_west, from_east, raw, co_out, even, pole):
+    a_base, b_base, _, _ = halo_places(even, pole)
     raw[...] = jnp.zeros(raw.shape, F32)
     for k in range(STEPS):
         kk = jnp.where(pole, STEPS - 1 - k, k)
@@ -120,14 +165,8 @@
         raw[pl.ds(pl.multiple_of(8 * (a_base + k), 8), 8), :] = a_in[at + 8 * k : at + 8 * k + 8, :]
         raw[pl.ds(pl.multiple_of(8 * (b_base + k), 8), 8), :] = b_in[pl.ds(pl.multiple_of(at + 8 * kk, 8), 8), :]
     co_out[8 : 8 + LANES, :] = raw[...].T + coef[...]
-    tile = jnp.concatenate([from_west[ROWS], from_east[ROWS]], 0)
-    plane = iota((8, LANES), 1) // 8
-    tile = jnp.where(plane // STEPS == a_base // STEPS, pltpu.roll(rim_a[ROWS], LANES // 2, 1), tile)
-    for k in range(STEPS):
-        shift = (8 * (b_base + k - STEPS - b_rows[k]) + 2 * LANES) % LANES
-        tile = jnp.where(plane == b_base + k, pltpu.roll(rim_b[ROWS], shift, 1), tile)
-    co_out[8 - STEPS : 8, :] = tile[0:STEPS]
-    co_out[8 + LANES : 8 + LANES + STEPS, :] = tile[STEPS : 2 * STEPS]
+    co_out[8 - STEPS : 8, :] = from_west[PLANES]
+    co_out[8 + LANES : 8 + LANES + STEPS, :] = from_east[PLANES]
 
 
 def expand(co, cl, ct, cc):
@@ -147,9 +186,9 @@
         cc[p] = 1.0 - 2.0 * (a * a + b * b)
 
 
-def diffuse(f, spare, cl, ct, cc, store=None):
+def diffuse(f, spare, cl, ct, cc, store):
     for step in range(STEPS):
-        last = step == STEPS - 1 and store is not None
+        last = step == STEPS - 1
 
         def row(p, carry, f=f, spare=spare, last=last):
             regs = [pl.ds(8 * q, 8) for q in range(REGS)]
@@ -196,31 +235,27 @@
 
 
 def middle_kernel(
-    own, coef, a_in, b_in, from_west, from_east, rim_a, rim_b, slots_in, operator,
-    dep_out, adj_out, code_out, w_out, e_out, f_out, co_out,
-    wide, raw, f, spare, cl, ct, cc,
+    own, coef, a_in, b_in, from_west, from_east, slots_in, operator,
+    dep_out, adj_out, code_out, w_out, e_out, f_out, co,
+    wide, raw, f, spare, cl, ct, cc, state,
 ):
     owners, bucket = (slots_in.shape[0], (slots_in.shape[1] - 8) // 2)
     slots = owners * bucket
     even, pole = position()
-    a_base, b_base, a_rows, b_rows = halo_places(even, pole)
+    a_base, b_base, _, _ = halo_places(even, pole)
     sign = wind_sign(pole, (1, LANES))
     inner = slice(8, 8 + LANES)
-    west, east = (slice(8 - STEPS, 8), slice(8 + LANES, 8 + LANES + STEPS))
-    coefs_wide(coef, a_in, b_in, from_west, from_east, rim_a, rim_b, raw, co_out, even, pole)
-    expand(co_out, cl, ct, cc)
+    coefs_wide(coef, a_in, b_in, from_west, from_east, raw, co, even, pole)
+    expand(co, cl, ct, cc)
     for k in range(STEPS):
         wide[a_base + k, inner, :] = a_in[k * LANES : (k + 1) * LANES, :]
-        wide[a_base + k, west, :] = rim_a[a_rows[k], 0:STEPS, :]
-        wide[a_base + k, east, :] = rim_a[a_rows[k], STEPS : 2 * STEPS, :]
         at = pl.multiple_of(jnp.where(pole, STEPS - 1 - k, k) * LANES, LANES)
         wide[b_base + k, inner, :] = b_in[pl.ds(at, LANES), :] * sign
-        wide[b_base + k, west, :] = rim_b[b_rows[k], 0:STEPS, :] * sign
-        wide[b_base + k, east, :] = rim_b[b_rows[k], STEPS : 2 * STEPS, :] * sign
     for r in range(ROWS):
         wide[STEPS + r, inner, :] = own[r]
-        wide[STEPS + r, west, :] = from_west[r]
-        wide[STEPS + r, east, :] = from_east[r]
+    for p in range(PLANES):
+        wide[p, 8 - STEPS : 8, :] = from_west[p]
+        wide[p, 8 + LANES : 8 + LANES + STEPS, :] = from_east[p]
 
     def interleave(p, carry):
         for q in range(REGS):
@@ -228,7 +263,11 @@
         return carry
 
     lax.fori_loop(0, PLANES, interleave, 0)
-    diffuse(f, spare, cl, ct, cc)
+
+    def store(r, q, value):
+        state[r, pl.ds(8 * q, 8), :] = value
+
+    diffuse(f, spare, cl, ct, cc, store)
 
     lane = iota((1, LANES), 1)
     per_tile = LANES // bucket
@@ -256,9 +295,9 @@
         ],
         1,
     )
-    state = jnp.concatenate(split(f[STEPS : STEPS + ROWS].reshape(depth, LANES)), 1)
-    state = jnp.concatenate([state, jnp.zeros((padded - depth, 2 * LANES), jnp.bfloat16)], 0)
-    column = halves(matmul(hot, state))
+    cells = jnp.concatenate(split(state[...].reshape(depth, LANES)), 1)
+    cells = jnp.concatenate([cells, jnp.zeros((padded - depth, 2 * LANES), jnp.bfloat16)], 0)
+    column = halves(matmul(hot, cells))
 
     masks = [kind == n for n in range(3)]
     op_high, op_low = split(operator[...])
@@ -294,7 +333,7 @@
         e_out[r] = f_out[r, pl.ds(8 * (LANES - 7 * REGS) + 7, STEPS, stride=8), :]
 
 
-def last_kernel(inc, f_in, co, from_west, from_east, a_in, b_in, out, f, spare, cl, ct, cc, wide):
+def last_kernel(inc, f_in, cl, ct, cc, from_west, from_east, a_in, b_in, out, f, spare, wide):
     rims = 8 * ROWS
     slots = (a_in.shape[0] - rims) * LANES // (LANES + 8)
     even, pole = position()
@@ -317,7 +356,6 @@
         f[STEPS + r] = f_in[r]
         f[STEPS + r, west, :] = from_west[r]
         f[STEPS + r, east, :] = from_east[r]
-    expand(co, cl, ct, cc)
 
     def store(r, q, value):
         wide[r, pl.ds(8 - STEPS + q, 8, stride=REGS), :] = value
@@ -328,10 +366,11 @@
         out[at, :] = inc[at, :] - wide[r, 8 : 8 + LANES, :].T
 
 
-def call(kernel, outs, args, scratch=(), spaces=None, flops=0, limit=48):
+def call(kernel, outs, args, scratch=(), spaces=None, flops=0, limit=20):
     spaces = spaces or {}
     specs = [pl.BlockSpec(memory_space=spaces.get(n, VMEM)) for n in range(len(args))]
     size = 4 * sum(x.size for x in list(args) + list(outs))
+    args = [pltpu.with_memory_space_constraint(x, HBM) if spaces.get(n) is HBM else x for n, x in enumerate(args)]
     return pl.pallas_call(
         kernel,
         out_shape=outs,
@@ -374,47 +413,50 @@
     cl = coef_lon.reshape(fields * ROWS, LANES)
     ct = coef_lat.reshape(fields * ROWS, LANES)
 
-    own, coef, b_send, a_send, w_send, e_send = call(
+    own, coef, b_send, a_send, rim_send, w_own, e_own, slots_send = call(
         pack_kernel,
         [
             shape(ROWS, LANES, LANES),
             shape(LANES, LANES),
             shape(STEPS * (LANES + 8), LANES),
-            shape(STEPS * (LANES + 8), LANES),
+            shape(STEPS * (LANES + 16) + 8, LANES),
+            shape(STEPS + 1, 8, LANES),
             shape(ROWS + 1, STEPS, LANES),
             shape(ROWS + 1, STEPS, LANES),
-        ],
-        [inc, cl, ct],
+            shape(lats, 2 * bucket + 8, LANES),
+        ],
+        [
+            inc,
+            cl,
+            ct,
+            obs_values.reshape(lats, bucket, LANES),
+            obs_weight.reshape(lats, bucket, LANES),
+            obs_columns.reshape(1, slots),
+            obs_types.reshape(1, slots),
+            obs_counts,
+        ],
         [
             VMEM(inc.shape, F32),
             VMEM(cl.shape, F32),
             VMEM(ct.shape, F32),
             VMEM((LANES, LANES), F32),
-            pltpu.SemaphoreType.DMA((3,)),
-        ],
-        spaces={0: HBM, 1: HBM, 2: HBM},
-    )
+            VMEM((1, slots), jnp.int32),
+            VMEM((1, slots), jnp.int32),
+            pltpu.SMEM(obs_counts.shape, jnp.int32),
+            pltpu.SemaphoreType.DMA((8,)),
+        ],
+        spaces={n: HBM for n in range(8)},
+    )
+    rim_b = send(rim_send, outer)
+    a_in = send(a_send, inner)
     b_in = send(b_send, outer)
+    slots_in = lax.all_to_all(slots_send, "lat", split_axis=0, concat_axis=0, tiled=True)
+    edge = shape(PLANES + 1, STEPS, LANES)
+    w_send, e_send = call(edge_kernel, [edge, edge], [w_own, e_own, a_in, rim_b])
     from_west = send(e_send, east)
     from_east = send(w_send, west)
-    a_in = send(a_send, inner)
-    (slots_send,) = call(
-        slots_kernel,
-        [shape(lats, 2 * bucket + 8, LANES)],
-        [
-            obs_counts,
-            obs_values.reshape(lats, bucket, LANES),
-            obs_weight.reshape(lats, bucket, LANES),
-            obs_columns.reshape(1, slots),
-            obs_types.reshape(1, slots),
-        ],
-        spaces={0: pltpu.SMEM},
-    )
-    slots_in = lax.all_to_all(slots_send, "lat", split_axis=0, concat_axis=0, tiled=True)
-    rim_send = jnp.concatenate([from_west, from_east], 1)
-    rim_a = send(rim_send, inner)
-    rim_b = send(rim_send, outer)
     grid = VMEM((PLANES, WIDE, LANES), F32)
+    planes = shape(PLANES, WIDE, LANES)
     departures, adjoint, code, w_send, e_send, forcing, co = call(
         middle_kernel,
         [
@@ -426,8 +468,10 @@
             shape(ROWS, WIDE, LANES),
             shape(PADDED, LANES),
         ],
-        [own, coef, a_in, b_in, from_west, from_east, rim_a, rim_b, slots_in, obs_operator],
-        [VMEM((PLANES, PADDED, LANES), F32), VMEM((LANES, LANES), F32)] + [grid] * 5,
+        [own, coef, a_in, b_in, from_west, from_east, slots_in, obs_operator],
+        [VMEM((PLANES, PADDED, LANES), F32), VMEM((LANES, LANES), F32)]
+        + [grid] * 5
+        + [VMEM((ROWS, WIDE, LANES), F32)],
         flops=10**8,
     )
     from_west = send(e_send, east)
@@ -439,13 +483,15 @@
     payload = jnp.concatenate([rims, adjoint, code], 0)
     a_in = send(payload, inner)
     b_in = send(payload, outer)
+    wl, wt, wc = call(expand, [planes, planes, planes], [co], flops=10**8)
     (gradient,) = call(
         last_kernel,
         [shape(*inc.shape)],
-        [inc, forcing, co, from_west, from_east, a_in, b_in],
-        [grid] * 5 + [VMEM((ROWS, PADDED, LANES), F32)],
-        flops=10**8,
-    )
+        [inc, forcing, wl, wt, wc, from_west, from_east, a_in, b_in],
+        [grid] * 2 + [VMEM((ROWS, PADDED, LANES), F32)],
+        flops=LONG,
+    )
+    gradient, back = lax.optimization_barrier((gradient, back))
     return (gradient.reshape(increment.shape), back.reshape(slots, LANES))
 
 

time: 46.1 us -> 42.6 us (0.924)
  blocking collectives: 7.85 us -> 0 us
  waiting for transfers between devices: 5.41 us -> 9.39 us
  local copies, waits for them, and re-layouts: 3.79 us -> 0.64 us
  starting transfers between devices: 18.3 us -> 21.4 us
  Pallas kernels: 9.42 us -> 10.2 us
    all_to_all x1 -> x0, blocking collectives: 7.85 us -> none  [local(): lax.all_to_all(departures.reshape(lats, bucket, LANES), 'lat', split_axis...]
    ppermute x10 -> x9, waiting for transfers between devices: 4.56 us -> 8.96 us  [local(): send = lambda x, route: lax.ppermute(x, ('lon', 'lat'), route)]
    all_to_all x0 -> x1, starting transfers between devices: none -> 3.35 us  [local(): lax.all_to_all(departures.reshape(lats, bucket, LANES), 'lat', split_axis...]
    unnamed x21 -> x5, local copies, waits for them, and re-layouts: 3.79 us -> 0.64 us
    all_to_all x1, waiting for transfers between devices: 0.85 us -> 0.01 us  [local(): lax.all_to_all(slots_send, 'lat', split_axis=0, concat_axis=0, tiled=True)]
    pallas_call x4 -> x5, Pallas kernels: 9.42 us -> 10.2 us  [call(): pl.pallas_call(kernel, out_shape=outs, in_specs=specs, out_specs=[pl.Bloc...]
    ppermute x10 -> x9, starting transfers between devices: 14.8 us -> 14.6 us  [local(): send = lambda x, route: lax.ppermute(x, ('lon', 'lat'), route)]
  transfers between devices with their start and end apart: 11 -> 11, of which waited for: 3 -> 6; matrix products, arithmetic and copies ran while one was open for 0% -> 0% of each run, Pallas kernels for 3% -> 9%
where the time goes in v3:
time: 42.6 us; the launch traced here: 42.3 us
  starting transfers between devices  21.4 us (50%)
  Pallas kernels  10.2 us (24%)
  waiting for transfers between devices  9.39 us (22%)
  between operations  0.69 us (2%)
  local copies, waits for them, and re-layouts  0.64 us (2%)
    ppermute x9, starting transfers between devices, local(): send = lambda x, route: lax.ppermute(x, ('lon', 'lat'), route)  14.6 us
    pallas_call x5, Pallas kernels, call(): pl.pallas_call(kernel, out_shape=outs, in_specs=specs, out_specs=[pl.Bloc...  10.2 us
    ppermute x9, waiting for transfers between devices, local(): send = lambda x, route: lax.ppermute(x, ('lon', 'lat'), route)  8.96 us
    all_to_all x1, starting transfers between devices, local(): lax.all_to_all(slots_send, 'lat', split_axis=0, concat_axis=0, tiled=True)  3.48 us
    all_to_all x1, starting transfers between devices, local(): lax.all_to_all(departures.reshape(lats, bucket, LANES), 'lat', split_axis...  3.35 us
  transfers between devices with their start and end apart: 11, of which 6 were waited for; matrix products, arithmetic and copies ran while one was open for 0% of the time, Pallas kernels for 9%

profile of v3, /device:TPU:0, one launch (start us, length us, event | category | flops | bytes accessed | tf_op | source)
XLA Modules:
  0.0 42.3 jit_solution(14416050190611987844)
XLA Ops:
  0.6 2.3 %shard_map.104 = (f32[8,128,128]{2,1,0:T(8,128)S(1)}, f32[128,128]{1,0:T(8,128)S(1)}, f32[544,128]{1,0:T(8,128)S(1)}, f32[584,128]{1,0:T(8,128)S(1)}, f32[5,8,12...) custom-call(f32[1024,128]{1,0:T(8,128)} %bitcast.12, ...), custom_call_target="tpu_custom_call" | custom-call | bytes 2077728 | tf_op jit(solution)/shard_map/pallas_call | solution.py:374
  2.9 0.5 %collective-permute-start = (f32[584,128]{1,0:T(8,128)S(1)}, f32[584,128]{1,0:T(8,128)S(1)}, u32[]{:S(2)}, u32[]{:S(2)}) collective-permute-start(f32[584,128]{1,0:T(8,128)S(1)} %get-tuple-element.26), channel_id=1, source_target_pairs={{0,1},{1,0},{2,3},{3,2},{4,5},{5,4},{6,7},{7,6},{8,9},{9,8},{10,11... | collective-permute-start | bytes 897032 | tf_op jit(solution)/shard_map/ppermute | solution.py:406
  3.5 3.7 %collective-permute-start.1 = (f32[544,128]{1,0:T(8,128)S(1)}, f32[544,128]{1,0:T(8,128)S(1)}, u32[]{:S(2)}, u32[]{:S(2)}) collective-permute-start(f32[544,128]{1,0:T(8,128)S(1)} %get-tuple-element.27), channel_id=1, source_target_pairs={{0,16},{1,2},{2,1},{3,4},{4,3},{5,6},{6,5},{7,23},{8,24},{9,10},{1... | collective-permute-start | bytes 835592 | tf_op jit(solution)/shard_map/ppermute | solution.py:406
  7.1 3.5 %all-to-all-start = ((f32[8,40,128]{2,1,0:T(8,128)}), f32[8,40,128]{2,1,0:T(8,128)S(1)}, u32[]{:S(2)}, u32[]{:S(2)}) async-start(f32[8,40,128]{2,1,0:T(8,128)} %get-tuple-element.33), calls=%async_computation | async-start | bytes 327680 | tf_op jit(solution)/shard_map/all_to_all | solution.py:453
  10.6 0.8 %collective-permute-start.2 = (f32[5,8,128]{2,1,0:T(8,128)S(1)}, f32[5,8,128]{2,1,0:T(8,128)S(1)}, u32[]{:S(2)}, u32[]{:S(2)}) collective-permute-start(f32[5,8,128]{2,1,0:T(8,128)S(1)} %get-tuple-element.30), channel_id=1, source_target_pairs={{0,16},{1,2},{2,1},{3,4},{4,3},{5,6},{6,5},{7,23},{8,24},{9,10},{1... | collective-permute-start | bytes 61448 | tf_op jit(solution)/shard_map/ppermute | solution.py:406
  11.4 3.9 %collective-permute-done.2.rim_b = f32[5,8,128]{2,1,0:T(8,128)S(1)} collective-permute-done((f32[5,8,128]{2,1,0:T(8,128)S(1)}, f32[5,8,128]{2,1,0:T(8,128)S(1)}, u32[]{:S(2)}, u32[]{:S(2)}) %collective-permute-start.2) | collective-permute-done | bytes 20512 | tf_op jit(solution)/shard_map/ppermute | solution.py:406
  15.3 0.0 collective-permute-done.a_in
  15.3 0.1 shard_map.105
  15.4 1.6 %collective-permute-start.3 = (f32[17,4,128]{2,1,0:T(4,128)S(1)}, f32[17,4,128]{2,1,0:T(4,128)S(1)}, u32[]{:S(2)}, u32[]{:S(2)}) collective-permute-start(f32[17,4,128]{2,1,0:T(4,128)S(1)} %get-tuple-element.31), channel_id=1, source_target_pairs={{0,8},{1,9},{2,10},{3,11},{4,12},{5,13},{6,14},{7,15},{8,16},{9,17... | collective-permute-start | bytes 104456 | tf_op jit(solution)/shard_map/ppermute | solution.py:406
  17.0 2.2 %collective-permute-start.4 = (f32[17,4,128]{2,1,0:T(4,128)S(1)}, f32[17,4,128]{2,1,0:T(4,128)S(1)}, u32[]{:S(2)}, u32[]{:S(2)}) collective-permute-start(f32[17,4,128]{2,1,0:T(4,128)S(1)} %get-tuple-element.32), channel_id=1, source_target_pairs={{0,24},{1,25},{2,26},{3,27},{4,28},{5,29},{6,30},{7,31},{8,0},{9,1... | collective-permute-start | bytes 104456 | tf_op jit(solution)/shard_map/ppermute | solution.py:406
  19.2 2.2 %collective-permute-done.3.from_west = f32[17,4,128]{2,1,0:T(4,128)S(1)} collective-permute-done((f32[17,4,128]{2,1,0:T(4,128)S(1)}, f32[17,4,128]{2,1,0:T(4,128)S(1)}, u32[]{:S(2)}, u32[]{:S(2)}) %collective-permute-start.3) | collective-permute-done | bytes 34848 | tf_op jit(solution)/shard_map/ppermute | solution.py:406
  21.5 0.4 %collective-permute-done.4.from_east = f32[17,4,128]{2,1,0:T(4,128)S(1)} collective-permute-done((f32[17,4,128]{2,1,0:T(4,128)S(1)}, f32[17,4,128]{2,1,0:T(4,128)S(1)}, u32[]{:S(2)}, u32[]{:S(2)}) %collective-permute-start.4) | collective-permute-done | bytes 34848 | tf_op jit(solution)/shard_map/ppermute | solution.py:406
  21.9 4.0 %shard_map.106 = (f32[128,128]{1,0:T(8,128)}, f32[128,128]{1,0:T(8,128)S(1)}, f32[8,128]{1,0:T(8,128)S(1)}, f32[8,4,128]{2,1,0:T(4,128)S(1)}, f32[8,4,128]{2,1,0...) custom-call(f32[8,128,128]{2,1,0:T(8,128)S(1)} %get-tuple-element.24.own, ...), custom_call_target="tpu_custom_call" | custom-call | flops 100000000 | bytes 2396160 | tf_op jit(solution)/shard_map/pallas_call | solution.py:374
  25.9 0.8 %collective-permute-start.5 = (f32[8,4,128]{2,1,0:T(4,128)S(1)}, f32[8,4,128]{2,1,0:T(4,128)S(1)}, u32[]{:S(2)}, u32[]{:S(2)}) collective-permute-start(f32[8,4,128]{2,1,0:T(4,128)S(1)} %get-tuple-element.39), channel_id=1, source_target_pairs={{0,8},{1,9},{2,10},{3,11},{4,12},{5,13},{6,14},{7,15},{8,16},{9,17... | collective-permute-start | bytes 49160 | tf_op jit(solution)/shard_map/ppermute | solution.py:406
  26.7 3.1 %collective-permute-start.6 = (f32[8,4,128]{2,1,0:T(4,128)S(1)}, f32[8,4,128]{2,1,0:T(4,128)S(1)}, u32[]{:S(2)}, u32[]{:S(2)}) collective-permute-start(f32[8,4,128]{2,1,0:T(4,128)S(1)} %get-tuple-element.40), channel_id=1, source_target_pairs={{0,24},{1,25},{2,26},{3,27},{4,28},{5,29},{6,30},{7,31},{8,0},{9,1... | collective-permute-start | bytes 49160 | tf_op jit(solution)/shard_map/ppermute | solution.py:406
  29.8 1.7 %collective-permute-done.5.from_west = f32[8,4,128]{2,1,0:T(4,128)S(1)} collective-permute-done((f32[8,4,128]{2,1,0:T(4,128)S(1)}, f32[8,4,128]{2,1,0:T(4,128)S(1)}, u32[]{:S(2)}, u32[]{:S(2)}) %collective-permute-start.5) | collective-permute-done | bytes 16416 | tf_op jit(solution)/shard_map/ppermute | solution.py:406
  31.5 0.0 collective-permute-done.6.from_east
  31.5 1.9 %collective-permute-start.8 = (f32[200,128]{1,0:T(8,128)S(1)}, f32[200,128]{1,0:T(8,128)S(1)}, u32[]{:S(2)}, u32[]{:S(2)}) collective-permute-start(f32[200,128]{1,0:T(8,128)S(1)} %pad_maximum_fusion), channel_id=1, source_target_pairs={{0,16},{1,2},{2,1},{3,4},{4,3},{5,6},{6,5},{7,23},{8,24},{9,10},{1... | collective-permute-start | bytes 307208 | tf_op jit(solution)/shard_map/ppermute | solution.py:406
  33.4 3.4 %all-to-all-start.1 = ((f32[8,16,128]{2,1,0:T(8,128)}), f32[8,16,128]{2,1,0:T(8,128)S(1)}, u32[]{:S(2)}, u32[]{:S(2)}) async-start(f32[8,16,128]{2,1,0:T(8,128)} %bitcast.8), calls=%async_computation.1 | async-start | bytes 131072 | tf_op jit(solution)/shard_map/all_to_all | solution.py:479
  36.7 0.8 %shard_map.107 = (f32[16,136,128]{2,1,0:T(8,128)S(1)}, f32[16,136,128]{2,1,0:T(8,128)S(1)}, f32[16,136,128]{2,1,0:T(8,128)S(1)}) custom-call(f32[144,128]{1,0:T(8,128)S(1)} %get-tuple-element.35.co), custom_call_target="tpu_custom_call" | custom-call | flops 100000000 | bytes 3416064 | tf_op jit(solution)/shard_map/pallas_call | solution.py:374
  37.5 0.7 %collective-permute-done.8.b_in = f32[200,128]{1,0:T(8,128)S(1)} collective-permute-done((f32[200,128]{1,0:T(8,128)S(1)}, f32[200,128]{1,0:T(8,128)S(1)}, u32[]{:S(2)}, u32[]{:S(2)}) %collective-permute-start.8) | collective-permute-done | bytes 102432 | tf_op jit(solution)/shard_map/ppermute | solution.py:406
  38.2 3.0 %shard_map.108 = f32[1024,128]{1,0:T(8,128)} custom-call(f32[1024,128]{1,0:T(8,128)S(1)} %bitcast.13, f32[8,136,128]{2,1,0:T(8,128)S(1)} %get-tuple-element.34.f_in, f32[16,136,128]{2,1,0:T(8,128)S(1)} %get-tuple-element.36.cl, f32[16,136,128]{2,1,0:T(8,128)S(1)} %get-tuple-element.37.ct, f32[16,136,128]{2,1,0:T(8,128)S(1)} %get-tuple-element.38.cc, ...), custom_call_target="tpu_custom_call" | custom-call | flops 10000000000 | bytes 5185536 | tf_op jit(solution)/shard_map/pallas_call | solution.py:374
  41.3 0.4 %all-to-all-done.1 = f32[8,16,128]{2,1,0:T(8,128)S(1)} async-done(((f32[8,16,128]{2,1,0:T(8,128)}), f32[8,16,128]{2,1,0:T(8,128)S(1)}, u32[]{:S(2)}, u32[]{:S(2)}) %all-to-all-start.1) | async-done | bytes 65568 | tf_op jit(solution)/shard_map/all_to_all | solution.py:479
  41.7 0.6 %copy.12 = f32[128,128]{1,0:T(8,128)} copy(f32[128,128]{1,0:T(8,128)S(1)} %bitcast.14) | data formatting | bytes 131072
  (10 shorter events, 0.0 us)
Async XLA Ops:
  0.6 21.3 %copy-start.1 = (f32[3,128,128]{2,1,0:T(8,128)S(1)}, f32[3,128,128]{2,1,0:T(8,128)}, u32[]{:S(2)}) copy-start(f32[3,128,128]{2,1,0:T(8,128)} %operator.1) | copy-start | bytes 589828
  2.9 12.4 %collective-permute-start = (f32[584,128]{1,0:T(8,128)S(1)}, f32[584,128]{1,0:T(8,128)S(1)}, u32[]{:S(2)}, u32[]{:S(2)}) collective-permute-start(f32[584,128]{1,0:T(8,128)S(1)} %get-tuple-element.26), channel_id=1, source_target_pairs={{0,1},{1,0},{2,3},{3,2},{4,5},{5,4},{6,7},{7,6},{8,9},{9,8},{10,11... | collective-permute-start | bytes 897032 | tf_op jit(solution)/shard_map/ppermute | solution.py:406
  3.5 15.8 %collective-permute-start.1 = (f32[544,128]{1,0:T(8,128)S(1)}, f32[544,128]{1,0:T(8,128)S(1)}, u32[]{:S(2)}, u32[]{:S(2)}) collective-permute-start(f32[544,128]{1,0:T(8,128)S(1)} %get-tuple-element.27), channel_id=1, source_target_pairs={{0,16},{1,2},{2,1},{3,4},{4,3},{5,6},{6,5},{7,23},{8,24},{9,10},{1... | collective-permute-start | bytes 835592 | tf_op jit(solution)/shard_map/ppermute | solution.py:406
  7.1 12.1 %all-to-all-start = ((f32[8,40,128]{2,1,0:T(8,128)}), f32[8,40,128]{2,1,0:T(8,128)S(1)}, u32[]{:S(2)}, u32[]{:S(2)}) async-start(f32[8,40,128]{2,1,0:T(8,128)} %get-tuple-element.33), calls=%async_computation | async-start | bytes 327680 | tf_op jit(solution)/shard_map/all_to_all | solution.py:453
  10.6 4.7 %collective-permute-start.2 = (f32[5,8,128]{2,1,0:T(8,128)S(1)}, f32[5,8,128]{2,1,0:T(8,128)S(1)}, u32[]{:S(2)}, u32[]{:S(2)}) collective-permute-start(f32[5,8,128]{2,1,0:T(8,128)S(1)} %get-tuple-element.30), channel_id=1, source_target_pairs={{0,16},{1,2},{2,1},{3,4},{4,3},{5,6},{6,5},{7,23},{8,24},{9,10},{1... | collective-permute-start | bytes 61448 | tf_op jit(solution)/shard_map/ppermute | solution.py:406
  15.4 6.1 %collective-permute-start.3 = (f32[17,4,128]{2,1,0:T(4,128)S(1)}, f32[17,4,128]{2,1,0:T(4,128)S(1)}, u32[]{:S(2)}, u32[]{:S(2)}) collective-permute-start(f32[17,4,128]{2,1,0:T(4,128)S(1)} %get-tuple-element.31), channel_id=1, source_target_pairs={{0,8},{1,9},{2,10},{3,11},{4,12},{5,13},{6,14},{7,15},{8,16},{9,17... | collective-permute-start | bytes 104456 | tf_op jit(solution)/shard_map/ppermute | solution.py:406
  17.0 4.9 %collective-permute-start.4 = (f32[17,4,128]{2,1,0:T(4,128)S(1)}, f32[17,4,128]{2,1,0:T(4,128)S(1)}, u32[]{:S(2)}, u32[]{:S(2)}) collective-permute-start(f32[17,4,128]{2,1,0:T(4,128)S(1)} %get-tuple-element.32), channel_id=1, source_target_pairs={{0,24},{1,25},{2,26},{3,27},{4,28},{5,29},{6,30},{7,31},{8,0},{9,1... | collective-permute-start | bytes 104456 | tf_op jit(solution)/shard_map/ppermute | solution.py:406
  21.9 16.3 %copy-start = (f32[4,32,8,128]{3,2,1,0:T(8,128)S(1)}, f32[4,32,8,128]{3,2,1,0:T(8,128)}, u32[]{:S(2)}) copy-start(f32[4,32,8,128]{3,2,1,0:T(8,128)} %param.9) | copy-start | bytes 1572868
  25.9 5.6 %collective-permute-start.5 = (f32[8,4,128]{2,1,0:T(4,128)S(1)}, f32[8,4,128]{2,1,0:T(4,128)S(1)}, u32[]{:S(2)}, u32[]{:S(2)}) collective-permute-start(f32[8,4,128]{2,1,0:T(4,128)S(1)} %get-tuple-element.39), channel_id=1, source_target_pairs={{0,8},{1,9},{2,10},{3,11},{4,12},{5,13},{6,14},{7,15},{8,16},{9,17... | collective-permute-start | bytes 49160 | tf_op jit(solution)/shard_map/ppermute | solution.py:406
  26.7 4.8 %collective-permute-start.6 = (f32[8,4,128]{2,1,0:T(4,128)S(1)}, f32[8,4,128]{2,1,0:T(4,128)S(1)}, u32[]{:S(2)}, u32[]{:S(2)}) collective-permute-start(f32[8,4,128]{2,1,0:T(4,128)S(1)} %get-tuple-element.40), channel_id=1, source_target_pairs={{0,24},{1,25},{2,26},{3,27},{4,28},{5,29},{6,30},{7,31},{8,0},{9,1... | collective-permute-start | bytes 49160 | tf_op jit(solution)/shard_map/ppermute | solution.py:406
  31.5 6.7 %collective-permute-start.8 = (f32[200,128]{1,0:T(8,128)S(1)}, f32[200,128]{1,0:T(8,128)S(1)}, u32[]{:S(2)}, u32[]{:S(2)}) collective-permute-start(f32[200,128]{1,0:T(8,128)S(1)} %pad_maximum_fusion), channel_id=1, source_target_pairs={{0,16},{1,2},{2,1},{3,4},{4,3},{5,6},{6,5},{7,23},{8,24},{9,10},{1... | collective-permute-start | bytes 307208 | tf_op jit(solution)/shard_map/ppermute | solution.py:406
  33.4 4.8 %collective-permute-start.7 = (f32[200,128]{1,0:T(8,128)S(1)}, f32[200,128]{1,0:T(8,128)S(1)}, u32[]{:S(2)}, u32[]{:S(2)}) collective-permute-start(f32[200,128]{1,0:T(8,128)S(1)} %pad_maximum_fusion), channel_id=1, source_target_pairs={{0,1},{1,0},{2,3},{3,2},{4,5},{5,4},{6,7},{7,6},{8,9},{9,8},{10,11... | collective-permute-start | bytes 307208 | tf_op jit(solution)/shard_map/ppermute | solution.py:406
  33.4 8.3 %all-to-all-start.1 = ((f32[8,16,128]{2,1,0:T(8,128)}), f32[8,16,128]{2,1,0:T(8,128)S(1)}, u32[]{:S(2)}, u32[]{:S(2)}) async-start(f32[8,16,128]{2,1,0:T(8,128)} %bitcast.8), calls=%async_computation.1 | async-start | bytes 131072 | tf_op jit(solution)/shard_map/all_to_all | solution.py:479

commit v4 on v3

v4 whole, which is shorter than its diff:
```python
import functools

import jax
import jax.numpy as jnp
from jax import lax
from jax.experimental import pallas as pl
from jax.experimental.pallas import tpu as pltpu
from jax.sharding import PartitionSpec as P

STEPS = 4
ROWS = 8
LANES = 128
PLANES = ROWS + 2 * STEPS
BODY = LANES // 8
RIM = 3
SIDE = 4 * RIM
VMEM = pltpu.VMEM
HBM = pltpu.HBM
MIB = 1 << 20
EDGE_COST = 10**10
EXPAND_COST = 10**8
STATE_COST = 10**9
SMOOTH_COST = 10**10
F32 = jnp.float32


def iota(shape, axis):
    return lax.broadcasted_iota(jnp.int32, shape, axis)


def position():
    lat, count = (lax.axis_index("lat"), lax.axis_size("lat"))
    return lat % 2 == 0, jnp.logical_or(lat == 0, lat == count - 1)


def halo_places(even, pole):
    a_base = jnp.where(even, PLANES - STEPS, 0)
    b_base = jnp.where(even, 0, PLANES - STEPS)
    a_rows = [jnp.where(even, k, STEPS + k) for k in range(STEPS)]
    b_rows = [
        jnp.where(
            pole,
            jnp.where(even, STEPS - 1 - k, ROWS - 1 - k),
            jnp.where(even, STEPS + k, k),
        )
        for k in range(STEPS)
    ]
    return a_base, b_base, a_rows, b_rows


def wind_sign(pole, shape):
    flipped = jnp.logical_and(iota(shape, len(shape) - 1) >= LANES // 2, pole)
    return jnp.where(flipped, -1.0, 1.0).astype(F32)


def split(x):
    high = x.astype(jnp.bfloat16)
    low = (x - high.astype(F32)).astype(jnp.bfloat16)
    return high, low


def matmul(a, b, dims=((1,), (0,))):
    return lax.dot_general(a, b, (dims, ((), ())), preferred_element_type=F32)


def halves(x):
    return x[:, :LANES] + x[:, LANES:]


def pack_kernel(
    inc_hbm, cl_hbm, ct_hbm, values, weights, columns_hbm, types_hbm, counts_hbm,
    own, coef, b_out, a_out, rim_b, rim_a, w_out, e_out, slots_out,
    inc, cl, ct, raw, columns, types, counts, sems,
):
    owners, bucket = (slots_out.shape[0], values.shape[1])
    moves = (
        (inc_hbm, inc),
        (cl_hbm, cl),
        (ct_hbm, ct),
        (columns_hbm, columns),
        (types_hbm, types),
        (counts_hbm, counts),
        (values, slots_out.at[:, pl.ds(0, bucket), :]),
        (weights, slots_out.at[:, pl.ds(bucket, bucket), :]),
    )
    copies = [pltpu.make_async_copy(src, dst, sems.at[n]) for n, (src, dst) in enumerate(moves)]
    for copy in copies:
        copy.start()
    for copy in copies[:3]:
        copy.wait()
    fields = cl.shape[0] // ROWS
    even, _ = position()
    raw[...] = jnp.zeros(raw.shape, F32)
    for r in range(ROWS):
        own[r] = inc[pl.ds(r, LANES, stride=ROWS), :].T
        at = 8 * (STEPS + r)
        raw[at : at + fields, :] = cl[pl.ds(r, fields, stride=ROWS), :]
        raw[at + fields : at + 2 * fields, :] = ct[pl.ds(r, fields, stride=ROWS), :]
        w_out[r] = own[r, 0:STEPS, :]
        e_out[r] = own[r, LANES - STEPS : LANES, :]
    coef[...] = raw[...].T
    w_out[ROWS] = coef[0:STEPS, :]
    e_out[ROWS] = coef[LANES - STEPS : LANES, :]
    a_row = jnp.where(even, STEPS, 0)
    b_row = STEPS - a_row
    for out, first in ((b_out, b_row), (a_out, a_row)):
        for k in range(STEPS):
            out[k] = own[first + k]
    for out, first in ((rim_b, b_row), (rim_a, a_row)):
        for k in range(STEPS):
            out[k, 0:STEPS, :] = own[first + k, 0:STEPS, :]
            out[k, STEPS : 2 * STEPS, :] = own[first + k, LANES - STEPS : LANES, :]
            out[STEPS + 1 + k] = raw[pl.ds(pl.multiple_of(8 * (STEPS + first + k), 8), 8), :]
        out[STEPS, 0:STEPS, :] = coef[0:STEPS, :]
        out[STEPS, STEPS : 2 * STEPS, :] = coef[LANES - STEPS : LANES, :]
    for copy in copies[3:]:
        copy.wait()
    slots = columns.shape[1]
    lane = iota((1, slots), 1)
    limit = jnp.zeros((1, slots), jnp.int32)
    for d in range(owners):
        limit = jnp.where(lane // bucket == d, counts[d], limit)
    code = jnp.where(lane % bucket < limit, columns[...] * 4 + types[...], -1).astype(F32)
    for d in range(owners):
        at = d * bucket
        window = code[:, at // LANES * LANES : at // LANES * LANES + LANES]
        moved = pltpu.roll(window, (-at) % LANES, 1)
        slots_out[d, 2 * bucket : 2 * bucket + 8, :] = jnp.broadcast_to(moved, (8, LANES))


def edge_kernel(w_own, e_own, coef, rim_a, rim_b, w_out, e_out, co, raw):
    even, pole = position()
    a_base, b_base, _, b_rows = halo_places(even, pole)
    sign = wind_sign(pole, (1, LANES))
    raw[...] = jnp.zeros(raw.shape, F32)
    for k in range(STEPS):
        kk = jnp.where(pole, STEPS - 1 - k, k)
        w_out[a_base + k] = rim_a[k, 0:STEPS, :]
        e_out[a_base + k] = rim_a[k, STEPS : 2 * STEPS, :]
        rim = rim_b[kk] * sign
        w_out[b_base + k] = rim[0:STEPS]
        e_out[b_base + k] = rim[STEPS : 2 * STEPS]
        raw[pl.ds(pl.multiple_of(8 * (a_base + k), 8), 8), :] = rim_a[STEPS + 1 + k]
        raw[pl.ds(pl.multiple_of(8 * (b_base + k), 8), 8), :] = rim_b[STEPS + 1 + kk]
    for r in range(ROWS):
        w_out[STEPS + r] = w_own[r]
        e_out[STEPS + r] = e_own[r]
    plane = iota((8, LANES), 1) // 8
    tile = jnp.concatenate([w_own[ROWS], e_own[ROWS]], 0)
    from_a = pltpu.roll(rim_a[STEPS], LANES // 2, 1)
    tile = jnp.where(plane // STEPS == a_base // STEPS, from_a, tile)
    for k in range(STEPS):
        shift = (8 * (b_base + k - STEPS - b_rows[k]) + 2 * LANES) % LANES
        tile = jnp.where(plane == b_base + k, pltpu.roll(rim_b[STEPS], shift, 1), tile)
    w_out[PLANES] = tile[0:STEPS]
    e_out[PLANES] = tile[STEPS : 2 * STEPS]
    co[...] = raw[...].T + coef[...]


def expand(co, cl, ct, cc, regs=BODY):
    high, low = split(jnp.concatenate([co[pl.ds(q, 8, stride=regs), :] for q in range(regs)], 0))
    tall = 2 * LANES - 16
    row, col = (iota((tall, 2 * LANES), 0), iota((tall, 2 * LANES), 1))
    wanted = LANES - 16 + col // LANES * 4 + col % LANES // (LANES // 4)
    picks = [jnp.where(row == wanted + 8 * odd, 1.0, 0.0).astype(jnp.bfloat16) for odd in range(2)]
    for p in range(PLANES):
        first = LANES - 16 - p // 2 * 16
        pick = picks[p % 2][first : first + LANES, :]
        both = matmul(high, pick) + matmul(low, pick)
        a, b = (both[:, :LANES], both[:, LANES:])
        cl[p] = a
        ct[p] = b
        cc[p] = 1.0 - 2.0 * (a * a + b * b)


def diffuse(f, spare, cl, ct, cc, store):
    regs = [pl.ds(8 * q, 8) for q in range(f.shape[1] // 8)]
    for step in range(STEPS):
        last = step == STEPS - 1

        def row(p, carry, f=f, spare=spare, last=last):
            here = [f[p, at, :] for at in regs]
            g = [cl[p, at, :] * x for at, x in zip(regs, here)]
            g = [pltpu.roll(g[-1], 1, 0)] + g + [pltpu.roll(g[0], 7, 0)]
            for q, at in enumerate(regs):
                sides = ct[p + 1, at, :] * f[p + 1, at, :] + ct[p - 1, at, :] * f[p - 1, at, :]
                new = cc[p, at, :] * here[q] + cl[p, at, :] * (g[q] + g[q + 2]) + ct[p, at, :] * sides
                if last:
                    store(p - STEPS, q, new)
                else:
                    spare[p, at, :] = new
            return carry

        lax.fori_loop(step + 1, PLANES - 1 - step, row, 0)
        f, spare = (spare, f)


def diffuse_rim(rim, f, spare, cl, ct, cc, west, east):
    for p in range(PLANES):
        rim[p, 0:STEPS, :] = west[p]
        rim[p, 2 * SIDE - STEPS : 2 * SIDE, :] = east[p]
        for q in range(RIM):
            f[p, 8 * q : 8 * q + 8, :] = rim[p, pl.ds(q, 8, stride=RIM), :]

    def store(r, q, value):
        rim[STEPS + r, pl.ds(q, 8, stride=RIM), :] = value

    diffuse(f, spare, cl, ct, cc, store)


def body_cell(n, rows):
    rest = n % LANES
    row = jnp.zeros(n.shape, jnp.int32)
    for k, r in enumerate(rows):
        row = jnp.where(n // LANES == k, r, row)
    return row * LANES + (rest % 8) * BODY + rest // 8


def edge_cell(n, rows):
    rest = n % 8
    row = jnp.zeros(n.shape, jnp.int32)
    for k, r in enumerate(rows):
        row = jnp.where(n // 8 == k, r, row)
    return row * LANES + jnp.where(rest < STEPS, rest, rest + LANES - 8)


def scatter(adjoint, code_row, cells):
    code = code_row.astype(jnp.int32)
    cell = jnp.where(code >= 0, code >> 2, -1)
    hot = jnp.concatenate(
        [
            jnp.where(cells == cell[:, t * LANES : (t + 1) * LANES], 1.0, 0.0).astype(jnp.bfloat16)
            for t in range(cell.shape[1] // LANES)
        ],
        1,
    )
    return halves(matmul(hot, jnp.concatenate(split(adjoint), 1)))


def payload_parts(ref):
    slots = ref.shape[0] * LANES // (LANES + 8)
    codes = [ref[slots + 8 * t : slots + 8 * t + 1, :] for t in range(slots // LANES)]
    return ref[0:slots, :], jnp.concatenate(codes, 1)


def state_kernel(own, a_in, b_in, cl, ct, cc, state, f, spare):
    even, pole = position()
    a_base, b_base, _, _ = halo_places(even, pole)
    sign = wind_sign(pole, (1, LANES))
    for q in range(BODY):
        at, to = (pl.ds(q, 8, stride=BODY), pl.ds(8 * q, 8))
        for k in range(STEPS):
            f[a_base + k, to, :] = a_in[k, at, :]
            f[b_base + k, to, :] = b_in[jnp.where(pole, STEPS - 1 - k, k), at, :] * sign
        for r in range(ROWS):
            f[STEPS + r, to, :] = own[r, at, :]

    def store(r, q, value):
        state[r, pl.ds(8 * q, 8), :] = value

    diffuse(f, spare, cl, ct, cc, store)


def observe_kernel(
    state_in, own, a_in, b_in, co, from_west, from_east, slots_in, operator,
    dep_out, pay_out, f_out, rl, rt, rc,
    rim, f, spare, co_rim, state,
):
    even, pole = position()
    a_base, b_base, _, _ = halo_places(even, pole)
    sign = wind_sign(pole, (1, LANES))
    co_rim[0:STEPS, :] = from_west[PLANES]
    co_rim[STEPS:SIDE, :] = co[0:8, :]
    co_rim[SIDE : 2 * SIDE - STEPS, :] = co[LANES - 8 : LANES, :]
    co_rim[2 * SIDE - STEPS : 2 * SIDE, :] = from_east[PLANES]
    expand(co_rim, rl, rt, rc, RIM)
    sides = ((slice(STEPS, SIDE), slice(0, 8)), (slice(SIDE, 2 * SIDE - STEPS), slice(LANES - 8, LANES)))
    for to, at in sides:
        for k in range(STEPS):
            rim[a_base + k, to, :] = a_in[k, at, :]
            rim[b_base + k, to, :] = b_in[jnp.where(pole, STEPS - 1 - k, k), at, :] * sign
        for r in range(ROWS):
            rim[STEPS + r, to, :] = own[r, at, :]
    diffuse_rim(rim, f, spare, rl, rt, rc, from_west, from_east)
    state[...] = state_in[...]
    for r in range(ROWS):
        state[r, pl.ds(0, STEPS, stride=8), :] = rim[STEPS + r, STEPS : 2 * STEPS, :]
        last = rim[STEPS + r, 2 * SIDE - 2 * STEPS : 2 * SIDE - STEPS, :]
        state[r, pl.ds(8 * (BODY - STEPS) + 7, STEPS, stride=8), :] = last

    owners, bucket = (slots_in.shape[0], (slots_in.shape[1] - 8) // 2)
    slots = owners * bucket
    lane = iota((1, LANES), 1)
    per_tile = LANES // bucket
    code_parts = []
    for t in range(slots // LANES):
        part = jnp.full((1, LANES), -1.0, F32)
        for n in range(per_tile):
            got = slots_in[t * per_tile + n, 2 * bucket : 2 * bucket + 1, :]
            part = jnp.where(lane // bucket == n, pltpu.roll(got, n * bucket, 1), part)
        code_parts.append(part)
        pay_out[slots + 8 * t : slots + 8 * t + 8, :] = jnp.broadcast_to(part, (8, LANES))
    code_row = jnp.concatenate(code_parts, 1)
    code = jnp.concatenate([jnp.broadcast_to(part, (LANES, LANES)).T for part in code_parts], 0)
    code = code.astype(jnp.int32)
    cell = jnp.where(code >= 0, code >> 2, -1)
    kind = jnp.where(code >= 0, code & 3, -1)

    depth = ROWS * LANES
    places = body_cell(iota((1, depth), 1), range(ROWS))
    hot = jnp.concatenate(
        [
            jnp.where(places[:, t : t + LANES] == cell, 1.0, 0.0).astype(jnp.bfloat16)
            for t in range(0, depth, LANES)
        ],
        1,
    )
    cells = jnp.concatenate(split(state[...].reshape(depth, LANES)), 1)
    column = halves(matmul(hot, cells))

    masks = [kind == n for n in range(3)]
    op_high, op_low = split(operator[...])
    zero = jnp.zeros((LANES, LANES), jnp.bfloat16)

    def by_kind(x):
        return jnp.concatenate([jnp.where(m, part, jnp.zeros_like(part)) for part in split(x) for m in masks], 1)

    forward = jnp.concatenate(
        [jnp.concatenate([op_high[n], op_low[n]], 1) for n in range(3)]
        + [jnp.concatenate([op_high[n], zero], 1) for n in range(3)],
        0,
    )
    model = halves(matmul(by_kind(column), forward))
    values = slots_in[:, 0:bucket, :].reshape(slots, LANES)
    weights = slots_in[:, bucket : 2 * bucket, :].reshape(slots, LANES)
    departures = jnp.where(code >= 0, values - model, 0.0)
    dep_out[...] = departures
    backward = jnp.concatenate(
        [
            jnp.concatenate([op_high[0], op_high[1], op_high[2]] * 2, 1),
            jnp.concatenate([op_low[0], op_low[1], op_low[2], zero, zero, zero], 1),
        ],
        0,
    )
    adjoint = halves(matmul(by_kind(weights * departures), backward, ((1,), (1,))))
    pay_out[0:slots, :] = adjoint
    f_out[...] = scatter(adjoint, code_row, body_cell(iota((depth, LANES), 0), range(ROWS))).reshape(f_out.shape)


def edge_forcing_kernel(f_in, a_in, b_in, w_out, e_out):
    even, pole = position()
    a_base, b_base, a_rows, b_rows = halo_places(even, pole)
    sign = wind_sign(pole, (1, LANES))
    for ref, rows, base, scale in ((a_in, a_rows, a_base, 1.0), (b_in, b_rows, b_base, sign)):
        got = scatter(*payload_parts(ref), edge_cell(iota((8 * STEPS, LANES), 0), rows)) * scale
        for k in range(STEPS):
            w_out[base + k] = got[8 * k : 8 * k + STEPS]
            e_out[base + k] = got[8 * k + STEPS : 8 * k + 8]
    for r in range(ROWS):
        w_out[STEPS + r] = f_in[r, pl.ds(0, STEPS, stride=8), :]
        e_out[STEPS + r] = f_in[r, pl.ds(8 * (BODY - STEPS) + 7, STEPS, stride=8), :]


def smooth_kernel(f_in, a_in, b_in, cl, ct, cc, smooth, rim, f, spare):
    even, pole = position()
    a_base, b_base, a_rows, b_rows = halo_places(even, pole)
    sign = wind_sign(pole, (1, LANES))
    for ref, rows, base, scale in ((a_in, a_rows, a_base, 1.0), (b_in, b_rows, b_base, sign)):
        got = scatter(*payload_parts(ref), body_cell(iota((STEPS * LANES, LANES), 0), rows)) * scale
        for k in range(STEPS):
            f[base + k] = got[k * LANES : (k + 1) * LANES]
    for r in range(ROWS):
        f[STEPS + r] = f_in[r]
    for p in range(PLANES):
        rim[p, 0:STEPS, :] = jnp.zeros((STEPS, LANES), F32)
        rim[p, STEPS:SIDE, :] = f[p, pl.ds(0, 8, stride=8), :]
        rim[p, SIDE : 2 * SIDE - STEPS, :] = f[p, pl.ds(8 * (BODY - 8) + 7, 8, stride=8), :]
        rim[p, 2 * SIDE - STEPS : 2 * SIDE, :] = jnp.zeros((STEPS, LANES), F32)

    def store(r, q, value):
        smooth[r, pl.ds(q, 8, stride=BODY), :] = value

    diffuse(f, spare, cl, ct, cc, store)


def last_kernel(inc, smooth, rim_in, from_west, from_east, rl, rt, rc, out, rim, f, spare, wide):
    rim[...] = rim_in[...]
    diffuse_rim(rim, f, spare, rl, rt, rc, from_west, from_east)
    for r in range(ROWS):
        wide[...] = smooth[r]
        wide[0:STEPS, :] = rim[STEPS + r, STEPS : 2 * STEPS, :]
        wide[LANES - STEPS : LANES, :] = rim[STEPS + r, 2 * SIDE - 2 * STEPS : 2 * SIDE - STEPS, :]
        at = pl.ds(r, LANES, stride=ROWS)
        out[at, :] = inc[at, :] - wide[...].T


def call(kernel, outs, args, scratch=(), spaces=None, flops=0, limit=20):
    spaces = spaces or {}
    specs = [pl.BlockSpec(memory_space=spaces.get(n, VMEM)) for n in range(len(args))]
    size = 4 * sum(x.size for x in list(args) + list(outs))
    args = [pltpu.with_memory_space_constraint(x, HBM) if spaces.get(n) is HBM else x for n, x in enumerate(args)]
    return pl.pallas_call(
        kernel,
        out_shape=outs,
        in_specs=specs,
        out_specs=[pl.BlockSpec(memory_space=VMEM) for _ in outs],
        scratch_shapes=list(scratch),
        compiler_params=pltpu.CompilerParams(vmem_limit_bytes=limit * MIB),
        cost_estimate=pl.CostEstimate(flops=flops, bytes_accessed=size, transcendentals=0),
    )(*args)


def routes():
    lons, lats = (lax.axis_size("lon"), lax.axis_size("lat"))
    at = lambda lon, lat: lon % lons * lats + lat
    cells = [(lon, lat) for lon in range(lons) for lat in range(lats)]
    inner = [(at(o, a), at(o, a ^ 1)) for o, a in cells]
    outer = []
    for o, a in cells:
        if a in (0, lats - 1):
            outer.append((at(o, a), at(o + lons // 2, a)))
        else:
            outer.append((at(o, a), at(o, a - 1 if a % 2 == 0 else a + 1)))
    east = [(at(o, a), at(o + 1, a)) for o, a in cells]
    west = [(at(o, a), at(o - 1, a)) for o, a in cells]
    return inner, outer, east, west


def local(
    increment, coef_lon, coef_lat, obs_values, obs_weight, obs_operator, obs_columns, obs_types, obs_counts
):
    shape = lambda *dims: jax.ShapeDtypeStruct(dims, F32)
    inner, outer, east, west = routes()
    send = lambda x, route: lax.ppermute(x, ("lon", "lat"), route)
    lats = lax.axis_size("lat")
    slots = obs_values.shape[0]
    bucket = slots // lats
    tiles = slots // LANES
    fields = increment.shape[0]
    inc = increment.reshape(-1, LANES)
    cl = coef_lon.reshape(fields * ROWS, LANES)
    ct = coef_lat.reshape(fields * ROWS, LANES)

    own, coef, b_send, a_send, rim_b, rim_a, w_own, e_own, slots_send = call(
        pack_kernel,
        [
            shape(ROWS, LANES, LANES),
            shape(LANES, LANES),
            shape(STEPS, LANES, LANES),
            shape(STEPS, LANES, LANES),
            shape(2 * STEPS + 1, 8, LANES),
            shape(2 * STEPS + 1, 8, LANES),
            shape(ROWS + 1, STEPS, LANES),
            shape(ROWS + 1, STEPS, LANES),
            shape(lats, 2 * bucket + 8, LANES),
        ],
        [
            inc,
            cl,
            ct,
            obs_values.reshape(lats, bucket, LANES),
            obs_weight.reshape(lats, bucket, LANES),
            obs_columns.reshape(1, slots),
            obs_types.reshape(1, slots),
            obs_counts,
        ],
        [
            VMEM(inc.shape, F32),
            VMEM(cl.shape, F32),
            VMEM(ct.shape, F32),
            VMEM((LANES, LANES), F32),
            VMEM((1, slots), jnp.int32),
            VMEM((1, slots), jnp.int32),
            pltpu.SMEM(obs_counts.shape, jnp.int32),
            pltpu.SemaphoreType.DMA((8,)),
        ],
        spaces={n: HBM for n in range(8)},
    )
    rim_a = send(rim_a, inner)
    a_in = send(a_send, inner)
    rim_b = send(rim_b, outer)
    b_in = send(b_send, outer)
    slots_send, _ = lax.optimization_barrier((slots_send, a_in))
    slots_in = lax.all_to_all(slots_send, "lat", split_axis=0, concat_axis=0, tiled=True)
    edge = shape(PLANES + 1, STEPS, LANES)
    block = shape(ROWS, LANES, LANES)
    planes = shape(PLANES, LANES, LANES)
    ends = shape(PLANES, 2 * SIDE, LANES)
    body_buffers = [VMEM(planes.shape, F32)] * 2
    rim_buffers = [VMEM(ends.shape, F32)] * 3
    w_send, e_send, co = call(
        edge_kernel,
        [edge, edge, shape(LANES, LANES)],
        [w_own, e_own, coef, rim_a, rim_b],
        [VMEM((LANES, LANES), F32)],
        flops=EDGE_COST,
    )
    from_west = send(e_send, east)
    from_east = send(w_send, west)
    wl, wt, wc = call(expand, [planes, planes, planes], [co], flops=EXPAND_COST)
    (state,) = call(state_kernel, [block], [own, a_in, b_in, wl, wt, wc], body_buffers, flops=STATE_COST)
    departures, payload, forcing, rl, rt, rc = call(
        observe_kernel,
        [shape(slots, LANES), shape(slots + 8 * tiles, LANES), block, ends, ends, ends],
        [state, own, a_in, b_in, co, from_west, from_east, slots_in, obs_operator],
        rim_buffers + [VMEM((2 * SIDE, LANES), F32), VMEM(block.shape, F32)],
        flops=10**8,
    )
    a_in = send(payload, inner)
    b_in = send(payload, outer)
    back = lax.all_to_all(
        departures.reshape(lats, bucket, LANES), "lat", split_axis=0, concat_axis=0, tiled=True
    )
    co, _ = lax.optimization_barrier((co, payload))
    wl, wt, wc = call(expand, [planes, planes, planes], [co], flops=EXPAND_COST)
    edge = shape(PLANES, STEPS, LANES)
    w_send, e_send = call(edge_forcing_kernel, [edge, edge], [forcing, a_in, b_in], flops=10**8)
    from_west = send(e_send, east)
    from_east = send(w_send, west)
    smooth, rim = call(
        smooth_kernel, [block, ends], [forcing, a_in, b_in, wl, wt, wc], body_buffers, flops=SMOOTH_COST
    )
    (gradient,) = call(
        last_kernel,
        [shape(*inc.shape)],
        [inc, smooth, rim, from_west, from_east, rl, rt, rc],
        rim_buffers + [VMEM((LANES, LANES), F32)],
        flops=10**8,
    )
    gradient, back = lax.optimization_barrier((gradient, back))
    return (gradient.reshape(increment.shape), back.reshape(slots, LANES))


def solution(mesh):
    return jax.shard_map(
        local,
        mesh=mesh,
        in_specs=(
            P(None, None, "lat", "lon"),
            P(None, "lat", "lon"),
            P(None, "lat", "lon"),
            P(("lon", "lat"), None),
            P(("lon", "lat"), None),
            P(),
            P(("lon", "lat")),
            P(("lon", "lat")),
            P(("lon", "lat")),
        ),
        out_specs=(P(None, None, "lat", "lon"), P(("lon", "lat"), None)),
        check_vma=False,
    )
```

time: 42.6 us -> 36.2 us (0.85)
  waiting for transfers between devices: 9.39 us -> 2.01 us
  Pallas kernels: 10.2 us -> 10.8 us
    ppermute x9 -> x10, waiting for transfers between devices: 8.96 us -> 2 us  [local(): send = lambda x, route: lax.ppermute(x, ('lon', 'lat'), route)]
    pallas_call x5 -> x9, Pallas kernels: 10.2 us -> 10.8 us  [call(): pl.pallas_call(kernel, out_shape=outs, in_specs=specs, out_specs=[pl.Bloc...]
    ppermute x9 -> x10, starting transfers between devices: 14.6 us -> 14.9 us  [local(): send = lambda x, route: lax.ppermute(x, ('lon', 'lat'), route)]
  transfers between devices with their start and end apart: 11 -> 12, of which waited for: 6 -> 3; matrix products, arithmetic and copies ran while one was open for 0% -> 0% of each run, Pallas kernels for 9% -> 18%
where the time goes in v4:
time: 36.2 us; the launch traced here: 35.9 us
  starting transfers between devices  21.7 us (60%)
  Pallas kernels  10.8 us (30%)
  waiting for transfers between devices  2.01 us (6%)
  between operations  0.77 us (2%)
  local copies, waits for them, and re-layouts  0.64 us (2%)
    ppermute x10, starting transfers between devices, local(): send = lambda x, route: lax.ppermute(x, ('lon', 'lat'), route)  14.9 us
    pallas_call x9, Pallas kernels, call(): pl.pallas_call(kernel, out_shape=outs, in_specs=specs, out_specs=[pl.Bloc...  10.8 us
    all_to_all x1, starting transfers between devices, local(): lax.all_to_all(slots_send, 'lat', split_axis=0, concat_axis=0, tiled=True)  3.38 us
    all_to_all x1, starting transfers between devices, local(): lax.all_to_all(departures.reshape(lats, bucket, LANES), 'lat', split_axis...  3.35 us
    ppermute x10, waiting for transfers between devices, local(): send = lambda x, route: lax.ppermute(x, ('lon', 'lat'), route)  2 us
  transfers between devices with their start and end apart: 12, of which 3 were waited for; matrix products, arithmetic and copies ran while one was open for 0% of the time, Pallas kernels for 18%

profile of v4, /device:TPU:0, one launch (start us, length us, event | category | flops | bytes accessed | tf_op | source)
XLA Modules:
  0.0 35.9 jit_solution(490704153756521475)
XLA Ops:
  0.6 2.2 %shard_map.104 = (f32[8,128,128]{2,1,0:T(8,128)S(1)}, f32[128,128]{1,0:T(8,128)S(1)}, f32[4,128,128]{2,1,0:T(8,128)S(1)}, f32[4,128,128]{2,1,0:T(8,128)S(1)}, f3...) custom-call(f32[1024,128]{1,0:T(8,128)} %bitcast.10, ...), custom_call_target="tpu_custom_call" | custom-call | bytes 2077728 | tf_op jit(solution)/shard_map/pallas_call | solution.py:402
  2.8 0.5 %collective-permute-start = (f32[4,128,128]{2,1,0:T(8,128)S(1)}, f32[4,128,128]{2,1,0:T(8,128)S(1)}, u32[]{:S(2)}, u32[]{:S(2)}) collective-permute-start(f32[4,128,128]{2,1,0:T(8,128)S(1)} %get-tuple-element.35), channel_id=1, source_target_pairs={{0,1},{1,0},{2,3},{3,2},{4,5},{5,4},{6,7},{7,6},{8,9},{9,8},{10,11... | collective-permute-start | bytes 786440 | tf_op jit(solution)/shard_map/ppermute | solution.py:434
  3.4 0.1 collective-permute-start.2
  3.4 4.0 %collective-permute-start.3 = (f32[9,8,128]{2,1,0:T(8,128)S(1)}, f32[9,8,128]{2,1,0:T(8,128)S(1)}, u32[]{:S(2)}, u32[]{:S(2)}) collective-permute-start(f32[9,8,128]{2,1,0:T(8,128)S(1)} %get-tuple-element.41), channel_id=1, source_target_pairs={{0,16},{1,2},{2,1},{3,4},{4,3},{5,6},{6,5},{7,23},{8,24},{9,10},{1... | collective-permute-start | bytes 110600 | tf_op jit(solution)/shard_map/ppermute | solution.py:434
  7.4 0.0 collective-permute-start.1
  7.5 3.4 %all-to-all-start = ((f32[8,40,128]{2,1,0:T(8,128)}), f32[8,40,128]{2,1,0:T(8,128)S(1)}, u32[]{:S(2)}, u32[]{:S(2)}) async-start(f32[8,40,128]{2,1,0:T(8,128)} %get-tuple-element.49), calls=%async_computation | async-start | bytes 327680 | tf_op jit(solution)/shard_map/all_to_all | solution.py:484
  10.9 0.1 shard_map.105
  11.0 2.8 %collective-permute-start.4 = (f32[17,4,128]{2,1,0:T(4,128)S(1)}, f32[17,4,128]{2,1,0:T(4,128)S(1)}, u32[]{:S(2)}, u32[]{:S(2)}) collective-permute-start(f32[17,4,128]{2,1,0:T(4,128)S(1)} %get-tuple-element.46), channel_id=1, source_target_pairs={{0,8},{1,9},{2,10},{3,11},{4,12},{5,13},{6,14},{7,15},{8,16},{9,17... | collective-permute-start | bytes 104456 | tf_op jit(solution)/shard_map/ppermute | solution.py:434
  13.8 2.8 %collective-permute-start.5 = (f32[17,4,128]{2,1,0:T(4,128)S(1)}, f32[17,4,128]{2,1,0:T(4,128)S(1)}, u32[]{:S(2)}, u32[]{:S(2)}) collective-permute-start(f32[17,4,128]{2,1,0:T(4,128)S(1)} %get-tuple-element.47), channel_id=1, source_target_pairs={{0,24},{1,25},{2,26},{3,27},{4,28},{5,29},{6,30},{7,31},{8,0},{9,1... | collective-permute-start | bytes 104456 | tf_op jit(solution)/shard_map/ppermute | solution.py:434
  16.7 0.7 %shard_map.106 = (f32[16,128,128]{2,1,0:T(8,128)S(1)}, f32[16,128,128]{2,1,0:T(8,128)S(1)}, f32[16,128,128]{2,1,0:T(8,128)S(1)}) custom-call(f32[128,128]{1,0:T(8,128)S(1)} %get-tuple-element.52.co), custom_call_target="tpu_custom_call" | custom-call | flops 100000000 | bytes 3211264 | tf_op jit(solution)/shard_map/pallas_call | solution.py:402
  17.4 1.3 %collective-permute-done.1.b_in = f32[4,128,128]{2,1,0:T(8,128)S(1)} collective-permute-done((f32[4,128,128]{2,1,0:T(8,128)S(1)}, f32[4,128,128]{2,1,0:T(8,128)S(1)}, u32[]{:S(2)}, u32[]{:S(2)}) %collective-permute-start.1) | collective-permute-done | bytes 262176 | tf_op jit(solution)/shard_map/ppermute | solution.py:434
  18.7 1.6 %shard_map.107.state_in = f32[8,128,128]{2,1,0:T(8,128)S(1)} custom-call(f32[8,128,128]{2,1,0:T(8,128)S(1)} %get-tuple-element.34.own, f32[4,128,128]{2,1,0:T(8,128)S(1)} %collective-permute-done.a_in, f32[4,128,128]{2,1,0:T(8,128)S(1)} %collective-permute-done.1.b_in, f32[16,128,128]{2,1,0:T(8,128)S(1)} %get-tuple-element.43.cl, ...), custom_call_target="tpu_custom_call" | custom-call | flops 1000000000 | bytes 4718592 | tf_op jit(solution)/shard_map/pallas_call | solution.py:402
  20.4 2.1 %shard_map.108 = (f32[128,128]{1,0:T(8,128)}, f32[136,128]{1,0:T(8,128)S(1)}, f32[8,128,128]{2,1,0:T(8,128)S(1)}, f32[16,24,128]{2,1,0:T(8,128)S(1)}, f32[16,24,...) custom-call(f32[8,128,128]{2,1,0:T(8,128)S(1)} %shard_map.107.state_in, f32[8,128,128]{2,1,0:T(8,128)S(1)} %get-tuple-element.34.own, ...), custom_call_target="tpu_custom_call" | custom-call | flops 100000000 | bytes 3317760 | tf_op jit(solution)/shard_map/pallas_call | solution.py:402
  22.5 0.8 %collective-permute-start.7 = (f32[136,128]{1,0:T(8,128)S(1)}, f32[136,128]{1,0:T(8,128)S(1)}, u32[]{:S(2)}, u32[]{:S(2)}) collective-permute-start(f32[136,128]{1,0:T(8,128)S(1)} %get-tuple-element.51), channel_id=1, source_target_pairs={{0,16},{1,2},{2,1},{3,4},{4,3},{5,6},{6,5},{7,23},{8,24},{9,10},{1... | collective-permute-start | bytes 208904 | tf_op jit(solution)/shard_map/ppermute | solution.py:434
  23.4 3.4 %all-to-all-start.1 = ((f32[8,16,128]{2,1,0:T(8,128)}), f32[8,16,128]{2,1,0:T(8,128)S(1)}, u32[]{:S(2)}, u32[]{:S(2)}) async-start(f32[8,16,128]{2,1,0:T(8,128)} %bitcast.7), calls=%async_computation.1 | async-start | bytes 131072 | tf_op jit(solution)/shard_map/all_to_all | solution.py:511
  26.7 0.7 %shard_map.109 = (f32[16,128,128]{2,1,0:T(8,128)S(1)}, f32[16,128,128]{2,1,0:T(8,128)S(1)}, f32[16,128,128]{2,1,0:T(8,128)S(1)}) custom-call(f32[128,128]{1,0:T(8,128)S(1)} %get-tuple-element.52.co), custom_call_target="tpu_custom_call" | custom-call | flops 100000000 | bytes 3211264 | tf_op jit(solution)/shard_map/pallas_call | solution.py:402
  27.4 0.4 %collective-permute-done.7.b_in = f32[136,128]{1,0:T(8,128)S(1)} collective-permute-done((f32[136,128]{1,0:T(8,128)S(1)}, f32[136,128]{1,0:T(8,128)S(1)}, u32[]{:S(2)}, u32[]{:S(2)}) %collective-permute-start.7) | collective-permute-done | bytes 69664 | tf_op jit(solution)/shard_map/ppermute | solution.py:434
  27.8 0.1 shard_map.111
  28.0 1.5 %collective-permute-start.8 = (f32[16,4,128]{2,1,0:T(4,128)S(1)}, f32[16,4,128]{2,1,0:T(4,128)S(1)}, u32[]{:S(2)}, u32[]{:S(2)}) collective-permute-start(f32[16,4,128]{2,1,0:T(4,128)S(1)} %get-tuple-element.58), channel_id=1, source_target_pairs={{0,8},{1,9},{2,10},{3,11},{4,12},{5,13},{6,14},{7,15},{8,16},{9,17... | collective-permute-start | bytes 98312 | tf_op jit(solution)/shard_map/ppermute | solution.py:434
  29.5 2.3 %collective-permute-start.9 = (f32[16,4,128]{2,1,0:T(4,128)S(1)}, f32[16,4,128]{2,1,0:T(4,128)S(1)}, u32[]{:S(2)}, u32[]{:S(2)}) collective-permute-start(f32[16,4,128]{2,1,0:T(4,128)S(1)} %get-tuple-element.59), channel_id=1, source_target_pairs={{0,24},{1,25},{2,26},{3,27},{4,28},{5,29},{6,30},{7,31},{8,0},{9,1... | collective-permute-start | bytes 98312 | tf_op jit(solution)/shard_map/ppermute | solution.py:434
  31.8 1.6 %shard_map.110 = (f32[8,128,128]{2,1,0:T(8,128)S(1)}, f32[16,24,128]{2,1,0:T(8,128)S(1)}) custom-call(f32[8,128,128]{2,1,0:T(8,128)S(1)} %get-tuple-element.50.f_in, f32[136,128]{1,0:T(8,128)S(1)} %collective-permute-done.6.a_in, f32[136,128]{1,0:T(8,128)S(1)} %collective-permute-done.7.b_in, f32[16,128,128]{2,1,0:T(8,128)S(1)} %get-tuple-element.53.cl, ...), custom_call_target="tpu_custom_call" | custom-call | flops 10000000000 | bytes 4530176 | tf_op jit(solution)/shard_map/pallas_call | solution.py:402
  33.5 0.3 collective-permute-done.8.from_west
  33.8 1.5 %shard_map.112 = f32[1024,128]{1,0:T(8,128)} custom-call(f32[1024,128]{1,0:T(8,128)S(1)} %bitcast.11, f32[8,128,128]{2,1,0:T(8,128)S(1)} %get-tuple-element.56.smooth, f32[16,24,128]{2,1,0:T(8,128)S(1)} %get-tuple-element.57.rim_in, f32[16,4,128]{2,1,0:T(4,128)S(1)} %collective-permute-done.8.from_west, f32[16,4,128]{2,1,0:T(4,128)S(1)} %collective-permute-done.9.from_east, ...), custom_call_target="tpu_custom_call" | custom-call | flops 100000000 | bytes 2424832 | tf_op jit(solution)/shard_map/pallas_call | solution.py:402
  35.3 0.6 %copy.12 = f32[128,128]{1,0:T(8,128)} copy(f32[128,128]{1,0:T(8,128)S(1)} %bitcast.13) | data formatting | bytes 131072
  (14 shorter events, 0.0 us)
Async XLA Ops:
  2.8 4.6 %collective-permute-start = (f32[4,128,128]{2,1,0:T(8,128)S(1)}, f32[4,128,128]{2,1,0:T(8,128)S(1)}, u32[]{:S(2)}, u32[]{:S(2)}) collective-permute-start(f32[4,128,128]{2,1,0:T(8,128)S(1)} %get-tuple-element.35), channel_id=1, source_target_pairs={{0,1},{1,0},{2,3},{3,2},{4,5},{5,4},{6,7},{7,6},{8,9},{9,8},{10,11... | collective-permute-start | bytes 786440 | tf_op jit(solution)/shard_map/ppermute | solution.py:434
  3.4 7.5 %collective-permute-start.2 = (f32[9,8,128]{2,1,0:T(8,128)S(1)}, f32[9,8,128]{2,1,0:T(8,128)S(1)}, u32[]{:S(2)}, u32[]{:S(2)}) collective-permute-start(f32[9,8,128]{2,1,0:T(8,128)S(1)} %get-tuple-element.40), channel_id=1, source_target_pairs={{0,1},{1,0},{2,3},{3,2},{4,5},{5,4},{6,7},{7,6},{8,9},{9,8},{10,11... | collective-permute-start | bytes 110600 | tf_op jit(solution)/shard_map/ppermute | solution.py:434
  3.4 7.5 %collective-permute-start.3 = (f32[9,8,128]{2,1,0:T(8,128)S(1)}, f32[9,8,128]{2,1,0:T(8,128)S(1)}, u32[]{:S(2)}, u32[]{:S(2)}) collective-permute-start(f32[9,8,128]{2,1,0:T(8,128)S(1)} %get-tuple-element.41), channel_id=1, source_target_pairs={{0,16},{1,2},{2,1},{3,4},{4,3},{5,6},{6,5},{7,23},{8,24},{9,10},{1... | collective-permute-start | bytes 110600 | tf_op jit(solution)/shard_map/ppermute | solution.py:434
  7.4 11.3 %collective-permute-start.1 = (f32[4,128,128]{2,1,0:T(8,128)S(1)}, f32[4,128,128]{2,1,0:T(8,128)S(1)}, u32[]{:S(2)}, u32[]{:S(2)}) collective-permute-start(f32[4,128,128]{2,1,0:T(8,128)S(1)} %get-tuple-element.36), channel_id=1, source_target_pairs={{0,16},{1,2},{2,1},{3,4},{4,3},{5,6},{6,5},{7,23},{8,24},{9,10},{1... | collective-permute-start | bytes 786440 | tf_op jit(solution)/shard_map/ppermute | solution.py:434
  7.5 12.9 %all-to-all-start = ((f32[8,40,128]{2,1,0:T(8,128)}), f32[8,40,128]{2,1,0:T(8,128)S(1)}, u32[]{:S(2)}, u32[]{:S(2)}) async-start(f32[8,40,128]{2,1,0:T(8,128)} %get-tuple-element.49), calls=%async_computation | async-start | bytes 327680 | tf_op jit(solution)/shard_map/all_to_all | solution.py:484
  11.0 9.3 %collective-permute-start.4 = (f32[17,4,128]{2,1,0:T(4,128)S(1)}, f32[17,4,128]{2,1,0:T(4,128)S(1)}, u32[]{:S(2)}, u32[]{:S(2)}) collective-permute-start(f32[17,4,128]{2,1,0:T(4,128)S(1)} %get-tuple-element.46), channel_id=1, source_target_pairs={{0,8},{1,9},{2,10},{3,11},{4,12},{5,13},{6,14},{7,15},{8,16},{9,17... | collective-permute-start | bytes 104456 | tf_op jit(solution)/shard_map/ppermute | solution.py:434
  13.8 6.5 %collective-permute-start.5 = (f32[17,4,128]{2,1,0:T(4,128)S(1)}, f32[17,4,128]{2,1,0:T(4,128)S(1)}, u32[]{:S(2)}, u32[]{:S(2)}) collective-permute-start(f32[17,4,128]{2,1,0:T(4,128)S(1)} %get-tuple-element.47), channel_id=1, source_target_pairs={{0,24},{1,25},{2,26},{3,27},{4,28},{5,29},{6,30},{7,31},{8,0},{9,1... | collective-permute-start | bytes 104456 | tf_op jit(solution)/shard_map/ppermute | solution.py:434
  18.7 1.6 %copy-start.1 = (f32[3,128,128]{2,1,0:T(8,128)S(1)}, f32[3,128,128]{2,1,0:T(8,128)}, u32[]{:S(2)}) copy-start(f32[3,128,128]{2,1,0:T(8,128)} %operator.1) | copy-start | bytes 589828
  22.5 4.9 %collective-permute-start.6 = (f32[136,128]{1,0:T(8,128)S(1)}, f32[136,128]{1,0:T(8,128)S(1)}, u32[]{:S(2)}, u32[]{:S(2)}) collective-permute-start(f32[136,128]{1,0:T(8,128)S(1)} %get-tuple-element.51), channel_id=1, source_target_pairs={{0,1},{1,0},{2,3},{3,2},{4,5},{5,4},{6,7},{7,6},{8,9},{9,8},{10,11... | collective-permute-start | bytes 208904 | tf_op jit(solution)/shard_map/ppermute | solution.py:434
  22.5 5.3 %collective-permute-start.7 = (f32[136,128]{1,0:T(8,128)S(1)}, f32[136,128]{1,0:T(8,128)S(1)}, u32[]{:S(2)}, u32[]{:S(2)}) collective-permute-start(f32[136,128]{1,0:T(8,128)S(1)} %get-tuple-element.51), channel_id=1, source_target_pairs={{0,16},{1,2},{2,1},{3,4},{4,3},{5,6},{6,5},{7,23},{8,24},{9,10},{1... | collective-permute-start | bytes 208904 | tf_op jit(solution)/shard_map/ppermute | solution.py:434
  23.4 12.0 %all-to-all-start.1 = ((f32[8,16,128]{2,1,0:T(8,128)}), f32[8,16,128]{2,1,0:T(8,128)S(1)}, u32[]{:S(2)}, u32[]{:S(2)}) async-start(f32[8,16,128]{2,1,0:T(8,128)} %bitcast.7), calls=%async_computation.1 | async-start | bytes 131072 | tf_op jit(solution)/shard_map/all_to_all | solution.py:511
  28.0 5.8 %collective-permute-start.8 = (f32[16,4,128]{2,1,0:T(4,128)S(1)}, f32[16,4,128]{2,1,0:T(4,128)S(1)}, u32[]{:S(2)}, u32[]{:S(2)}) collective-permute-start(f32[16,4,128]{2,1,0:T(4,128)S(1)} %get-tuple-element.58), channel_id=1, source_target_pairs={{0,8},{1,9},{2,10},{3,11},{4,12},{5,13},{6,14},{7,15},{8,16},{9,17... | collective-permute-start | bytes 98312 | tf_op jit(solution)/shard_map/ppermute | solution.py:434
  29.5 4.3 %collective-permute-start.9 = (f32[16,4,128]{2,1,0:T(4,128)S(1)}, f32[16,4,128]{2,1,0:T(4,128)S(1)}, u32[]{:S(2)}, u32[]{:S(2)}) collective-permute-start(f32[16,4,128]{2,1,0:T(4,128)S(1)} %get-tuple-element.59), channel_id=1, source_target_pairs={{0,24},{1,25},{2,26},{3,27},{4,28},{5,29},{6,30},{7,31},{8,0},{9,1... | collective-permute-start | bytes 98312 | tf_op jit(solution)/shard_map/ppermute | solution.py:434
  31.8 1.9 %copy-start = (f32[4,32,8,128]{3,2,1,0:T(8,128)S(1)}, f32[4,32,8,128]{3,2,1,0:T(8,128)}, u32[]{:S(2)}) copy-start(f32[4,32,8,128]{3,2,1,0:T(8,128)} %param.9) | copy-start | bytes 1572868

commit v5 on v4

--- a/solution.py
+++ b/solution.py
@@ -17,6 +17,8 @@
 VMEM = pltpu.VMEM
 HBM = pltpu.HBM
 MIB = 1 << 20
+RIM_UNROLL = True
+BODY_UNROLL = 2
 EDGE_COST = 10**10
 EXPAND_COST = 10**8
 STATE_COST = 10**9
@@ -70,24 +72,39 @@
 def pack_kernel(
     inc_hbm, cl_hbm, ct_hbm, values, weights, columns_hbm, types_hbm, counts_hbm,
     own, coef, b_out, a_out, rim_b, rim_a, w_out, e_out, slots_out,
-    inc, cl, ct, raw, columns, types, counts, sems,
+    inc, cl, ct, raw, columns, types, counts, staged, sems,
 ):
     owners, bucket = (slots_out.shape[0], values.shape[1])
     moves = (
+        (columns_hbm, columns),
+        (types_hbm, types),
+        (counts_hbm, counts),
         (inc_hbm, inc),
         (cl_hbm, cl),
         (ct_hbm, ct),
-        (columns_hbm, columns),
-        (types_hbm, types),
-        (counts_hbm, counts),
-        (values, slots_out.at[:, pl.ds(0, bucket), :]),
-        (weights, slots_out.at[:, pl.ds(bucket, bucket), :]),
+        (values, staged.at[:, pl.ds(0, bucket), :]),
+        (weights, staged.at[:, pl.ds(bucket, bucket), :]),
+        (staged, slots_out),
     )
     copies = [pltpu.make_async_copy(src, dst, sems.at[n]) for n, (src, dst) in enumerate(moves)]
-    for copy in copies:
+    for copy in copies[:8]:
         copy.start()
     for copy in copies[:3]:
         copy.wait()
+    slots = columns.shape[1]
+    lane = iota((1, slots), 1)
+    limit = jnp.zeros((1, slots), jnp.int32)
+    for d in range(owners):
+        limit = jnp.where(lane // bucket == d, counts[d], limit)
+    code = jnp.where(lane % bucket < limit, columns[...] * 4 + types[...], -1).astype(F32)
+    for d in range(owners):
+        at = d * bucket
+        window = code[:, at // LANES * LANES : at // LANES * LANES + LANES]
+        moved = pltpu.roll(window, (-at) % LANES, 1)
+        staged[d, 2 * bucket : 2 * bucket + 8, :] = jnp.broadcast_to(moved, (8, LANES))
+    for copy in copies[3:8]:
+        copy.wait()
+    copies[8].start()
     fields = cl.shape[0] // ROWS
     even, _ = position()
     raw[...] = jnp.zeros(raw.shape, F32)
@@ -113,19 +130,7 @@
             out[STEPS + 1 + k] = raw[pl.ds(pl.multiple_of(8 * (STEPS + first + k), 8), 8), :]
         out[STEPS, 0:STEPS, :] = coef[0:STEPS, :]
         out[STEPS, STEPS : 2 * STEPS, :] = coef[LANES - STEPS : LANES, :]
-    for copy in copies[3:]:
-        copy.wait()
-    slots = columns.shape[1]
-    lane = iota((1, slots), 1)
-    limit = jnp.zeros((1, slots), jnp.int32)
-    for d in range(owners):
-        limit = jnp.where(lane // bucket == d, counts[d], limit)
-    code = jnp.where(lane % bucket < limit, columns[...] * 4 + types[...], -1).astype(F32)
-    for d in range(owners):
-        at = d * bucket
-        window = code[:, at // LANES * LANES : at // LANES * LANES + LANES]
-        moved = pltpu.roll(window, (-at) % LANES, 1)
-        slots_out[d, 2 * bucket : 2 * bucket + 8, :] = jnp.broadcast_to(moved, (8, LANES))
+    copies[8].wait()
 
 
 def edge_kernel(w_own, e_own, coef, rim_a, rim_b, w_out, e_out, co, raw):
@@ -173,7 +178,7 @@
         cc[p] = 1.0 - 2.0 * (a * a + b * b)
 
 
-def diffuse(f, spare, cl, ct, cc, store):
+def diffuse(f, spare, cl, ct, cc, store, unroll=1):
     regs = [pl.ds(8 * q, 8) for q in range(f.shape[1] // 8)]
     for step in range(STEPS):
         last = step == STEPS - 1
@@ -191,7 +196,7 @@
                     spare[p, at, :] = new
             return carry
 
-        lax.fori_loop(step + 1, PLANES - 1 - step, row, 0)
+        lax.fori_loop(step + 1, PLANES - 1 - step, row, 0, unroll=unroll)
         f, spare = (spare, f)
 
 
@@ -205,7 +210,7 @@
     def store(r, q, value):
         rim[STEPS + r, pl.ds(q, 8, stride=RIM), :] = value
 
-    diffuse(f, spare, cl, ct, cc, store)
+    diffuse(f, spare, cl, ct, cc, store, RIM_UNROLL)
 
 
 def body_cell(n, rows):
@@ -258,7 +263,7 @@
     def store(r, q, value):
         state[r, pl.ds(8 * q, 8), :] = value
 
-    diffuse(f, spare, cl, ct, cc, store)
+    diffuse(f, spare, cl, ct, cc, store, BODY_UNROLL)
 
 
 def observe_kernel(
@@ -380,10 +385,11 @@
     def store(r, q, value):
         smooth[r, pl.ds(q, 8, stride=BODY), :] = value
 
-    diffuse(f, spare, cl, ct, cc, store)
-
-
-def last_kernel(inc, smooth, rim_in, from_west, from_east, rl, rt, rc, out, rim, f, spare, wide):
+    diffuse(f, spare, cl, ct, cc, store, BODY_UNROLL)
+
+
+def last_kernel(inc, smooth, rim_in, from_west, from_east, rl, rt, rc, back, out, dep_out, rim, f, spare, wide):
+    dep_out[...] = back[...]
     rim[...] = rim_in[...]
     diffuse_rim(rim, f, spare, rl, rt, rc, from_west, from_east)
     for r in range(ROWS):
@@ -394,7 +400,7 @@
         out[at, :] = inc[at, :] - wide[...].T
 
 
-def call(kernel, outs, args, scratch=(), spaces=None, flops=0, limit=20):
+def call(kernel, outs, args, scratch=(), spaces=None, out_spaces=None, flops=0, limit=20):
     spaces = spaces or {}
     specs = [pl.BlockSpec(memory_space=spaces.get(n, VMEM)) for n in range(len(args))]
     size = 4 * sum(x.size for x in list(args) + list(outs))
@@ -403,7 +409,7 @@
         kernel,
         out_shape=outs,
         in_specs=specs,
-        out_specs=[pl.BlockSpec(memory_space=VMEM) for _ in outs],
+        out_specs=[pl.BlockSpec(memory_space=(out_spaces or {}).get(n, VMEM)) for n in range(len(outs))],
         scratch_shapes=list(scratch),
         compiler_params=pltpu.CompilerParams(vmem_limit_bytes=limit * MIB),
         cost_estimate=pl.CostEstimate(flops=flops, bytes_accessed=size, transcendentals=0),
@@ -472,9 +478,11 @@
             VMEM((1, slots), jnp.int32),
             VMEM((1, slots), jnp.int32),
             pltpu.SMEM(obs_counts.shape, jnp.int32),
-            pltpu.SemaphoreType.DMA((8,)),
+            VMEM((lats, 2 * bucket + 8, LANES), F32),
+            pltpu.SemaphoreType.DMA((9,)),
         ],
         spaces={n: HBM for n in range(8)},
+        out_spaces={8: pl.ANY},
     )
     rim_a = send(rim_a, inner)
     a_in = send(a_send, inner)
@@ -520,15 +528,14 @@
     smooth, rim = call(
         smooth_kernel, [block, ends], [forcing, a_in, b_in, wl, wt, wc], body_buffers, flops=SMOOTH_COST
     )
-    (gradient,) = call(
+    gradient, departures = call(
         last_kernel,
-        [shape(*inc.shape)],
-        [inc, smooth, rim, from_west, from_east, rl, rt, rc],
+        [shape(*inc.shape), shape(slots, LANES)],
+        [inc, smooth, rim, from_west, from_east, rl, rt, rc, back.reshape(slots, LANES)],
         rim_buffers + [VMEM((LANES, LANES), F32)],
         flops=10**8,
     )
-    gradient, back = lax.optimization_barrier((gradient, back))
-    return (gradient.reshape(increment.shape), back.reshape(slots, LANES))
+    return (gradient.reshape(increment.shape), departures)
 
 
 def solution(mesh):

time: 36.2 us -> 34.3 us (0.948)
  Pallas kernels: 10.8 us -> 9.3 us
  local copies, waits for them, and re-layouts: 0.64 us -> 0.01 us
    pallas_call x9, Pallas kernels: 10.8 us -> 9.3 us  [call(): pl.pallas_call(kernel, out_shape=outs, in_specs=specs, out_specs=[pl.Bloc...]
    unnamed x5 -> x4, local copies, waits for them, and re-layouts: 0.64 us -> 0.01 us
  transfers between devices with their start and end apart: 12 -> 12, of which waited for: 3 -> 4; matrix products, arithmetic and copies ran while one was open for 0% -> 0% of each run, Pallas kernels for 18% -> 14%
where the time goes in v5:
time: 34.3 us; the launch traced here: 34 us
  starting transfers between devices  21.8 us (64%)
  Pallas kernels  9.3 us (27%)
  waiting for transfers between devices  2.1 us (6%)
  between operations  0.78 us (2%)
    ppermute x10, starting transfers between devices, local(): send = lambda x, route: lax.ppermute(x, ('lon', 'lat'), route)  15.1 us
    pallas_call x9, Pallas kernels, call(): pl.pallas_call(kernel, out_shape=outs, in_specs=specs, out_specs=[pl.Bloc...  9.3 us
    all_to_all x1, starting transfers between devices, local(): lax.all_to_all(slots_send, 'lat', split_axis=0, concat_axis=0, tiled=True)  3.38 us
    all_to_all x1, starting transfers between devices, local(): lax.all_to_all(departures.reshape(lats, bucket, LANES), 'lat', split_axis...  3.35 us
    ppermute x10, waiting for transfers between devices, local(): send = lambda x, route: lax.ppermute(x, ('lon', 'lat'), route)  2.1 us
  transfers between devices with their start and end apart: 12, of which 4 were waited for; matrix products, arithmetic and copies ran while one was open for 0% of the time, Pallas kernels for 14%

profile of v5, /device:TPU:0, one launch (start us, length us, event | category | flops | bytes accessed | tf_op | source)
XLA Modules:
  0.0 34.0 jit_solution(8948983712381101346)
XLA Ops:
  0.6 1.8 %shard_map.104 = (f32[8,128,128]{2,1,0:T(8,128)S(1)}, f32[128,128]{1,0:T(8,128)S(1)}, f32[4,128,128]{2,1,0:T(8,128)S(1)}, f32[4,128,128]{2,1,0:T(8,128)S(1)}, f3...) custom-call(f32[1024,128]{1,0:T(8,128)} %bitcast.10, ...), custom_call_target="tpu_custom_call" | custom-call | bytes 2077728 | tf_op jit(solution)/shard_map/pallas_call | solution.py:408
  2.5 0.5 %collective-permute-start = (f32[4,128,128]{2,1,0:T(8,128)S(1)}, f32[4,128,128]{2,1,0:T(8,128)S(1)}, u32[]{:S(2)}, u32[]{:S(2)}) collective-permute-start(f32[4,128,128]{2,1,0:T(8,128)S(1)} %get-tuple-element.35), channel_id=1, source_target_pairs={{0,1},{1,0},{2,3},{3,2},{4,5},{5,4},{6,7},{7,6},{8,9},{9,8},{10,11... | collective-permute-start | bytes 786440 | tf_op jit(solution)/shard_map/ppermute | solution.py:440
  3.0 0.1 collective-permute-start.2
  3.1 4.0 %collective-permute-start.3 = (f32[9,8,128]{2,1,0:T(8,128)S(1)}, f32[9,8,128]{2,1,0:T(8,128)S(1)}, u32[]{:S(2)}, u32[]{:S(2)}) collective-permute-start(f32[9,8,128]{2,1,0:T(8,128)S(1)} %get-tuple-element.41), channel_id=1, source_target_pairs={{0,16},{1,2},{2,1},{3,4},{4,3},{5,6},{6,5},{7,23},{8,24},{9,10},{1... | collective-permute-start | bytes 110600 | tf_op jit(solution)/shard_map/ppermute | solution.py:440
  7.1 0.0 collective-permute-start.1
  7.1 3.4 %all-to-all-start = ((f32[8,40,128]{2,1,0:T(8,128)}), f32[8,40,128]{2,1,0:T(8,128)S(1)}, u32[]{:S(2)}, u32[]{:S(2)}) async-start(f32[8,40,128]{2,1,0:T(8,128)} %get-tuple-element.49), calls=%async_computation | async-start | bytes 327680 | tf_op jit(solution)/shard_map/all_to_all | solution.py:492
  10.5 0.1 shard_map.105
  10.7 2.8 %collective-permute-start.4 = (f32[17,4,128]{2,1,0:T(4,128)S(1)}, f32[17,4,128]{2,1,0:T(4,128)S(1)}, u32[]{:S(2)}, u32[]{:S(2)}) collective-permute-start(f32[17,4,128]{2,1,0:T(4,128)S(1)} %get-tuple-element.46), channel_id=1, source_target_pairs={{0,8},{1,9},{2,10},{3,11},{4,12},{5,13},{6,14},{7,15},{8,16},{9,17... | collective-permute-start | bytes 104456 | tf_op jit(solution)/shard_map/ppermute | solution.py:440
  13.5 2.8 %collective-permute-start.5 = (f32[17,4,128]{2,1,0:T(4,128)S(1)}, f32[17,4,128]{2,1,0:T(4,128)S(1)}, u32[]{:S(2)}, u32[]{:S(2)}) collective-permute-start(f32[17,4,128]{2,1,0:T(4,128)S(1)} %get-tuple-element.47), channel_id=1, source_target_pairs={{0,24},{1,25},{2,26},{3,27},{4,28},{5,29},{6,30},{7,31},{8,0},{9,1... | collective-permute-start | bytes 104456 | tf_op jit(solution)/shard_map/ppermute | solution.py:440
  16.3 0.7 %shard_map.106 = (f32[16,128,128]{2,1,0:T(8,128)S(1)}, f32[16,128,128]{2,1,0:T(8,128)S(1)}, f32[16,128,128]{2,1,0:T(8,128)S(1)}) custom-call(f32[128,128]{1,0:T(8,128)S(1)} %get-tuple-element.52.co), custom_call_target="tpu_custom_call" | custom-call | flops 100000000 | bytes 3211264 | tf_op jit(solution)/shard_map/pallas_call | solution.py:408
  17.0 1.3 %collective-permute-done.1.b_in = f32[4,128,128]{2,1,0:T(8,128)S(1)} collective-permute-done((f32[4,128,128]{2,1,0:T(8,128)S(1)}, f32[4,128,128]{2,1,0:T(8,128)S(1)}, u32[]{:S(2)}, u32[]{:S(2)}) %collective-permute-start.1) | collective-permute-done | bytes 262176 | tf_op jit(solution)/shard_map/ppermute | solution.py:440
  18.4 1.5 %shard_map.107.state_in = f32[8,128,128]{2,1,0:T(8,128)S(1)} custom-call(f32[8,128,128]{2,1,0:T(8,128)S(1)} %get-tuple-element.34.own, f32[4,128,128]{2,1,0:T(8,128)S(1)} %collective-permute-done.a_in, f32[4,128,128]{2,1,0:T(8,128)S(1)} %collective-permute-done.1.b_in, f32[16,128,128]{2,1,0:T(8,128)S(1)} %get-tuple-element.43.cl, ...), custom_call_target="tpu_custom_call" | custom-call | flops 1000000000 | bytes 4718592 | tf_op jit(solution)/shard_map/pallas_call | solution.py:408
  19.9 1.6 %shard_map.108 = (f32[128,128]{1,0:T(8,128)}, f32[136,128]{1,0:T(8,128)S(1)}, f32[8,128,128]{2,1,0:T(8,128)S(1)}, f32[16,24,128]{2,1,0:T(8,128)S(1)}, f32[16,24,...) custom-call(f32[8,128,128]{2,1,0:T(8,128)S(1)} %shard_map.107.state_in, f32[8,128,128]{2,1,0:T(8,128)S(1)} %get-tuple-element.34.own, ...), custom_call_target="tpu_custom_call" | custom-call | flops 100000000 | bytes 3317760 | tf_op jit(solution)/shard_map/pallas_call | solution.py:408
  21.5 0.9 %collective-permute-start.7 = (f32[136,128]{1,0:T(8,128)S(1)}, f32[136,128]{1,0:T(8,128)S(1)}, u32[]{:S(2)}, u32[]{:S(2)}) collective-permute-start(f32[136,128]{1,0:T(8,128)S(1)} %get-tuple-element.51), channel_id=1, source_target_pairs={{0,16},{1,2},{2,1},{3,4},{4,3},{5,6},{6,5},{7,23},{8,24},{9,10},{1... | collective-permute-start | bytes 208904 | tf_op jit(solution)/shard_map/ppermute | solution.py:440
  22.4 3.4 %all-to-all-start.1 = ((f32[8,16,128]{2,1,0:T(8,128)}), f32[8,16,128]{2,1,0:T(8,128)S(1)}, u32[]{:S(2)}, u32[]{:S(2)}) async-start(f32[8,16,128]{2,1,0:T(8,128)} %bitcast.7), calls=%async_computation.1 | async-start | bytes 131072 | tf_op jit(solution)/shard_map/all_to_all | solution.py:519
  25.8 0.7 %shard_map.109 = (f32[16,128,128]{2,1,0:T(8,128)S(1)}, f32[16,128,128]{2,1,0:T(8,128)S(1)}, f32[16,128,128]{2,1,0:T(8,128)S(1)}) custom-call(f32[128,128]{1,0:T(8,128)S(1)} %get-tuple-element.52.co), custom_call_target="tpu_custom_call" | custom-call | flops 100000000 | bytes 3211264 | tf_op jit(solution)/shard_map/pallas_call | solution.py:408
  26.5 0.3 collective-permute-done.7.b_in
  26.8 0.1 shard_map.111
  26.9 1.6 %collective-permute-start.8 = (f32[16,4,128]{2,1,0:T(4,128)S(1)}, f32[16,4,128]{2,1,0:T(4,128)S(1)}, u32[]{:S(2)}, u32[]{:S(2)}) collective-permute-start(f32[16,4,128]{2,1,0:T(4,128)S(1)} %get-tuple-element.58), channel_id=1, source_target_pairs={{0,8},{1,9},{2,10},{3,11},{4,12},{5,13},{6,14},{7,15},{8,16},{9,17... | collective-permute-start | bytes 98312 | tf_op jit(solution)/shard_map/ppermute | solution.py:440
  28.6 2.2 %collective-permute-start.9 = (f32[16,4,128]{2,1,0:T(4,128)S(1)}, f32[16,4,128]{2,1,0:T(4,128)S(1)}, u32[]{:S(2)}, u32[]{:S(2)}) collective-permute-start(f32[16,4,128]{2,1,0:T(4,128)S(1)} %get-tuple-element.59), channel_id=1, source_target_pairs={{0,24},{1,25},{2,26},{3,27},{4,28},{5,29},{6,30},{7,31},{8,0},{9,1... | collective-permute-start | bytes 98312 | tf_op jit(solution)/shard_map/ppermute | solution.py:440
  30.8 1.5 %shard_map.110 = (f32[8,128,128]{2,1,0:T(8,128)S(1)}, f32[16,24,128]{2,1,0:T(8,128)S(1)}) custom-call(f32[8,128,128]{2,1,0:T(8,128)S(1)} %get-tuple-element.50.f_in, f32[136,128]{1,0:T(8,128)S(1)} %collective-permute-done.6.a_in, f32[136,128]{1,0:T(8,128)S(1)} %collective-permute-done.7.b_in, f32[16,128,128]{2,1,0:T(8,128)S(1)} %get-tuple-element.53.cl, ...), custom_call_target="tpu_custom_call" | custom-call | flops 10000000000 | bytes 4530176 | tf_op jit(solution)/shard_map/pallas_call | solution.py:408
  32.3 0.4 %collective-permute-done.8.from_west = f32[16,4,128]{2,1,0:T(4,128)S(1)} collective-permute-done((f32[16,4,128]{2,1,0:T(4,128)S(1)}, f32[16,4,128]{2,1,0:T(4,128)S(1)}, u32[]{:S(2)}, u32[]{:S(2)}) %collective-permute-start.8) | collective-permute-done | bytes 32800 | tf_op jit(solution)/shard_map/ppermute | solution.py:440
  32.7 0.1 collective-permute-done.9.from_east
  32.8 1.2 %shard_map.112 = (f32[1024,128]{1,0:T(8,128)}, f32[128,128]{1,0:T(8,128)}) custom-call(f32[1024,128]{1,0:T(8,128)S(1)} %bitcast.11, f32[8,128,128]{2,1,0:T(8,128)S(1)} %get-tuple-element.56.smooth, f32[16,24,128]{2,1,0:T(8,128)S(1)} %get-tuple-element.57.rim_in, f32[16,4,128]{2,1,0:T(4,128)S(1)} %collective-permute-done.8.from_west, ...), custom_call_target="tpu_custom_call" | custom-call | flops 100000000 | bytes 2555904 | tf_op jit(solution)/shard_map/pallas_call | solution.py:408
  (13 shorter events, 0.0 us)
Async XLA Ops:
  2.5 4.6 %collective-permute-start = (f32[4,128,128]{2,1,0:T(8,128)S(1)}, f32[4,128,128]{2,1,0:T(8,128)S(1)}, u32[]{:S(2)}, u32[]{:S(2)}) collective-permute-start(f32[4,128,128]{2,1,0:T(8,128)S(1)} %get-tuple-element.35), channel_id=1, source_target_pairs={{0,1},{1,0},{2,3},{3,2},{4,5},{5,4},{6,7},{7,6},{8,9},{9,8},{10,11... | collective-permute-start | bytes 786440 | tf_op jit(solution)/shard_map/ppermute | solution.py:440
  3.0 7.5 %collective-permute-start.2 = (f32[9,8,128]{2,1,0:T(8,128)S(1)}, f32[9,8,128]{2,1,0:T(8,128)S(1)}, u32[]{:S(2)}, u32[]{:S(2)}) collective-permute-start(f32[9,8,128]{2,1,0:T(8,128)S(1)} %get-tuple-element.40), channel_id=1, source_target_pairs={{0,1},{1,0},{2,3},{3,2},{4,5},{5,4},{6,7},{7,6},{8,9},{9,8},{10,11... | collective-permute-start | bytes 110600 | tf_op jit(solution)/shard_map/ppermute | solution.py:440
  3.1 7.5 %collective-permute-start.3 = (f32[9,8,128]{2,1,0:T(8,128)S(1)}, f32[9,8,128]{2,1,0:T(8,128)S(1)}, u32[]{:S(2)}, u32[]{:S(2)}) collective-permute-start(f32[9,8,128]{2,1,0:T(8,128)S(1)} %get-tuple-element.41), channel_id=1, source_target_pairs={{0,16},{1,2},{2,1},{3,4},{4,3},{5,6},{6,5},{7,23},{8,24},{9,10},{1... | collective-permute-start | bytes 110600 | tf_op jit(solution)/shard_map/ppermute | solution.py:440
  7.1 11.3 %collective-permute-start.1 = (f32[4,128,128]{2,1,0:T(8,128)S(1)}, f32[4,128,128]{2,1,0:T(8,128)S(1)}, u32[]{:S(2)}, u32[]{:S(2)}) collective-permute-start(f32[4,128,128]{2,1,0:T(8,128)S(1)} %get-tuple-element.36), channel_id=1, source_target_pairs={{0,16},{1,2},{2,1},{3,4},{4,3},{5,6},{6,5},{7,23},{8,24},{9,10},{1... | collective-permute-start | bytes 786440 | tf_op jit(solution)/shard_map/ppermute | solution.py:440
  7.1 12.7 %all-to-all-start = ((f32[8,40,128]{2,1,0:T(8,128)}), f32[8,40,128]{2,1,0:T(8,128)S(1)}, u32[]{:S(2)}, u32[]{:S(2)}) async-start(f32[8,40,128]{2,1,0:T(8,128)} %get-tuple-element.49), calls=%async_computation | async-start | bytes 327680 | tf_op jit(solution)/shard_map/all_to_all | solution.py:492
  10.7 9.2 %collective-permute-start.4 = (f32[17,4,128]{2,1,0:T(4,128)S(1)}, f32[17,4,128]{2,1,0:T(4,128)S(1)}, u32[]{:S(2)}, u32[]{:S(2)}) collective-permute-start(f32[17,4,128]{2,1,0:T(4,128)S(1)} %get-tuple-element.46), channel_id=1, source_target_pairs={{0,8},{1,9},{2,10},{3,11},{4,12},{5,13},{6,14},{7,15},{8,16},{9,17... | collective-permute-start | bytes 104456 | tf_op jit(solution)/shard_map/ppermute | solution.py:440
  13.5 6.4 %collective-permute-start.5 = (f32[17,4,128]{2,1,0:T(4,128)S(1)}, f32[17,4,128]{2,1,0:T(4,128)S(1)}, u32[]{:S(2)}, u32[]{:S(2)}) collective-permute-start(f32[17,4,128]{2,1,0:T(4,128)S(1)} %get-tuple-element.47), channel_id=1, source_target_pairs={{0,24},{1,25},{2,26},{3,27},{4,28},{5,29},{6,30},{7,31},{8,0},{9,1... | collective-permute-start | bytes 104456 | tf_op jit(solution)/shard_map/ppermute | solution.py:440
  18.4 1.5 %copy-start.1 = (f32[3,128,128]{2,1,0:T(8,128)S(1)}, f32[3,128,128]{2,1,0:T(8,128)}, u32[]{:S(2)}) copy-start(f32[3,128,128]{2,1,0:T(8,128)} %operator.1) | copy-start | bytes 589828
  21.5 5.0 %collective-permute-start.6 = (f32[136,128]{1,0:T(8,128)S(1)}, f32[136,128]{1,0:T(8,128)S(1)}, u32[]{:S(2)}, u32[]{:S(2)}) collective-permute-start(f32[136,128]{1,0:T(8,128)S(1)} %get-tuple-element.51), channel_id=1, source_target_pairs={{0,1},{1,0},{2,3},{3,2},{4,5},{5,4},{6,7},{7,6},{8,9},{9,8},{10,11... | collective-permute-start | bytes 208904 | tf_op jit(solution)/shard_map/ppermute | solution.py:440
  21.5 5.3 %collective-permute-start.7 = (f32[136,128]{1,0:T(8,128)S(1)}, f32[136,128]{1,0:T(8,128)S(1)}, u32[]{:S(2)}, u32[]{:S(2)}) collective-permute-start(f32[136,128]{1,0:T(8,128)S(1)} %get-tuple-element.51), channel_id=1, source_target_pairs={{0,16},{1,2},{2,1},{3,4},{4,3},{5,6},{6,5},{7,23},{8,24},{9,10},{1... | collective-permute-start | bytes 208904 | tf_op jit(solution)/shard_map/ppermute | solution.py:440
  22.4 9.9 %all-to-all-start.1 = ((f32[8,16,128]{2,1,0:T(8,128)}), f32[8,16,128]{2,1,0:T(8,128)S(1)}, u32[]{:S(2)}, u32[]{:S(2)}) async-start(f32[8,16,128]{2,1,0:T(8,128)} %bitcast.7), calls=%async_computation.1 | async-start | bytes 131072 | tf_op jit(solution)/shard_map/all_to_all | solution.py:519
  26.9 5.8 %collective-permute-start.8 = (f32[16,4,128]{2,1,0:T(4,128)S(1)}, f32[16,4,128]{2,1,0:T(4,128)S(1)}, u32[]{:S(2)}, u32[]{:S(2)}) collective-permute-start(f32[16,4,128]{2,1,0:T(4,128)S(1)} %get-tuple-element.58), channel_id=1, source_target_pairs={{0,8},{1,9},{2,10},{3,11},{4,12},{5,13},{6,14},{7,15},{8,16},{9,17... | collective-permute-start | bytes 98312 | tf_op jit(solution)/shard_map/ppermute | solution.py:440
  28.6 4.3 %collective-permute-start.9 = (f32[16,4,128]{2,1,0:T(4,128)S(1)}, f32[16,4,128]{2,1,0:T(4,128)S(1)}, u32[]{:S(2)}, u32[]{:S(2)}) collective-permute-start(f32[16,4,128]{2,1,0:T(4,128)S(1)} %get-tuple-element.59), channel_id=1, source_target_pairs={{0,24},{1,25},{2,26},{3,27},{4,28},{5,29},{6,30},{7,31},{8,0},{9,1... | collective-permute-start | bytes 98312 | tf_op jit(solution)/shard_map/ppermute | solution.py:440
  30.8 2.1 %copy-start = (f32[4,32,8,128]{3,2,1,0:T(8,128)S(1)}, f32[4,32,8,128]{3,2,1,0:T(8,128)}, u32[]{:S(2)}) copy-start(f32[4,32,8,128]{3,2,1,0:T(8,128)} %param.9) | copy-start | bytes 1572868

commit v6 on v5

--- a/solution.py
+++ b/solution.py
@@ -162,8 +162,9 @@
     co[...] = raw[...].T + coef[...]
 
 
-def expand(co, cl, ct, cc, regs=BODY):
-    high, low = split(jnp.concatenate([co[pl.ds(q, 8, stride=regs), :] for q in range(regs)], 0))
+def expand(co, cl, ct, cc):
+    parts = split(jnp.concatenate([co[pl.ds(q, 8, stride=BODY), :] for q in range(BODY)], 0))
+    both_parts = jnp.concatenate(parts, 1)
     tall = 2 * LANES - 16
     row, col = (iota((tall, 2 * LANES), 0), iota((tall, 2 * LANES), 1))
     wanted = LANES - 16 + col // LANES * 4 + col % LANES // (LANES // 4)
@@ -171,29 +172,48 @@
     for p in range(PLANES):
         first = LANES - 16 - p // 2 * 16
         pick = picks[p % 2][first : first + LANES, :]
-        both = matmul(high, pick) + matmul(low, pick)
+        both = matmul(both_parts, jnp.concatenate([pick, pick], 0))
         a, b = (both[:, :LANES], both[:, LANES:])
         cl[p] = a
         ct[p] = b
         cc[p] = 1.0 - 2.0 * (a * a + b * b)
 
 
+def expand_rim(co, cl, ct, cc):
+    wide = jnp.concatenate([co[pl.ds(q, 8, stride=RIM), :] for q in range(RIM)], 0)
+    tall = jnp.concatenate([pltpu.roll(wide, (-8 * p) % LANES, 1) for p in range(PLANES)], 0)
+    row, col = (iota((LANES, 2 * LANES), 0), iota((LANES, 2 * LANES), 1))
+    pick = jnp.where(row == col // LANES * 4 + col % LANES // (LANES // 4), 1.0, 0.0).astype(jnp.bfloat16)
+    both = matmul(jnp.concatenate(split(tall), 1), jnp.concatenate([pick, pick], 0))
+    for p in range(PLANES):
+        a = both[2 * SIDE * p : 2 * SIDE * (p + 1), :LANES]
+        b = both[2 * SIDE * p : 2 * SIDE * (p + 1), LANES:]
+        cl[p] = a
+        ct[p] = b
+        cc[p] = 1.0 - 2.0 * (a * a + b * b)
+
+
+def relax(p, f, cl, ct, cc, emit):
+    regs = [pl.ds(8 * q, 8) for q in range(f.shape[1] // 8)]
+    here = [f[p, at, :] for at in regs]
+    g = [cl[p, at, :] * x for at, x in zip(regs, here)]
+    g = [pltpu.roll(g[-1], 1, 0)] + g + [pltpu.roll(g[0], 7, 0)]
+    for q, at in enumerate(regs):
+        sides = ct[p + 1, at, :] * f[p + 1, at, :] + ct[p - 1, at, :] * f[p - 1, at, :]
+        emit(q, at, cc[p, at, :] * here[q] + cl[p, at, :] * (g[q] + g[q + 2]) + ct[p, at, :] * sides)
+
+
 def diffuse(f, spare, cl, ct, cc, store, unroll=1):
-    regs = [pl.ds(8 * q, 8) for q in range(f.shape[1] // 8)]
     for step in range(STEPS):
-        last = step == STEPS - 1
-
-        def row(p, carry, f=f, spare=spare, last=last):
-            here = [f[p, at, :] for at in regs]
-            g = [cl[p, at, :] * x for at, x in zip(regs, here)]
-            g = [pltpu.roll(g[-1], 1, 0)] + g + [pltpu.roll(g[0], 7, 0)]
-            for q, at in enumerate(regs):
-                sides = ct[p + 1, at, :] * f[p + 1, at, :] + ct[p - 1, at, :] * f[p - 1, at, :]
-                new = cc[p, at, :] * here[q] + cl[p, at, :] * (g[q] + g[q + 2]) + ct[p, at, :] * sides
+
+        def row(p, carry, f=f, spare=spare, last=step == STEPS - 1):
+            def emit(q, at, new):
                 if last:
                     store(p - STEPS, q, new)
                 else:
                     spare[p, at, :] = new
+
+            relax(p, f, cl, ct, cc, emit)
             return carry
 
         lax.fori_loop(step + 1, PLANES - 1 - step, row, 0, unroll=unroll)
@@ -248,53 +268,72 @@
     return ref[0:slots, :], jnp.concatenate(codes, 1)
 
 
-def state_kernel(own, a_in, b_in, cl, ct, cc, state, f, spare):
+def near_half_kernel(own, a_in, cl, ct, cc, part, strips, f, spare):
     even, pole = position()
-    a_base, b_base, _, _ = halo_places(even, pole)
-    sign = wind_sign(pole, (1, LANES))
+    a_base, _, _, _ = halo_places(even, pole)
     for q in range(BODY):
         at, to = (pl.ds(q, 8, stride=BODY), pl.ds(8 * q, 8))
         for k in range(STEPS):
             f[a_base + k, to, :] = a_in[k, at, :]
-            f[b_base + k, to, :] = b_in[jnp.where(pole, STEPS - 1 - k, k), at, :] * sign
         for r in range(ROWS):
             f[STEPS + r, to, :] = own[r, at, :]
-
-    def store(r, q, value):
-        state[r, pl.ds(8 * q, 8), :] = value
-
-    diffuse(f, spare, cl, ct, cc, store, BODY_UNROLL)
-
-
-def observe_kernel(
-    state_in, own, a_in, b_in, co, from_west, from_east, slots_in, operator,
-    dep_out, pay_out, f_out, rl, rt, rc,
-    rim, f, spare, co_rim, state,
-):
+    for step in range(STEPS):
+        low = jnp.where(even, STEPS + 1 + step, 1 + step)
+
+        def row(i, carry, f=f, spare=spare, low=low, last=step == STEPS - 1):
+            def emit(q, at, new):
+                if last:
+                    part[i, at, :] = new
+                else:
+                    spare[low + i, at, :] = new
+
+            relax(low + i, f, cl, ct, cc, emit)
+            return carry
+
+        lax.fori_loop(0, ROWS + 2 - 2 * step, row, 0, unroll=BODY_UNROLL)
+        if step < STEPS - 1:
+            first = jnp.where(even, STEPS + 1 + step, ROWS + 1 - step)
+            strips[step, 0] = spare[first]
+            strips[step, 1] = spare[first + 1]
+        f, spare = (spare, f)
+
+
+def far_half_kernel(own, b_in, strips, cl, ct, cc, part, f, spare):
     even, pole = position()
-    a_base, b_base, _, _ = halo_places(even, pole)
+    _, b_base, _, _ = halo_places(even, pole)
     sign = wind_sign(pole, (1, LANES))
-    co_rim[0:STEPS, :] = from_west[PLANES]
-    co_rim[STEPS:SIDE, :] = co[0:8, :]
-    co_rim[SIDE : 2 * SIDE - STEPS, :] = co[LANES - 8 : LANES, :]
-    co_rim[2 * SIDE - STEPS : 2 * SIDE, :] = from_east[PLANES]
-    expand(co_rim, rl, rt, rc, RIM)
-    sides = ((slice(STEPS, SIDE), slice(0, 8)), (slice(SIDE, 2 * SIDE - STEPS), slice(LANES - 8, LANES)))
-    for to, at in sides:
+    first = jnp.where(even, 0, ROWS - 2)
+    for q in range(BODY):
+        at, to = (pl.ds(q, 8, stride=BODY), pl.ds(8 * q, 8))
         for k in range(STEPS):
-            rim[a_base + k, to, :] = a_in[k, at, :]
-            rim[b_base + k, to, :] = b_in[jnp.where(pole, STEPS - 1 - k, k), at, :] * sign
-        for r in range(ROWS):
-            rim[STEPS + r, to, :] = own[r, at, :]
-    diffuse_rim(rim, f, spare, rl, rt, rc, from_west, from_east)
-    state[...] = state_in[...]
-    for r in range(ROWS):
-        state[r, pl.ds(0, STEPS, stride=8), :] = rim[STEPS + r, STEPS : 2 * STEPS, :]
-        last = rim[STEPS + r, 2 * SIDE - 2 * STEPS : 2 * SIDE - STEPS, :]
-        state[r, pl.ds(8 * (BODY - STEPS) + 7, STEPS, stride=8), :] = last
-
+            f[b_base + k, to, :] = b_in[jnp.where(pole, STEPS - 1 - k, k), at, :] * sign
+        for i in range(2):
+            f[STEPS + first + i, to, :] = own[first + i, at, :]
+    for step in range(STEPS):
+        low = jnp.where(even, 1 + step, PLANES - 1 - STEPS - step)
+
+        def row(i, carry, f=f, spare=spare, low=low, last=step == STEPS - 1):
+            def emit(q, at, new):
+                if last:
+                    part[i, at, :] = new
+                else:
+                    spare[low + i, at, :] = new
+
+            relax(low + i, f, cl, ct, cc, emit)
+            return carry
+
+        lax.fori_loop(0, STEPS, row, 0, unroll=BODY_UNROLL)
+        if step < STEPS - 1:
+            first = jnp.where(even, STEPS + 1 + step, ROWS + 1 - step)
+            spare[first] = strips[step, 0]
+            spare[first + 1] = strips[step, 1]
+        f, spare = (spare, f)
+
+
+def gather_kernel(near_half, far_half, slots_in, operator, column, code_out, row_out, forward, backward):
     owners, bucket = (slots_in.shape[0], (slots_in.shape[1] - 8) // 2)
     slots = owners * bucket
+    even, _ = position()
     lane = iota((1, LANES), 1)
     per_tile = LANES // bucket
     code_parts = []
@@ -304,51 +343,92 @@
             got = slots_in[t * per_tile + n, 2 * bucket : 2 * bucket + 1, :]
             part = jnp.where(lane // bucket == n, pltpu.roll(got, n * bucket, 1), part)
         code_parts.append(part)
-        pay_out[slots + 8 * t : slots + 8 * t + 8, :] = jnp.broadcast_to(part, (8, LANES))
-    code_row = jnp.concatenate(code_parts, 1)
+        row_out[8 * t : 8 * t + 8, :] = jnp.broadcast_to(part, (8, LANES))
     code = jnp.concatenate([jnp.broadcast_to(part, (LANES, LANES)).T for part in code_parts], 0)
     code = code.astype(jnp.int32)
+    code_out[...] = code
     cell = jnp.where(code >= 0, code >> 2, -1)
-    kind = jnp.where(code >= 0, code & 3, -1)
-
-    depth = ROWS * LANES
-    places = body_cell(iota((1, depth), 1), range(ROWS))
-    hot = jnp.concatenate(
-        [
-            jnp.where(places[:, t : t + LANES] == cell, 1.0, 0.0).astype(jnp.bfloat16)
-            for t in range(0, depth, LANES)
-        ],
-        1,
-    )
-    cells = jnp.concatenate(split(state[...].reshape(depth, LANES)), 1)
-    column = halves(matmul(hot, cells))
-
-    masks = [kind == n for n in range(3)]
+    half = STEPS * LANES
+    near_row = jnp.where(even, ROWS - STEPS, 0)
+    places = iota((1, half), 1)
+    ends = (places % 8 == 0) & (places % LANES < 8 * STEPS) | (places % 8 == 7) & (places % LANES >= LANES - 8 * STEPS)
+    total = None
+    for ref, first in ((near_half, near_row), (far_half, ROWS - STEPS - near_row)):
+        cells = jnp.where(ends, -2, body_cell(places, [first + k for k in range(STEPS)]))
+        hot = jnp.concatenate(
+            [
+                jnp.where(cells[:, t : t + LANES] == cell, 1.0, 0.0).astype(jnp.bfloat16)
+                for t in range(0, half, LANES)
+            ],
+            1,
+        )
+        got = matmul(hot, jnp.concatenate(split(ref[...].reshape(half, LANES)), 1))
+        total = got if total is None else total + got
+    column[...] = halves(total)
     op_high, op_low = split(operator[...])
     zero = jnp.zeros((LANES, LANES), jnp.bfloat16)
-
-    def by_kind(x):
-        return jnp.concatenate([jnp.where(m, part, jnp.zeros_like(part)) for part in split(x) for m in masks], 1)
-
-    forward = jnp.concatenate(
+    forward[...] = jnp.concatenate(
         [jnp.concatenate([op_high[n], op_low[n]], 1) for n in range(3)]
         + [jnp.concatenate([op_high[n], zero], 1) for n in range(3)],
         0,
     )
-    model = halves(matmul(by_kind(column), forward))
-    values = slots_in[:, 0:bucket, :].reshape(slots, LANES)
-    weights = slots_in[:, bucket : 2 * bucket, :].reshape(slots, LANES)
-    departures = jnp.where(code >= 0, values - model, 0.0)
-    dep_out[...] = departures
-    backward = jnp.concatenate(
+    backward[...] = jnp.concatenate(
         [
             jnp.concatenate([op_high[0], op_high[1], op_high[2]] * 2, 1),
             jnp.concatenate([op_low[0], op_low[1], op_low[2], zero, zero, zero], 1),
         ],
         0,
     )
-    adjoint = halves(matmul(by_kind(weights * departures), backward, ((1,), (1,))))
+
+
+def observe_kernel(
+    column_in, code_in, row_in, forward, backward, own, a_in, b_in, co, from_west, from_east, slots_in,
+    dep_out, pay_out, f_out, rl, rt, rc,
+    rim, f, spare, co_rim, ends,
+):
+    even, pole = position()
+    a_base, b_base, _, _ = halo_places(even, pole)
+    sign = wind_sign(pole, (1, LANES))
+    co_rim[0:STEPS, :] = from_west[PLANES]
+    co_rim[STEPS:SIDE, :] = co[0:8, :]
+    co_rim[SIDE : 2 * SIDE - STEPS, :] = co[LANES - 8 : LANES, :]
+    co_rim[2 * SIDE - STEPS : 2 * SIDE, :] = from_east[PLANES]
+    expand_rim(co_rim, rl, rt, rc)
+    sides = ((slice(STEPS, SIDE), slice(0, 8)), (slice(SIDE, 2 * SIDE - STEPS), slice(LANES - 8, LANES)))
+    for to, at in sides:
+        for k in range(STEPS):
+            rim[a_base + k, to, :] = a_in[k, at, :]
+            rim[b_base + k, to, :] = b_in[jnp.where(pole, STEPS - 1 - k, k), at, :] * sign
+        for r in range(ROWS):
+            rim[STEPS + r, to, :] = own[r, at, :]
+    diffuse_rim(rim, f, spare, rl, rt, rc, from_west, from_east)
+    slots = column_in.shape[0]
+    bucket = (slots_in.shape[1] - 8) // 2
+    code = code_in[...]
+    cell = jnp.where(code >= 0, code >> 2, -1)
+    kind = jnp.where(code >= 0, code & 3, -1)
+    for r in range(ROWS):
+        ends[8 * r : 8 * r + STEPS, :] = rim[STEPS + r, STEPS : 2 * STEPS, :]
+        ends[8 * r + STEPS : 8 * r + 8, :] = rim[STEPS + r, 2 * SIDE - 2 * STEPS : 2 * SIDE - STEPS, :]
+    ends[8 * ROWS : LANES, :] = jnp.zeros((LANES - 8 * ROWS, LANES), F32)
+    hot = jnp.where(edge_cell(iota((1, LANES), 1), range(ROWS)) == cell, 1.0, 0.0).astype(jnp.bfloat16)
+    column = column_in[...] + halves(matmul(hot, jnp.concatenate(split(ends[...]), 1)))
+
+    masks = [kind == n for n in range(3)]
+
+    def by_kind(x):
+        return jnp.concatenate([jnp.where(m, part, jnp.zeros_like(part)) for part in split(x) for m in masks], 1)
+
+    model = halves(matmul(by_kind(column), forward[...]))
+    values = slots_in[:, 0:bucket, :].reshape(slots, LANES)
+    weights = slots_in[:, bucket : 2 * bucket, :].reshape(slots, LANES)
+    departures = jnp.where(code >= 0, values - model, 0.0)
+    dep_out[...] = departures
+    adjoint = halves(matmul(by_kind(weights * departures), backward[...], ((1,), (1,))))
     pay_out[0:slots, :] = adjoint
+    pay_out[slots:, :] = row_in[...]
+    code_row = jnp.concatenate([row_in[8 * t : 8 * t + 1, :] for t in range(slots // LANES)], 1)
+    depth = ROWS * LANES
     f_out[...] = scatter(adjoint, code_row, body_cell(iota((depth, LANES), 0), range(ROWS))).reshape(f_out.shape)
 
 
@@ -506,12 +586,34 @@
     from_west = send(e_send, east)
     from_east = send(w_send, west)
     wl, wt, wc = call(expand, [planes, planes, planes], [co], flops=EXPAND_COST)
-    (state,) = call(state_kernel, [block], [own, a_in, b_in, wl, wt, wc], body_buffers, flops=STATE_COST)
+    half = shape(STEPS, LANES, LANES)
+    near_half, strips = call(
+        near_half_kernel,
+        [half, shape(STEPS - 1, 2, LANES, LANES)],
+        [own, a_in, wl, wt, wc],
+        body_buffers,
+        flops=STATE_COST,
+    )
+    (far_half,) = call(
+        far_half_kernel, [half], [own, b_in, strips, wl, wt, wc], body_buffers, flops=10**8
+    )
+    column, code, code_row, forward, backward = call(
+        gather_kernel,
+        [
+            shape(slots, LANES),
+            jax.ShapeDtypeStruct((slots, LANES), jnp.int32),
+            shape(8 * tiles, LANES),
+            jax.ShapeDtypeStruct((6 * LANES, 2 * LANES), jnp.bfloat16),
+            jax.ShapeDtypeStruct((2 * LANES, 6 * LANES), jnp.bfloat16),
+        ],
+        [near_half, far_half, slots_in, obs_operator],
+        flops=10**8,
+    )
     departures, payload, forcing, rl, rt, rc = call(
         observe_kernel,
         [shape(slots, LANES), shape(slots + 8 * tiles, LANES), block, ends, ends, ends],
-        [state, own, a_in, b_in, co, from_west, from_east, slots_in, obs_operator],
-        rim_buffers + [VMEM((2 * SIDE, LANES), F32), VMEM(block.shape, F32)],
+        [column, code, code_row, forward, backward, own, a_in, b_in, co, from_west, from_east, slots_in],
+        rim_buffers + [VMEM((2 * SIDE, LANES), F32), VMEM((LANES, LANES), F32)],
         flops=10**8,
     )
     a_in = send(payload, inner)

time: 34.3 us -> 34 us (level)
  waiting for transfers between devices: 2.1 us -> 1.41 us
    ppermute x10, waiting for transfers between devices: 2.1 us -> 1.4 us  [local(): send = lambda x, route: lax.ppermute(x, ('lon', 'lat'), route)]
    pallas_call x9 -> x11, Pallas kernels: 9.3 us -> 9.19 us  [call(): pl.pallas_call(kernel, out_shape=outs, in_specs=specs, out_specs=[pl.Bloc...]
  transfers between devices with their start and end apart: 12 -> 12, of which waited for: 4 -> 3; matrix products, arithmetic and copies ran while one was open for 0% -> 0% of each run, Pallas kernels for 14% -> 14%
where the time goes in v6:
time: 34 us; the launch traced here: 33.6 us
  starting transfers between devices  21.9 us (64%)
  Pallas kernels  9.19 us (27%)
  waiting for transfers between devices  1.41 us (4%)
  between operations  0.77 us (2%)
  local copies, waits for them, and re-layouts  0.34 us (1%)
    ppermute x10, starting transfers between devices, local(): send = lambda x, route: lax.ppermute(x, ('lon', 'lat'), route)  15.2 us
    pallas_call x11, Pallas kernels, call(): pl.pallas_call(kernel, out_shape=outs, in_specs=specs, out_specs=[pl.Bloc...  9.19 us
    all_to_all x1, starting transfers between devices, local(): lax.all_to_all(slots_send, 'lat', split_axis=0, concat_axis=0, tiled=True)  3.38 us
    all_to_all x1, starting transfers between devices, local(): lax.all_to_all(departures.reshape(lats, bucket, LANES), 'lat', split_axis...  3.35 us
    ppermute x10, waiting for transfers between devices, local(): send = lambda x, route: lax.ppermute(x, ('lon', 'lat'), route)  1.4 us
  transfers between devices with their start and end apart: 12, of which 3 were waited for; matrix products, arithmetic and copies ran while one was open for 0% of the time, Pallas kernels for 14%

profile of v6, /device:TPU:0, one launch (start us, length us, event | category | flops | bytes accessed | tf_op | source)
XLA Modules:
  0.0 33.6 jit_solution(13392811872061034925)
XLA Ops:
  0.6 1.8 %shard_map.104 = (f32[8,128,128]{2,1,0:T(8,128)S(1)}, f32[128,128]{1,0:T(8,128)S(1)}, f32[4,128,128]{2,1,0:T(8,128)S(1)}, f32[4,128,128]{2,1,0:T(8,128)S(1)}, f3...) custom-call(f32[1024,128]{1,0:T(8,128)} %bitcast.10, ...), custom_call_target="tpu_custom_call" | custom-call | bytes 2077728 | tf_op jit(solution)/shard_map/pallas_call | solution.py:488
  2.5 0.5 %collective-permute-start = (f32[4,128,128]{2,1,0:T(8,128)S(1)}, f32[4,128,128]{2,1,0:T(8,128)S(1)}, u32[]{:S(2)}, u32[]{:S(2)}) collective-permute-start(f32[4,128,128]{2,1,0:T(8,128)S(1)} %get-tuple-element.42), channel_id=1, source_target_pairs={{0,1},{1,0},{2,3},{3,2},{4,5},{5,4},{6,7},{7,6},{8,9},{9,8},{10,11... | collective-permute-start | bytes 786440 | tf_op jit(solution)/shard_map/ppermute | solution.py:520
  3.1 4.0 %collective-permute-start.2 = (f32[9,8,128]{2,1,0:T(8,128)S(1)}, f32[9,8,128]{2,1,0:T(8,128)S(1)}, u32[]{:S(2)}, u32[]{:S(2)}) collective-permute-start(f32[9,8,128]{2,1,0:T(8,128)S(1)} %get-tuple-element.47), channel_id=1, source_target_pairs={{0,16},{1,2},{2,1},{3,4},{4,3},{5,6},{6,5},{7,23},{8,24},{9,10},{1... | collective-permute-start | bytes 110600 | tf_op jit(solution)/shard_map/ppermute | solution.py:520
  7.1 3.4 %all-to-all-start = ((f32[8,40,128]{2,1,0:T(8,128)}), f32[8,40,128]{2,1,0:T(8,128)S(1)}, u32[]{:S(2)}, u32[]{:S(2)}) async-start(f32[8,40,128]{2,1,0:T(8,128)} %get-tuple-element.56), calls=%async_computation | async-start | bytes 327680 | tf_op jit(solution)/shard_map/all_to_all | solution.py:572
  10.5 0.1 shard_map.105
  10.7 2.8 %collective-permute-start.4 = (f32[17,4,128]{2,1,0:T(4,128)S(1)}, f32[17,4,128]{2,1,0:T(4,128)S(1)}, u32[]{:S(2)}, u32[]{:S(2)}) collective-permute-start(f32[17,4,128]{2,1,0:T(4,128)S(1)} %get-tuple-element.62), channel_id=1, source_target_pairs={{0,8},{1,9},{2,10},{3,11},{4,12},{5,13},{6,14},{7,15},{8,16},{9,17... | collective-permute-start | bytes 104456 | tf_op jit(solution)/shard_map/ppermute | solution.py:520
  13.5 2.8 %collective-permute-start.5 = (f32[17,4,128]{2,1,0:T(4,128)S(1)}, f32[17,4,128]{2,1,0:T(4,128)S(1)}, u32[]{:S(2)}, u32[]{:S(2)}) collective-permute-start(f32[17,4,128]{2,1,0:T(4,128)S(1)} %get-tuple-element.63), channel_id=1, source_target_pairs={{0,24},{1,25},{2,26},{3,27},{4,28},{5,29},{6,30},{7,31},{8,0},{9,1... | collective-permute-start | bytes 104456 | tf_op jit(solution)/shard_map/ppermute | solution.py:520
  16.3 0.5 %shard_map.106 = (f32[16,128,128]{2,1,0:T(8,128)S(1)}, f32[16,128,128]{2,1,0:T(8,128)S(1)}, f32[16,128,128]{2,1,0:T(8,128)S(1)}) custom-call(f32[128,128]{1,0:T(8,128)S(1)} %get-tuple-element.66.co), custom_call_target="tpu_custom_call" | custom-call | flops 100000000 | bytes 3211264 | tf_op jit(solution)/shard_map/pallas_call | solution.py:488
  16.8 1.0 %shard_map.107 = (f32[4,128,128]{2,1,0:T(8,128)S(1)}, f32[3,2,128,128]{3,2,1,0:T(8,128)S(1)}) custom-call(f32[8,128,128]{2,1,0:T(8,128)S(1)} %get-tuple-element.41.own, f32[4,128,128]{2,1,0:T(8,128)S(1)} %collective-permute-done.a_in, f32[16,128,128]{2,1,0:T(8,128)S(1)} %get-tuple-element.49.cl, f32[16,128,128]{2,1,0:T(8,128)S(1)} %get-tuple-element.50.ct, ...), custom_call_target="tpu_custom_call" | custom-call | flops 1000000000 | bytes 4587520 | tf_op jit(solution)/shard_map/pallas_call | solution.py:488
  17.8 0.5 %collective-permute-done.3.b_in = f32[4,128,128]{2,1,0:T(8,128)S(1)} collective-permute-done((f32[4,128,128]{2,1,0:T(8,128)S(1)}, f32[4,128,128]{2,1,0:T(8,128)S(1)}, u32[]{:S(2)}, u32[]{:S(2)}) %collective-permute-start.3) | collective-permute-done | bytes 262176 | tf_op jit(solution)/shard_map/ppermute | solution.py:520
  18.4 0.6 %shard_map.108.far_half = f32[4,128,128]{2,1,0:T(8,128)S(1)} custom-call(f32[8,128,128]{2,1,0:T(8,128)S(1)} %get-tuple-element.41.own, f32[4,128,128]{2,1,0:T(8,128)S(1)} %collective-permute-done.3.b_in, f32[3,2,128,128]{3,2,1,0:T(8,128)S(1)} %get-tuple-element.54.strips, f32[16,128,128]{2,1,0:T(8,128)S(1)} %get-tuple-element.49.cl, ...), custom_call_target="tpu_custom_call" | custom-call | flops 100000000 | bytes 4587520 | tf_op jit(solution)/shard_map/pallas_call | solution.py:488
  18.9 0.3 copy-done.1
  19.3 0.4 %shard_map.109 = (f32[128,128]{1,0:T(8,128)S(1)}, s32[128,128]{1,0:T(8,128)S(1)}, f32[8,128]{1,0:T(8,128)S(1)}, bf16[768,256]{1,0:T(8,128)(2,1)S(1)}, bf16[256,768]{1,0:T(8,128)(2,1)S(1)}) custom-call(f32[4,128,128]{2,1,0:T(8,128)S(1)} %get-tuple-element.52.near_half, f32[4,128,128]{2,1,0:T(8,128)S(1)} %shard_map.108.far_half, ...), custom_call_target="tpu_custom_call" | custom-call | flops 100000000 | bytes 2592768 | tf_op jit(solution)/shard_map/pallas_call | solution.py:488
  19.7 1.5 %shard_map.110 = (f32[128,128]{1,0:T(8,128)}, f32[136,128]{1,0:T(8,128)S(1)}, f32[8,128,128]{2,1,0:T(8,128)S(1)}, f32[16,24,128]{2,1,0:T(8,128)S(1)}, f32[16,24,...) custom-call(f32[128,128]{1,0:T(8,128)S(1)} %get-tuple-element.57.column_in, s32[128,128]{1,0:T(8,128)S(1)} %get-tuple-element.58.code_in, ...), custom_call_target="tpu_custom_call" | custom-call | flops 100000000 | bytes 4304896 | tf_op jit(solution)/shard_map/pallas_call | solution.py:488
  21.2 1.1 %collective-permute-start.7 = (f32[136,128]{1,0:T(8,128)S(1)}, f32[136,128]{1,0:T(8,128)S(1)}, u32[]{:S(2)}, u32[]{:S(2)}) collective-permute-start(f32[136,128]{1,0:T(8,128)S(1)} %get-tuple-element.65), channel_id=1, source_target_pairs={{0,16},{1,2},{2,1},{3,4},{4,3},{5,6},{6,5},{7,23},{8,24},{9,10},{1... | collective-permute-start | bytes 208904 | tf_op jit(solution)/shard_map/ppermute | solution.py:520
  22.2 3.4 %all-to-all-start.1 = ((f32[8,16,128]{2,1,0:T(8,128)}), f32[8,16,128]{2,1,0:T(8,128)S(1)}, u32[]{:S(2)}, u32[]{:S(2)}) async-start(f32[8,16,128]{2,1,0:T(8,128)} %bitcast.7), calls=%async_computation.1 | async-start | bytes 131072 | tf_op jit(solution)/shard_map/all_to_all | solution.py:621
  25.6 0.5 %shard_map.111 = (f32[16,128,128]{2,1,0:T(8,128)S(1)}, f32[16,128,128]{2,1,0:T(8,128)S(1)}, f32[16,128,128]{2,1,0:T(8,128)S(1)}) custom-call(f32[128,128]{1,0:T(8,128)S(1)} %get-tuple-element.66.co), custom_call_target="tpu_custom_call" | custom-call | flops 100000000 | bytes 3211264 | tf_op jit(solution)/shard_map/pallas_call | solution.py:488
  26.1 0.5 %collective-permute-done.7.b_in = f32[136,128]{1,0:T(8,128)S(1)} collective-permute-done((f32[136,128]{1,0:T(8,128)S(1)}, f32[136,128]{1,0:T(8,128)S(1)}, u32[]{:S(2)}, u32[]{:S(2)}) %collective-permute-start.7) | collective-permute-done | bytes 69664 | tf_op jit(solution)/shard_map/ppermute | solution.py:520
  26.6 0.1 shard_map.113
  26.7 1.4 %collective-permute-start.8 = (f32[16,4,128]{2,1,0:T(4,128)S(1)}, f32[16,4,128]{2,1,0:T(4,128)S(1)}, u32[]{:S(2)}, u32[]{:S(2)}) collective-permute-start(f32[16,4,128]{2,1,0:T(4,128)S(1)} %get-tuple-element.72), channel_id=1, source_target_pairs={{0,8},{1,9},{2,10},{3,11},{4,12},{5,13},{6,14},{7,15},{8,16},{9,17... | collective-permute-start | bytes 98312 | tf_op jit(solution)/shard_map/ppermute | solution.py:520
  28.1 2.4 %collective-permute-start.9 = (f32[16,4,128]{2,1,0:T(4,128)S(1)}, f32[16,4,128]{2,1,0:T(4,128)S(1)}, u32[]{:S(2)}, u32[]{:S(2)}) collective-permute-start(f32[16,4,128]{2,1,0:T(4,128)S(1)} %get-tuple-element.73), channel_id=1, source_target_pairs={{0,24},{1,25},{2,26},{3,27},{4,28},{5,29},{6,30},{7,31},{8,0},{9,1... | collective-permute-start | bytes 98312 | tf_op jit(solution)/shard_map/ppermute | solution.py:520
  30.6 1.5 %shard_map.112 = (f32[8,128,128]{2,1,0:T(8,128)S(1)}, f32[16,24,128]{2,1,0:T(8,128)S(1)}) custom-call(f32[8,128,128]{2,1,0:T(8,128)S(1)} %get-tuple-element.64.f_in, f32[136,128]{1,0:T(8,128)S(1)} %collective-permute-done.6.a_in, f32[136,128]{1,0:T(8,128)S(1)} %collective-permute-done.7.b_in, f32[16,128,128]{2,1,0:T(8,128)S(1)} %get-tuple-element.67.cl, ...), custom_call_target="tpu_custom_call" | custom-call | flops 10000000000 | bytes 4530176 | tf_op jit(solution)/shard_map/pallas_call | solution.py:488
  32.1 0.3 collective-permute-done.8.from_west
  32.5 1.2 %shard_map.114 = (f32[1024,128]{1,0:T(8,128)}, f32[128,128]{1,0:T(8,128)}) custom-call(f32[1024,128]{1,0:T(8,128)S(1)} %bitcast.11, f32[8,128,128]{2,1,0:T(8,128)S(1)} %get-tuple-element.70.smooth, f32[16,24,128]{2,1,0:T(8,128)S(1)} %get-tuple-element.71.rim_in, f32[16,4,128]{2,1,0:T(4,128)S(1)} %collective-permute-done.8.from_west, ...), custom_call_target="tpu_custom_call" | custom-call | flops 100000000 | bytes 2555904 | tf_op jit(solution)/shard_map/pallas_call | solution.py:488
  (15 shorter events, 0.1 us)
Async XLA Ops:
  2.5 4.6 %collective-permute-start = (f32[4,128,128]{2,1,0:T(8,128)S(1)}, f32[4,128,128]{2,1,0:T(8,128)S(1)}, u32[]{:S(2)}, u32[]{:S(2)}) collective-permute-start(f32[4,128,128]{2,1,0:T(8,128)S(1)} %get-tuple-element.42), channel_id=1, source_target_pairs={{0,1},{1,0},{2,3},{3,2},{4,5},{5,4},{6,7},{7,6},{8,9},{9,8},{10,11... | collective-permute-start | bytes 786440 | tf_op jit(solution)/shard_map/ppermute | solution.py:520
  3.0 7.5 %collective-permute-start.1 = (f32[9,8,128]{2,1,0:T(8,128)S(1)}, f32[9,8,128]{2,1,0:T(8,128)S(1)}, u32[]{:S(2)}, u32[]{:S(2)}) collective-permute-start(f32[9,8,128]{2,1,0:T(8,128)S(1)} %get-tuple-element.46), channel_id=1, source_target_pairs={{0,1},{1,0},{2,3},{3,2},{4,5},{5,4},{6,7},{7,6},{8,9},{9,8},{10,11... | collective-permute-start | bytes 110600 | tf_op jit(solution)/shard_map/ppermute | solution.py:520
  3.1 7.5 %collective-permute-start.2 = (f32[9,8,128]{2,1,0:T(8,128)S(1)}, f32[9,8,128]{2,1,0:T(8,128)S(1)}, u32[]{:S(2)}, u32[]{:S(2)}) collective-permute-start(f32[9,8,128]{2,1,0:T(8,128)S(1)} %get-tuple-element.47), channel_id=1, source_target_pairs={{0,16},{1,2},{2,1},{3,4},{4,3},{5,6},{6,5},{7,23},{8,24},{9,10},{1... | collective-permute-start | bytes 110600 | tf_op jit(solution)/shard_map/ppermute | solution.py:520
  7.1 11.3 %collective-permute-start.3 = (f32[4,128,128]{2,1,0:T(8,128)S(1)}, f32[4,128,128]{2,1,0:T(8,128)S(1)}, u32[]{:S(2)}, u32[]{:S(2)}) collective-permute-start(f32[4,128,128]{2,1,0:T(8,128)S(1)} %get-tuple-element.53), channel_id=1, source_target_pairs={{0,16},{1,2},{2,1},{3,4},{4,3},{5,6},{6,5},{7,23},{8,24},{9,10},{1... | collective-permute-start | bytes 786440 | tf_op jit(solution)/shard_map/ppermute | solution.py:520
  7.1 11.8 %all-to-all-start = ((f32[8,40,128]{2,1,0:T(8,128)}), f32[8,40,128]{2,1,0:T(8,128)S(1)}, u32[]{:S(2)}, u32[]{:S(2)}) async-start(f32[8,40,128]{2,1,0:T(8,128)} %get-tuple-element.56), calls=%async_computation | async-start | bytes 327680 | tf_op jit(solution)/shard_map/all_to_all | solution.py:572
  10.7 9.0 %collective-permute-start.4 = (f32[17,4,128]{2,1,0:T(4,128)S(1)}, f32[17,4,128]{2,1,0:T(4,128)S(1)}, u32[]{:S(2)}, u32[]{:S(2)}) collective-permute-start(f32[17,4,128]{2,1,0:T(4,128)S(1)} %get-tuple-element.62), channel_id=1, source_target_pairs={{0,8},{1,9},{2,10},{3,11},{4,12},{5,13},{6,14},{7,15},{8,16},{9,17... | collective-permute-start | bytes 104456 | tf_op jit(solution)/shard_map/ppermute | solution.py:520
  13.5 6.2 %collective-permute-start.5 = (f32[17,4,128]{2,1,0:T(4,128)S(1)}, f32[17,4,128]{2,1,0:T(4,128)S(1)}, u32[]{:S(2)}, u32[]{:S(2)}) collective-permute-start(f32[17,4,128]{2,1,0:T(4,128)S(1)} %get-tuple-element.63), channel_id=1, source_target_pairs={{0,24},{1,25},{2,26},{3,27},{4,28},{5,29},{6,30},{7,31},{8,0},{9,1... | collective-permute-start | bytes 104456 | tf_op jit(solution)/shard_map/ppermute | solution.py:520
  18.4 0.9 %copy-start.1 = (f32[3,128,128]{2,1,0:T(8,128)S(1)}, f32[3,128,128]{2,1,0:T(8,128)}, u32[]{:S(2)}) copy-start(f32[3,128,128]{2,1,0:T(8,128)} %operator.1) | copy-start | bytes 589828
  21.2 5.4 %collective-permute-start.7 = (f32[136,128]{1,0:T(8,128)S(1)}, f32[136,128]{1,0:T(8,128)S(1)}, u32[]{:S(2)}, u32[]{:S(2)}) collective-permute-start(f32[136,128]{1,0:T(8,128)S(1)} %get-tuple-element.65), channel_id=1, source_target_pairs={{0,16},{1,2},{2,1},{3,4},{4,3},{5,6},{6,5},{7,23},{8,24},{9,10},{1... | collective-permute-start | bytes 208904 | tf_op jit(solution)/shard_map/ppermute | solution.py:520
  22.2 4.3 %collective-permute-start.6 = (f32[136,128]{1,0:T(8,128)S(1)}, f32[136,128]{1,0:T(8,128)S(1)}, u32[]{:S(2)}, u32[]{:S(2)}) collective-permute-start(f32[136,128]{1,0:T(8,128)S(1)} %get-tuple-element.65), channel_id=1, source_target_pairs={{0,1},{1,0},{2,3},{3,2},{4,5},{5,4},{6,7},{7,6},{8,9},{9,8},{10,11... | collective-permute-start | bytes 208904 | tf_op jit(solution)/shard_map/ppermute | solution.py:520
  22.2 9.9 %all-to-all-start.1 = ((f32[8,16,128]{2,1,0:T(8,128)}), f32[8,16,128]{2,1,0:T(8,128)S(1)}, u32[]{:S(2)}, u32[]{:S(2)}) async-start(f32[8,16,128]{2,1,0:T(8,128)} %bitcast.7), calls=%async_computation.1 | async-start | bytes 131072 | tf_op jit(solution)/shard_map/all_to_all | solution.py:621
  26.7 5.7 %collective-permute-start.8 = (f32[16,4,128]{2,1,0:T(4,128)S(1)}, f32[16,4,128]{2,1,0:T(4,128)S(1)}, u32[]{:S(2)}, u32[]{:S(2)}) collective-permute-start(f32[16,4,128]{2,1,0:T(4,128)S(1)} %get-tuple-element.72), channel_id=1, source_target_pairs={{0,8},{1,9},{2,10},{3,11},{4,12},{5,13},{6,14},{7,15},{8,16},{9,17... | collective-permute-start | bytes 98312 | tf_op jit(solution)/shard_map/ppermute | solution.py:520
  28.1 4.3 %collective-permute-start.9 = (f32[16,4,128]{2,1,0:T(4,128)S(1)}, f32[16,4,128]{2,1,0:T(4,128)S(1)}, u32[]{:S(2)}, u32[]{:S(2)}) collective-permute-start(f32[16,4,128]{2,1,0:T(4,128)S(1)} %get-tuple-element.73), channel_id=1, source_target_pairs={{0,24},{1,25},{2,26},{3,27},{4,28},{5,29},{6,30},{7,31},{8,0},{9,1... | collective-permute-start | bytes 98312 | tf_op jit(solution)/shard_map/ppermute | solution.py:520
  30.6 1.9 %copy-start = (f32[4,32,8,128]{3,2,1,0:T(8,128)S(1)}, f32[4,32,8,128]{3,2,1,0:T(8,128)}, u32[]{:S(2)}) copy-start(f32[4,32,8,128]{3,2,1,0:T(8,128)} %param.9) | copy-start | bytes 1572868

commit v7 on v6

--- a/solution.py
+++ b/solution.py
@@ -71,7 +71,7 @@
 
 def pack_kernel(
     inc_hbm, cl_hbm, ct_hbm, values, weights, columns_hbm, types_hbm, counts_hbm,
-    own, coef, b_out, a_out, rim_b, rim_a, w_out, e_out, slots_out,
+    own, coef, b_out, a_out, rim_b, w_out, e_out, slots_out,
     inc, cl, ct, raw, columns, types, counts, staged, sems,
 ):
     owners, bucket = (slots_out.shape[0], values.shape[1])
@@ -122,37 +122,38 @@
     b_row = STEPS - a_row
     for out, first in ((b_out, b_row), (a_out, a_row)):
         for k in range(STEPS):
-            out[k] = own[first + k]
-    for out, first in ((rim_b, b_row), (rim_a, a_row)):
-        for k in range(STEPS):
-            out[k, 0:STEPS, :] = own[first + k, 0:STEPS, :]
-            out[k, STEPS : 2 * STEPS, :] = own[first + k, LANES - STEPS : LANES, :]
-            out[STEPS + 1 + k] = raw[pl.ds(pl.multiple_of(8 * (STEPS + first + k), 8), 8), :]
-        out[STEPS, 0:STEPS, :] = coef[0:STEPS, :]
-        out[STEPS, STEPS : 2 * STEPS, :] = coef[LANES - STEPS : LANES, :]
+            out[k, 0:LANES, :] = own[first + k]
+    ends = jnp.concatenate([coef[0:STEPS, :], coef[LANES - STEPS : LANES, :]], 0)
+    rim_b[STEPS] = ends
+    for k in range(STEPS):
+        rim_b[k, 0:STEPS, :] = own[b_row + k, 0:STEPS, :]
+        rim_b[k, STEPS : 2 * STEPS, :] = own[b_row + k, LANES - STEPS : LANES, :]
+        rim_b[STEPS + 1 + k] = raw[pl.ds(pl.multiple_of(8 * (STEPS + b_row + k), 8), 8), :]
+        a_out[k, LANES : LANES + 8, :] = raw[pl.ds(pl.multiple_of(8 * (STEPS + a_row + k), 8), 8), :]
+        a_out[k, LANES + 8 : LANES + 16, :] = ends
     copies[8].wait()
 
 
-def edge_kernel(w_own, e_own, coef, rim_a, rim_b, w_out, e_out, co, raw):
+def edge_kernel(w_own, e_own, coef, a_in, rim_b, w_out, e_out, co, raw):
     even, pole = position()
     a_base, b_base, _, b_rows = halo_places(even, pole)
     sign = wind_sign(pole, (1, LANES))
     raw[...] = jnp.zeros(raw.shape, F32)
     for k in range(STEPS):
         kk = jnp.where(pole, STEPS - 1 - k, k)
-        w_out[a_base + k] = rim_a[k, 0:STEPS, :]
-        e_out[a_base + k] = rim_a[k, STEPS : 2 * STEPS, :]
+        w_out[a_base + k] = a_in[k, 0:STEPS, :]
+        e_out[a_base + k] = a_in[k, LANES - STEPS : LANES, :]
         rim = rim_b[kk] * sign
         w_out[b_base + k] = rim[0:STEPS]
         e_out[b_base + k] = rim[STEPS : 2 * STEPS]
-        raw[pl.ds(pl.multiple_of(8 * (a_base + k), 8), 8), :] = rim_a[STEPS + 1 + k]
+        raw[pl.ds(pl.multiple_of(8 * (a_base + k), 8), 8), :] = a_in[k, LANES : LANES + 8, :]
         raw[pl.ds(pl.multiple_of(8 * (b_base + k), 8), 8), :] = rim_b[STEPS + 1 + kk]
     for r in range(ROWS):
         w_out[STEPS + r] = w_own[r]
         e_out[STEPS + r] = e_own[r]
     plane = iota((8, LANES), 1) // 8
     tile = jnp.concatenate([w_own[ROWS], e_own[ROWS]], 0)
-    from_a = pltpu.roll(rim_a[STEPS], LANES // 2, 1)
+    from_a = pltpu.roll(a_in[0, LANES + 8 : LANES + 16, :], LANES // 2, 1)
     tile = jnp.where(plane // STEPS == a_base // STEPS, from_a, tile)
     for k in range(STEPS):
         shift = (8 * (b_base + k - STEPS - b_rows[k]) + 2 * LANES) % LANES
@@ -527,14 +528,13 @@
     cl = coef_lon.reshape(fields * ROWS, LANES)
     ct = coef_lat.reshape(fields * ROWS, LANES)
 
-    own, coef, b_send, a_send, rim_b, rim_a, w_own, e_own, slots_send = call(
+    own, coef, b_send, a_send, rim_b, w_own, e_own, slots_send = call(
         pack_kernel,
         [
             shape(ROWS, LANES, LANES),
             shape(LANES, LANES),
             shape(STEPS, LANES, LANES),
-            shape(STEPS, LANES, LANES),
-            shape(2 * STEPS + 1, 8, LANES),
+            shape(STEPS, LANES + 16, LANES),
             shape(2 * STEPS + 1, 8, LANES),
             shape(ROWS + 1, STEPS, LANES),
             shape(ROWS + 1, STEPS, LANES),
@@ -562,9 +562,8 @@
             pltpu.SemaphoreType.DMA((9,)),
         ],
         spaces={n: HBM for n in range(8)},
-        out_spaces={8: pl.ANY},
-    )
-    rim_a = send(rim_a, inner)
+        out_spaces={7: pl.ANY},
+    )
     a_in = send(a_send, inner)
     rim_b = send(rim_b, outer)
     b_in = send(b_send, outer)
@@ -579,7 +578,7 @@
     w_send, e_send, co = call(
         edge_kernel,
         [edge, edge, shape(LANES, LANES)],
-        [w_own, e_own, coef, rim_a, rim_b],
+        [w_own, e_own, coef, a_in, rim_b],
         [VMEM((LANES, LANES), F32)],
         flops=EDGE_COST,
     )

time: 34 us -> 33.5 us (0.985)
  starting transfers between devices: 21.9 us -> 21.5 us
    ppermute x10 -> x9, starting transfers between devices: 15.2 us -> 14.7 us  [local(): send = lambda x, route: lax.ppermute(x, ('lon', 'lat'), route)]
    ppermute x10 -> x9, waiting for transfers between devices: 1.4 us -> 1.43 us  [local(): send = lambda x, route: lax.ppermute(x, ('lon', 'lat'), route)]
  transfers between devices with their start and end apart: 12 -> 11, of which waited for: 3 -> 3; matrix products, arithmetic and copies ran while one was open for 0% -> 0% of each run, Pallas kernels for 14% -> 14%
where the time goes in v7:
time: 33.5 us; the launch traced here: 33.2 us
  starting transfers between devices  21.5 us (64%)
  Pallas kernels  9.18 us (27%)
  waiting for transfers between devices  1.43 us (4%)
  between operations  0.75 us (2%)
  local copies, waits for them, and re-layouts  0.34 us (1%)
    ppermute x9, starting transfers between devices, local(): send = lambda x, route: lax.ppermute(x, ('lon', 'lat'), route)  14.7 us
    pallas_call x11, Pallas kernels, call(): pl.pallas_call(kernel, out_shape=outs, in_specs=specs, out_specs=[pl.Bloc...  9.18 us
    all_to_all x1, starting transfers between devices, local(): lax.all_to_all(slots_send, 'lat', split_axis=0, concat_axis=0, tiled=True)  3.46 us
    all_to_all x1, starting transfers between devices, local(): lax.all_to_all(departures.reshape(lats, bucket, LANES), 'lat', split_axis...  3.35 us
    ppermute x9, waiting for transfers between devices, local(): send = lambda x, route: lax.ppermute(x, ('lon', 'lat'), route)  1.43 us
  transfers between devices with their start and end apart: 11, of which 3 were waited for; matrix products, arithmetic and copies ran while one was open for 0% of the time, Pallas kernels for 14%

profile of v7, /device:TPU:0, one launch (start us, length us, event | category | flops | bytes accessed | tf_op | source)
XLA Modules:
  0.0 33.2 jit_solution(17215227528445111052)
XLA Ops:
  0.6 1.8 %shard_map.104 = (f32[8,128,128]{2,1,0:T(8,128)S(1)}, f32[128,128]{1,0:T(8,128)S(1)}, f32[4,128,128]{2,1,0:T(8,128)S(1)}, f32[4,144,128]{2,1,0:T(8,128)S(1)}, f3...) custom-call(f32[1024,128]{1,0:T(8,128)} %bitcast.10, ...), custom_call_target="tpu_custom_call" | custom-call | bytes 2073632 | tf_op jit(solution)/shard_map/pallas_call | solution.py:489
  2.5 0.5 %collective-permute-start = (f32[4,144,128]{2,1,0:T(8,128)S(1)}, f32[4,144,128]{2,1,0:T(8,128)S(1)}, u32[]{:S(2)}, u32[]{:S(2)}) collective-permute-start(f32[4,144,128]{2,1,0:T(8,128)S(1)} %get-tuple-element.41), channel_id=1, source_target_pairs={{0,1},{1,0},{2,3},{3,2},{4,5},{5,4},{6,7},{7,6},{8,9},{9,8},{10,11... | collective-permute-start | bytes 884744 | tf_op jit(solution)/shard_map/ppermute | solution.py:521
  3.0 3.7 %collective-permute-start.1 = (f32[9,8,128]{2,1,0:T(8,128)S(1)}, f32[9,8,128]{2,1,0:T(8,128)S(1)}, u32[]{:S(2)}, u32[]{:S(2)}) collective-permute-start(f32[9,8,128]{2,1,0:T(8,128)S(1)} %get-tuple-element.45), channel_id=1, source_target_pairs={{0,16},{1,2},{2,1},{3,4},{4,3},{5,6},{6,5},{7,23},{8,24},{9,10},{1... | collective-permute-start | bytes 110600 | tf_op jit(solution)/shard_map/ppermute | solution.py:521
  6.7 3.5 %all-to-all-start = ((f32[8,40,128]{2,1,0:T(8,128)}), f32[8,40,128]{2,1,0:T(8,128)S(1)}, u32[]{:S(2)}, u32[]{:S(2)}) async-start(f32[8,40,128]{2,1,0:T(8,128)} %get-tuple-element.54), calls=%async_computation | async-start | bytes 327680 | tf_op jit(solution)/shard_map/all_to_all | solution.py:571
  10.2 0.1 shard_map.105
  10.3 2.7 %collective-permute-start.3 = (f32[17,4,128]{2,1,0:T(4,128)S(1)}, f32[17,4,128]{2,1,0:T(4,128)S(1)}, u32[]{:S(2)}, u32[]{:S(2)}) collective-permute-start(f32[17,4,128]{2,1,0:T(4,128)S(1)} %get-tuple-element.60), channel_id=1, source_target_pairs={{0,8},{1,9},{2,10},{3,11},{4,12},{5,13},{6,14},{7,15},{8,16},{9,17... | collective-permute-start | bytes 104456 | tf_op jit(solution)/shard_map/ppermute | solution.py:521
  13.0 2.8 %collective-permute-start.4 = (f32[17,4,128]{2,1,0:T(4,128)S(1)}, f32[17,4,128]{2,1,0:T(4,128)S(1)}, u32[]{:S(2)}, u32[]{:S(2)}) collective-permute-start(f32[17,4,128]{2,1,0:T(4,128)S(1)} %get-tuple-element.61), channel_id=1, source_target_pairs={{0,24},{1,25},{2,26},{3,27},{4,28},{5,29},{6,30},{7,31},{8,0},{9,1... | collective-permute-start | bytes 104456 | tf_op jit(solution)/shard_map/ppermute | solution.py:521
  15.9 0.5 %shard_map.106 = (f32[16,128,128]{2,1,0:T(8,128)S(1)}, f32[16,128,128]{2,1,0:T(8,128)S(1)}, f32[16,128,128]{2,1,0:T(8,128)S(1)}) custom-call(f32[128,128]{1,0:T(8,128)S(1)} %get-tuple-element.64.co), custom_call_target="tpu_custom_call" | custom-call | flops 100000000 | bytes 3211264 | tf_op jit(solution)/shard_map/pallas_call | solution.py:489
  16.3 1.0 %shard_map.107 = (f32[4,128,128]{2,1,0:T(8,128)S(1)}, f32[3,2,128,128]{3,2,1,0:T(8,128)S(1)}) custom-call(f32[8,128,128]{2,1,0:T(8,128)S(1)} %get-tuple-element.40.own, f32[4,144,128]{2,1,0:T(8,128)S(1)} %collective-permute-done.a_in, f32[16,128,128]{2,1,0:T(8,128)S(1)} %get-tuple-element.47.cl, f32[16,128,128]{2,1,0:T(8,128)S(1)} %get-tuple-element.48.ct, ...), custom_call_target="tpu_custom_call" | custom-call | flops 1000000000 | bytes 4620288 | tf_op jit(solution)/shard_map/pallas_call | solution.py:489
  17.4 0.6 %collective-permute-done.2.b_in = f32[4,128,128]{2,1,0:T(8,128)S(1)} collective-permute-done((f32[4,128,128]{2,1,0:T(8,128)S(1)}, f32[4,128,128]{2,1,0:T(8,128)S(1)}, u32[]{:S(2)}, u32[]{:S(2)}) %collective-permute-start.2) | collective-permute-done | bytes 262176 | tf_op jit(solution)/shard_map/ppermute | solution.py:521
  17.9 0.6 %shard_map.108.far_half = f32[4,128,128]{2,1,0:T(8,128)S(1)} custom-call(f32[8,128,128]{2,1,0:T(8,128)S(1)} %get-tuple-element.40.own, f32[4,128,128]{2,1,0:T(8,128)S(1)} %collective-permute-done.2.b_in, f32[3,2,128,128]{3,2,1,0:T(8,128)S(1)} %get-tuple-element.52.strips, f32[16,128,128]{2,1,0:T(8,128)S(1)} %get-tuple-element.47.cl, ...), custom_call_target="tpu_custom_call" | custom-call | flops 100000000 | bytes 4587520 | tf_op jit(solution)/shard_map/pallas_call | solution.py:489
  18.5 0.3 %copy-done.1 = f32[3,128,128]{2,1,0:T(8,128)S(1)} copy-done((f32[3,128,128]{2,1,0:T(8,128)S(1)}, f32[3,128,128]{2,1,0:T(8,128)}, u32[]{:S(2)}) %copy-start.1) | copy-done | bytes 196632
  18.9 0.4 %shard_map.109 = (f32[128,128]{1,0:T(8,128)S(1)}, s32[128,128]{1,0:T(8,128)S(1)}, f32[8,128]{1,0:T(8,128)S(1)}, bf16[768,256]{1,0:T(8,128)(2,1)S(1)}, bf16[256,768]{1,0:T(8,128)(2,1)S(1)}) custom-call(f32[4,128,128]{2,1,0:T(8,128)S(1)} %get-tuple-element.50.near_half, f32[4,128,128]{2,1,0:T(8,128)S(1)} %shard_map.108.far_half, ...), custom_call_target="tpu_custom_call" | custom-call | flops 100000000 | bytes 2592768 | tf_op jit(solution)/shard_map/pallas_call | solution.py:489
  19.3 1.5 %shard_map.110 = (f32[128,128]{1,0:T(8,128)}, f32[136,128]{1,0:T(8,128)S(1)}, f32[8,128,128]{2,1,0:T(8,128)S(1)}, f32[16,24,128]{2,1,0:T(8,128)S(1)}, f32[16,24,...) custom-call(f32[128,128]{1,0:T(8,128)S(1)} %get-tuple-element.55.column_in, s32[128,128]{1,0:T(8,128)S(1)} %get-tuple-element.56.code_in, ...), custom_call_target="tpu_custom_call" | custom-call | flops 100000000 | bytes 4337664 | tf_op jit(solution)/shard_map/pallas_call | solution.py:489
  20.7 1.0 %collective-permute-start.6 = (f32[136,128]{1,0:T(8,128)S(1)}, f32[136,128]{1,0:T(8,128)S(1)}, u32[]{:S(2)}, u32[]{:S(2)}) collective-permute-start(f32[136,128]{1,0:T(8,128)S(1)} %get-tuple-element.63), channel_id=1, source_target_pairs={{0,16},{1,2},{2,1},{3,4},{4,3},{5,6},{6,5},{7,23},{8,24},{9,10},{1... | collective-permute-start | bytes 208904 | tf_op jit(solution)/shard_map/ppermute | solution.py:521
  21.8 3.4 %all-to-all-start.1 = ((f32[8,16,128]{2,1,0:T(8,128)}), f32[8,16,128]{2,1,0:T(8,128)S(1)}, u32[]{:S(2)}, u32[]{:S(2)}) async-start(f32[8,16,128]{2,1,0:T(8,128)} %bitcast.7), calls=%async_computation.1 | async-start | bytes 131072 | tf_op jit(solution)/shard_map/all_to_all | solution.py:620
  25.2 0.5 %shard_map.111 = (f32[16,128,128]{2,1,0:T(8,128)S(1)}, f32[16,128,128]{2,1,0:T(8,128)S(1)}, f32[16,128,128]{2,1,0:T(8,128)S(1)}) custom-call(f32[128,128]{1,0:T(8,128)S(1)} %get-tuple-element.64.co), custom_call_target="tpu_custom_call" | custom-call | flops 100000000 | bytes 3211264 | tf_op jit(solution)/shard_map/pallas_call | solution.py:489
  25.6 0.5 %collective-permute-done.6.b_in = f32[136,128]{1,0:T(8,128)S(1)} collective-permute-done((f32[136,128]{1,0:T(8,128)S(1)}, f32[136,128]{1,0:T(8,128)S(1)}, u32[]{:S(2)}, u32[]{:S(2)}) %collective-permute-start.6) | collective-permute-done | bytes 69664 | tf_op jit(solution)/shard_map/ppermute | solution.py:521
  26.1 0.1 shard_map.113
  26.3 1.4 %collective-permute-start.7 = (f32[16,4,128]{2,1,0:T(4,128)S(1)}, f32[16,4,128]{2,1,0:T(4,128)S(1)}, u32[]{:S(2)}, u32[]{:S(2)}) collective-permute-start(f32[16,4,128]{2,1,0:T(4,128)S(1)} %get-tuple-element.70), channel_id=1, source_target_pairs={{0,8},{1,9},{2,10},{3,11},{4,12},{5,13},{6,14},{7,15},{8,16},{9,17... | collective-permute-start | bytes 98312 | tf_op jit(solution)/shard_map/ppermute | solution.py:521
  27.7 2.4 %collective-permute-start.8 = (f32[16,4,128]{2,1,0:T(4,128)S(1)}, f32[16,4,128]{2,1,0:T(4,128)S(1)}, u32[]{:S(2)}, u32[]{:S(2)}) collective-permute-start(f32[16,4,128]{2,1,0:T(4,128)S(1)} %get-tuple-element.71), channel_id=1, source_target_pairs={{0,24},{1,25},{2,26},{3,27},{4,28},{5,29},{6,30},{7,31},{8,0},{9,1... | collective-permute-start | bytes 98312 | tf_op jit(solution)/shard_map/ppermute | solution.py:521
  30.1 1.5 %shard_map.112 = (f32[8,128,128]{2,1,0:T(8,128)S(1)}, f32[16,24,128]{2,1,0:T(8,128)S(1)}) custom-call(f32[8,128,128]{2,1,0:T(8,128)S(1)} %get-tuple-element.62.f_in, f32[136,128]{1,0:T(8,128)S(1)} %collective-permute-done.5.a_in, f32[136,128]{1,0:T(8,128)S(1)} %collective-permute-done.6.b_in, f32[16,128,128]{2,1,0:T(8,128)S(1)} %get-tuple-element.65.cl, ...), custom_call_target="tpu_custom_call" | custom-call | flops 10000000000 | bytes 4530176 | tf_op jit(solution)/shard_map/pallas_call | solution.py:489
  31.7 0.3 collective-permute-done.7.from_west
  32.0 1.2 %shard_map.114 = (f32[1024,128]{1,0:T(8,128)}, f32[128,128]{1,0:T(8,128)}) custom-call(f32[1024,128]{1,0:T(8,128)S(1)} %bitcast.11, f32[8,128,128]{2,1,0:T(8,128)S(1)} %get-tuple-element.68.smooth, f32[16,24,128]{2,1,0:T(8,128)S(1)} %get-tuple-element.69.rim_in, f32[16,4,128]{2,1,0:T(4,128)S(1)} %collective-permute-done.7.from_west, ...), custom_call_target="tpu_custom_call" | custom-call | flops 100000000 | bytes 2555904 | tf_op jit(solution)/shard_map/pallas_call | solution.py:489
  (13 shorter events, 0.1 us)
Async XLA Ops:
  2.5 4.3 %collective-permute-start = (f32[4,144,128]{2,1,0:T(8,128)S(1)}, f32[4,144,128]{2,1,0:T(8,128)S(1)}, u32[]{:S(2)}, u32[]{:S(2)}) collective-permute-start(f32[4,144,128]{2,1,0:T(8,128)S(1)} %get-tuple-element.41), channel_id=1, source_target_pairs={{0,1},{1,0},{2,3},{3,2},{4,5},{5,4},{6,7},{7,6},{8,9},{9,8},{10,11... | collective-permute-start | bytes 884744 | tf_op jit(solution)/shard_map/ppermute | solution.py:521
  3.0 7.2 %collective-permute-start.1 = (f32[9,8,128]{2,1,0:T(8,128)S(1)}, f32[9,8,128]{2,1,0:T(8,128)S(1)}, u32[]{:S(2)}, u32[]{:S(2)}) collective-permute-start(f32[9,8,128]{2,1,0:T(8,128)S(1)} %get-tuple-element.45), channel_id=1, source_target_pairs={{0,16},{1,2},{2,1},{3,4},{4,3},{5,6},{6,5},{7,23},{8,24},{9,10},{1... | collective-permute-start | bytes 110600 | tf_op jit(solution)/shard_map/ppermute | solution.py:521
  6.6 11.3 %collective-permute-start.2 = (f32[4,128,128]{2,1,0:T(8,128)S(1)}, f32[4,128,128]{2,1,0:T(8,128)S(1)}, u32[]{:S(2)}, u32[]{:S(2)}) collective-permute-start(f32[4,128,128]{2,1,0:T(8,128)S(1)} %get-tuple-element.51), channel_id=1, source_target_pairs={{0,16},{1,2},{2,1},{3,4},{4,3},{5,6},{6,5},{7,23},{8,24},{9,10},{1... | collective-permute-start | bytes 786440 | tf_op jit(solution)/shard_map/ppermute | solution.py:521
  6.7 11.8 %all-to-all-start = ((f32[8,40,128]{2,1,0:T(8,128)}), f32[8,40,128]{2,1,0:T(8,128)S(1)}, u32[]{:S(2)}, u32[]{:S(2)}) async-start(f32[8,40,128]{2,1,0:T(8,128)} %get-tuple-element.54), calls=%async_computation | async-start | bytes 327680 | tf_op jit(solution)/shard_map/all_to_all | solution.py:571
  10.3 8.9 %collective-permute-start.3 = (f32[17,4,128]{2,1,0:T(4,128)S(1)}, f32[17,4,128]{2,1,0:T(4,128)S(1)}, u32[]{:S(2)}, u32[]{:S(2)}) collective-permute-start(f32[17,4,128]{2,1,0:T(4,128)S(1)} %get-tuple-element.60), channel_id=1, source_target_pairs={{0,8},{1,9},{2,10},{3,11},{4,12},{5,13},{6,14},{7,15},{8,16},{9,17... | collective-permute-start | bytes 104456 | tf_op jit(solution)/shard_map/ppermute | solution.py:521
  13.0 6.2 %collective-permute-start.4 = (f32[17,4,128]{2,1,0:T(4,128)S(1)}, f32[17,4,128]{2,1,0:T(4,128)S(1)}, u32[]{:S(2)}, u32[]{:S(2)}) collective-permute-start(f32[17,4,128]{2,1,0:T(4,128)S(1)} %get-tuple-element.61), channel_id=1, source_target_pairs={{0,24},{1,25},{2,26},{3,27},{4,28},{5,29},{6,30},{7,31},{8,0},{9,1... | collective-permute-start | bytes 104456 | tf_op jit(solution)/shard_map/ppermute | solution.py:521
  17.9 0.9 %copy-start.1 = (f32[3,128,128]{2,1,0:T(8,128)S(1)}, f32[3,128,128]{2,1,0:T(8,128)}, u32[]{:S(2)}) copy-start(f32[3,128,128]{2,1,0:T(8,128)} %operator.1) | copy-start | bytes 589828
  20.7 5.4 %collective-permute-start.6 = (f32[136,128]{1,0:T(8,128)S(1)}, f32[136,128]{1,0:T(8,128)S(1)}, u32[]{:S(2)}, u32[]{:S(2)}) collective-permute-start(f32[136,128]{1,0:T(8,128)S(1)} %get-tuple-element.63), channel_id=1, source_target_pairs={{0,16},{1,2},{2,1},{3,4},{4,3},{5,6},{6,5},{7,23},{8,24},{9,10},{1... | collective-permute-start | bytes 208904 | tf_op jit(solution)/shard_map/ppermute | solution.py:521
  21.8 4.3 %collective-permute-start.5 = (f32[136,128]{1,0:T(8,128)S(1)}, f32[136,128]{1,0:T(8,128)S(1)}, u32[]{:S(2)}, u32[]{:S(2)}) collective-permute-start(f32[136,128]{1,0:T(8,128)S(1)} %get-tuple-element.63), channel_id=1, source_target_pairs={{0,1},{1,0},{2,3},{3,2},{4,5},{5,4},{6,7},{7,6},{8,9},{9,8},{10,11... | collective-permute-start | bytes 208904 | tf_op jit(solution)/shard_map/ppermute | solution.py:521
  21.8 9.9 %all-to-all-start.1 = ((f32[8,16,128]{2,1,0:T(8,128)}), f32[8,16,128]{2,1,0:T(8,128)S(1)}, u32[]{:S(2)}, u32[]{:S(2)}) async-start(f32[8,16,128]{2,1,0:T(8,128)} %bitcast.7), calls=%async_computation.1 | async-start | bytes 131072 | tf_op jit(solution)/shard_map/all_to_all | solution.py:620
  26.3 5.7 %collective-permute-start.7 = (f32[16,4,128]{2,1,0:T(4,128)S(1)}, f32[16,4,128]{2,1,0:T(4,128)S(1)}, u32[]{:S(2)}, u32[]{:S(2)}) collective-permute-start(f32[16,4,128]{2,1,0:T(4,128)S(1)} %get-tuple-element.70), channel_id=1, source_target_pairs={{0,8},{1,9},{2,10},{3,11},{4,12},{5,13},{6,14},{7,15},{8,16},{9,17... | collective-permute-start | bytes 98312 | tf_op jit(solution)/shard_map/ppermute | solution.py:521
  27.7 4.3 %collective-permute-start.8 = (f32[16,4,128]{2,1,0:T(4,128)S(1)}, f32[16,4,128]{2,1,0:T(4,128)S(1)}, u32[]{:S(2)}, u32[]{:S(2)}) collective-permute-start(f32[16,4,128]{2,1,0:T(4,128)S(1)} %get-tuple-element.71), channel_id=1, source_target_pairs={{0,24},{1,25},{2,26},{3,27},{4,28},{5,29},{6,30},{7,31},{8,0},{9,1... | collective-permute-start | bytes 98312 | tf_op jit(solution)/shard_map/ppermute | solution.py:521
  30.1 1.9 %copy-start = (f32[4,32,8,128]{3,2,1,0:T(8,128)S(1)}, f32[4,32,8,128]{3,2,1,0:T(8,128)}, u32[]{:S(2)}) copy-start(f32[4,32,8,128]{3,2,1,0:T(8,128)} %param.9) | copy-start | bytes 1572868

commit v8 on v7

--- a/solution.py
+++ b/solution.py
@@ -18,7 +18,7 @@
 HBM = pltpu.HBM
 MIB = 1 << 20
 RIM_UNROLL = True
-BODY_UNROLL = 2
+BODY_UNROLL = True
 EDGE_COST = 10**10
 EXPAND_COST = 10**8
 STATE_COST = 10**9

time: 33.5 us -> 33.5 us (level)
  no operation moved by 1% of the time
where the time goes in v8:
time: 33.5 us; the launch traced here: 33.2 us
  starting transfers between devices  21.5 us (64%)
  Pallas kernels  9.21 us (27%)
  waiting for transfers between devices  1.42 us (4%)
  between operations  0.74 us (2%)
  local copies, waits for them, and re-layouts  0.34 us (1%)
    ppermute x9, starting transfers between devices, local(): send = lambda x, route: lax.ppermute(x, ('lon', 'lat'), route)  14.7 us
    pallas_call x11, Pallas kernels, call(): pl.pallas_call(kernel, out_shape=outs, in_specs=specs, out_specs=[pl.Bloc...  9.21 us
    all_to_all x1, starting transfers between devices, local(): lax.all_to_all(slots_send, 'lat', split_axis=0, concat_axis=0, tiled=True)  3.46 us
    all_to_all x1, starting transfers between devices, local(): lax.all_to_all(departures.reshape(lats, bucket, LANES), 'lat', split_axis...  3.35 us
    ppermute x9, waiting for transfers between devices, local(): send = lambda x, route: lax.ppermute(x, ('lon', 'lat'), route)  1.41 us
  transfers between devices with their start and end apart: 11, of which 3 were waited for; matrix products, arithmetic and copies ran while one was open for 0% of the time, Pallas kernels for 14%

profile of v8, /device:TPU:0, one launch (start us, length us, event | category | flops | bytes accessed | tf_op | source)
XLA Modules:
  0.0 33.2 jit_solution(12913460081327550500)
XLA Ops:
  0.6 1.8 %shard_map.104 = (f32[8,128,128]{2,1,0:T(8,128)S(1)}, f32[128,128]{1,0:T(8,128)S(1)}, f32[4,128,128]{2,1,0:T(8,128)S(1)}, f32[4,144,128]{2,1,0:T(8,128)S(1)}, f3...) custom-call(f32[1024,128]{1,0:T(8,128)} %bitcast.10, ...), custom_call_target="tpu_custom_call" | custom-call | bytes 2073632 | tf_op jit(solution)/shard_map/pallas_call | solution.py:489
  2.5 0.5 %collective-permute-start = (f32[4,144,128]{2,1,0:T(8,128)S(1)}, f32[4,144,128]{2,1,0:T(8,128)S(1)}, u32[]{:S(2)}, u32[]{:S(2)}) collective-permute-start(f32[4,144,128]{2,1,0:T(8,128)S(1)} %get-tuple-element.41), channel_id=1, source_target_pairs={{0,1},{1,0},{2,3},{3,2},{4,5},{5,4},{6,7},{7,6},{8,9},{9,8},{10,11... | collective-permute-start | bytes 884744 | tf_op jit(solution)/shard_map/ppermute | solution.py:521
  3.0 3.7 %collective-permute-start.1 = (f32[9,8,128]{2,1,0:T(8,128)S(1)}, f32[9,8,128]{2,1,0:T(8,128)S(1)}, u32[]{:S(2)}, u32[]{:S(2)}) collective-permute-start(f32[9,8,128]{2,1,0:T(8,128)S(1)} %get-tuple-element.45), channel_id=1, source_target_pairs={{0,16},{1,2},{2,1},{3,4},{4,3},{5,6},{6,5},{7,23},{8,24},{9,10},{1... | collective-permute-start | bytes 110600 | tf_op jit(solution)/shard_map/ppermute | solution.py:521
  6.7 3.5 %all-to-all-start = ((f32[8,40,128]{2,1,0:T(8,128)}), f32[8,40,128]{2,1,0:T(8,128)S(1)}, u32[]{:S(2)}, u32[]{:S(2)}) async-start(f32[8,40,128]{2,1,0:T(8,128)} %get-tuple-element.54), calls=%async_computation | async-start | bytes 327680 | tf_op jit(solution)/shard_map/all_to_all | solution.py:571
  10.2 0.1 shard_map.105
  10.3 2.7 %collective-permute-start.3 = (f32[17,4,128]{2,1,0:T(4,128)S(1)}, f32[17,4,128]{2,1,0:T(4,128)S(1)}, u32[]{:S(2)}, u32[]{:S(2)}) collective-permute-start(f32[17,4,128]{2,1,0:T(4,128)S(1)} %get-tuple-element.60), channel_id=1, source_target_pairs={{0,8},{1,9},{2,10},{3,11},{4,12},{5,13},{6,14},{7,15},{8,16},{9,17... | collective-permute-start | bytes 104456 | tf_op jit(solution)/shard_map/ppermute | solution.py:521
  13.0 2.8 %collective-permute-start.4 = (f32[17,4,128]{2,1,0:T(4,128)S(1)}, f32[17,4,128]{2,1,0:T(4,128)S(1)}, u32[]{:S(2)}, u32[]{:S(2)}) collective-permute-start(f32[17,4,128]{2,1,0:T(4,128)S(1)} %get-tuple-element.61), channel_id=1, source_target_pairs={{0,24},{1,25},{2,26},{3,27},{4,28},{5,29},{6,30},{7,31},{8,0},{9,1... | collective-permute-start | bytes 104456 | tf_op jit(solution)/shard_map/ppermute | solution.py:521
  15.9 0.5 %shard_map.106 = (f32[16,128,128]{2,1,0:T(8,128)S(1)}, f32[16,128,128]{2,1,0:T(8,128)S(1)}, f32[16,128,128]{2,1,0:T(8,128)S(1)}) custom-call(f32[128,128]{1,0:T(8,128)S(1)} %get-tuple-element.64.co), custom_call_target="tpu_custom_call" | custom-call | flops 100000000 | bytes 3211264 | tf_op jit(solution)/shard_map/pallas_call | solution.py:489
  16.3 1.1 %shard_map.107 = (f32[4,128,128]{2,1,0:T(8,128)S(1)}, f32[3,2,128,128]{3,2,1,0:T(8,128)S(1)}) custom-call(f32[8,128,128]{2,1,0:T(8,128)S(1)} %get-tuple-element.40.own, f32[4,144,128]{2,1,0:T(8,128)S(1)} %collective-permute-done.a_in, f32[16,128,128]{2,1,0:T(8,128)S(1)} %get-tuple-element.47.cl, f32[16,128,128]{2,1,0:T(8,128)S(1)} %get-tuple-element.48.ct, ...), custom_call_target="tpu_custom_call" | custom-call | flops 1000000000 | bytes 4620288 | tf_op jit(solution)/shard_map/pallas_call | solution.py:489
  17.4 0.5 %collective-permute-done.2.b_in = f32[4,128,128]{2,1,0:T(8,128)S(1)} collective-permute-done((f32[4,128,128]{2,1,0:T(8,128)S(1)}, f32[4,128,128]{2,1,0:T(8,128)S(1)}, u32[]{:S(2)}, u32[]{:S(2)}) %collective-permute-start.2) | collective-permute-done | bytes 262176 | tf_op jit(solution)/shard_map/ppermute | solution.py:521
  17.9 0.6 %shard_map.108.far_half = f32[4,128,128]{2,1,0:T(8,128)S(1)} custom-call(f32[8,128,128]{2,1,0:T(8,128)S(1)} %get-tuple-element.40.own, f32[4,128,128]{2,1,0:T(8,128)S(1)} %collective-permute-done.2.b_in, f32[3,2,128,128]{3,2,1,0:T(8,128)S(1)} %get-tuple-element.52.strips, f32[16,128,128]{2,1,0:T(8,128)S(1)} %get-tuple-element.47.cl, ...), custom_call_target="tpu_custom_call" | custom-call | flops 100000000 | bytes 4587520 | tf_op jit(solution)/shard_map/pallas_call | solution.py:489
  18.5 0.3 %copy-done.1 = f32[3,128,128]{2,1,0:T(8,128)S(1)} copy-done((f32[3,128,128]{2,1,0:T(8,128)S(1)}, f32[3,128,128]{2,1,0:T(8,128)}, u32[]{:S(2)}) %copy-start.1) | copy-done | bytes 196632
  18.9 0.4 %shard_map.109 = (f32[128,128]{1,0:T(8,128)S(1)}, s32[128,128]{1,0:T(8,128)S(1)}, f32[8,128]{1,0:T(8,128)S(1)}, bf16[768,256]{1,0:T(8,128)(2,1)S(1)}, bf16[256,768]{1,0:T(8,128)(2,1)S(1)}) custom-call(f32[4,128,128]{2,1,0:T(8,128)S(1)} %get-tuple-element.50.near_half, f32[4,128,128]{2,1,0:T(8,128)S(1)} %shard_map.108.far_half, ...), custom_call_target="tpu_custom_call" | custom-call | flops 100000000 | bytes 2592768 | tf_op jit(solution)/shard_map/pallas_call | solution.py:489
  19.3 1.5 %shard_map.110 = (f32[128,128]{1,0:T(8,128)}, f32[136,128]{1,0:T(8,128)S(1)}, f32[8,128,128]{2,1,0:T(8,128)S(1)}, f32[16,24,128]{2,1,0:T(8,128)S(1)}, f32[16,24,...) custom-call(f32[128,128]{1,0:T(8,128)S(1)} %get-tuple-element.55.column_in, s32[128,128]{1,0:T(8,128)S(1)} %get-tuple-element.56.code_in, ...), custom_call_target="tpu_custom_call" | custom-call | flops 100000000 | bytes 4337664 | tf_op jit(solution)/shard_map/pallas_call | solution.py:489
  20.7 1.0 %collective-permute-start.6 = (f32[136,128]{1,0:T(8,128)S(1)}, f32[136,128]{1,0:T(8,128)S(1)}, u32[]{:S(2)}, u32[]{:S(2)}) collective-permute-start(f32[136,128]{1,0:T(8,128)S(1)} %get-tuple-element.63), channel_id=1, source_target_pairs={{0,16},{1,2},{2,1},{3,4},{4,3},{5,6},{6,5},{7,23},{8,24},{9,10},{1... | collective-permute-start | bytes 208904 | tf_op jit(solution)/shard_map/ppermute | solution.py:521
  21.8 3.4 %all-to-all-start.1 = ((f32[8,16,128]{2,1,0:T(8,128)}), f32[8,16,128]{2,1,0:T(8,128)S(1)}, u32[]{:S(2)}, u32[]{:S(2)}) async-start(f32[8,16,128]{2,1,0:T(8,128)} %bitcast.7), calls=%async_computation.1 | async-start | bytes 131072 | tf_op jit(solution)/shard_map/all_to_all | solution.py:620
  25.2 0.5 %shard_map.111 = (f32[16,128,128]{2,1,0:T(8,128)S(1)}, f32[16,128,128]{2,1,0:T(8,128)S(1)}, f32[16,128,128]{2,1,0:T(8,128)S(1)}) custom-call(f32[128,128]{1,0:T(8,128)S(1)} %get-tuple-element.64.co), custom_call_target="tpu_custom_call" | custom-call | flops 100000000 | bytes 3211264 | tf_op jit(solution)/shard_map/pallas_call | solution.py:489
  25.6 0.5 %collective-permute-done.6.b_in = f32[136,128]{1,0:T(8,128)S(1)} collective-permute-done((f32[136,128]{1,0:T(8,128)S(1)}, f32[136,128]{1,0:T(8,128)S(1)}, u32[]{:S(2)}, u32[]{:S(2)}) %collective-permute-start.6) | collective-permute-done | bytes 69664 | tf_op jit(solution)/shard_map/ppermute | solution.py:521
  26.1 0.1 shard_map.113
  26.3 1.4 %collective-permute-start.7 = (f32[16,4,128]{2,1,0:T(4,128)S(1)}, f32[16,4,128]{2,1,0:T(4,128)S(1)}, u32[]{:S(2)}, u32[]{:S(2)}) collective-permute-start(f32[16,4,128]{2,1,0:T(4,128)S(1)} %get-tuple-element.70), channel_id=1, source_target_pairs={{0,8},{1,9},{2,10},{3,11},{4,12},{5,13},{6,14},{7,15},{8,16},{9,17... | collective-permute-start | bytes 98312 | tf_op jit(solution)/shard_map/ppermute | solution.py:521
  27.7 2.4 %collective-permute-start.8 = (f32[16,4,128]{2,1,0:T(4,128)S(1)}, f32[16,4,128]{2,1,0:T(4,128)S(1)}, u32[]{:S(2)}, u32[]{:S(2)}) collective-permute-start(f32[16,4,128]{2,1,0:T(4,128)S(1)} %get-tuple-element.71), channel_id=1, source_target_pairs={{0,24},{1,25},{2,26},{3,27},{4,28},{5,29},{6,30},{7,31},{8,0},{9,1... | collective-permute-start | bytes 98312 | tf_op jit(solution)/shard_map/ppermute | solution.py:521
  30.1 1.5 %shard_map.112 = (f32[8,128,128]{2,1,0:T(8,128)S(1)}, f32[16,24,128]{2,1,0:T(8,128)S(1)}) custom-call(f32[8,128,128]{2,1,0:T(8,128)S(1)} %get-tuple-element.62.f_in, f32[136,128]{1,0:T(8,128)S(1)} %collective-permute-done.5.a_in, f32[136,128]{1,0:T(8,128)S(1)} %collective-permute-done.6.b_in, f32[16,128,128]{2,1,0:T(8,128)S(1)} %get-tuple-element.65.cl, ...), custom_call_target="tpu_custom_call" | custom-call | flops 10000000000 | bytes 4530176 | tf_op jit(solution)/shard_map/pallas_call | solution.py:489
  31.7 0.3 %collective-permute-done.7.from_west = f32[16,4,128]{2,1,0:T(4,128)S(1)} collective-permute-done((f32[16,4,128]{2,1,0:T(4,128)S(1)}, f32[16,4,128]{2,1,0:T(4,128)S(1)}, u32[]{:S(2)}, u32[]{:S(2)}) %collective-permute-start.7) | collective-permute-done | bytes 32800 | tf_op jit(solution)/shard_map/ppermute | solution.py:521
  32.0 1.2 %shard_map.114 = (f32[1024,128]{1,0:T(8,128)}, f32[128,128]{1,0:T(8,128)}) custom-call(f32[1024,128]{1,0:T(8,128)S(1)} %bitcast.11, f32[8,128,128]{2,1,0:T(8,128)S(1)} %get-tuple-element.68.smooth, f32[16,24,128]{2,1,0:T(8,128)S(1)} %get-tuple-element.69.rim_in, f32[16,4,128]{2,1,0:T(4,128)S(1)} %collective-permute-done.7.from_west, ...), custom_call_target="tpu_custom_call" | custom-call | flops 100000000 | bytes 2555904 | tf_op jit(solution)/shard_map/pallas_call | solution.py:489
  (13 shorter events, 0.1 us)
Async XLA Ops:
  2.5 4.3 %collective-permute-start = (f32[4,144,128]{2,1,0:T(8,128)S(1)}, f32[4,144,128]{2,1,0:T(8,128)S(1)}, u32[]{:S(2)}, u32[]{:S(2)}) collective-permute-start(f32[4,144,128]{2,1,0:T(8,128)S(1)} %get-tuple-element.41), channel_id=1, source_target_pairs={{0,1},{1,0},{2,3},{3,2},{4,5},{5,4},{6,7},{7,6},{8,9},{9,8},{10,11... | collective-permute-start | bytes 884744 | tf_op jit(solution)/shard_map/ppermute | solution.py:521
  3.0 7.2 %collective-permute-start.1 = (f32[9,8,128]{2,1,0:T(8,128)S(1)}, f32[9,8,128]{2,1,0:T(8,128)S(1)}, u32[]{:S(2)}, u32[]{:S(2)}) collective-permute-start(f32[9,8,128]{2,1,0:T(8,128)S(1)} %get-tuple-element.45), channel_id=1, source_target_pairs={{0,16},{1,2},{2,1},{3,4},{4,3},{5,6},{6,5},{7,23},{8,24},{9,10},{1... | collective-permute-start | bytes 110600 | tf_op jit(solution)/shard_map/ppermute | solution.py:521
  6.6 11.3 %collective-permute-start.2 = (f32[4,128,128]{2,1,0:T(8,128)S(1)}, f32[4,128,128]{2,1,0:T(8,128)S(1)}, u32[]{:S(2)}, u32[]{:S(2)}) collective-permute-start(f32[4,128,128]{2,1,0:T(8,128)S(1)} %get-tuple-element.51), channel_id=1, source_target_pairs={{0,16},{1,2},{2,1},{3,4},{4,3},{5,6},{6,5},{7,23},{8,24},{9,10},{1... | collective-permute-start | bytes 786440 | tf_op jit(solution)/shard_map/ppermute | solution.py:521
  6.7 11.8 %all-to-all-start = ((f32[8,40,128]{2,1,0:T(8,128)}), f32[8,40,128]{2,1,0:T(8,128)S(1)}, u32[]{:S(2)}, u32[]{:S(2)}) async-start(f32[8,40,128]{2,1,0:T(8,128)} %get-tuple-element.54), calls=%async_computation | async-start | bytes 327680 | tf_op jit(solution)/shard_map/all_to_all | solution.py:571
  10.3 8.9 %collective-permute-start.3 = (f32[17,4,128]{2,1,0:T(4,128)S(1)}, f32[17,4,128]{2,1,0:T(4,128)S(1)}, u32[]{:S(2)}, u32[]{:S(2)}) collective-permute-start(f32[17,4,128]{2,1,0:T(4,128)S(1)} %get-tuple-element.60), channel_id=1, source_target_pairs={{0,8},{1,9},{2,10},{3,11},{4,12},{5,13},{6,14},{7,15},{8,16},{9,17... | collective-permute-start | bytes 104456 | tf_op jit(solution)/shard_map/ppermute | solution.py:521
  13.0 6.2 %collective-permute-start.4 = (f32[17,4,128]{2,1,0:T(4,128)S(1)}, f32[17,4,128]{2,1,0:T(4,128)S(1)}, u32[]{:S(2)}, u32[]{:S(2)}) collective-permute-start(f32[17,4,128]{2,1,0:T(4,128)S(1)} %get-tuple-element.61), channel_id=1, source_target_pairs={{0,24},{1,25},{2,26},{3,27},{4,28},{5,29},{6,30},{7,31},{8,0},{9,1... | collective-permute-start | bytes 104456 | tf_op jit(solution)/shard_map/ppermute | solution.py:521
  17.9 0.9 %copy-start.1 = (f32[3,128,128]{2,1,0:T(8,128)S(1)}, f32[3,128,128]{2,1,0:T(8,128)}, u32[]{:S(2)}) copy-start(f32[3,128,128]{2,1,0:T(8,128)} %operator.1) | copy-start | bytes 589828
  20.7 5.4 %collective-permute-start.6 = (f32[136,128]{1,0:T(8,128)S(1)}, f32[136,128]{1,0:T(8,128)S(1)}, u32[]{:S(2)}, u32[]{:S(2)}) collective-permute-start(f32[136,128]{1,0:T(8,128)S(1)} %get-tuple-element.63), channel_id=1, source_target_pairs={{0,16},{1,2},{2,1},{3,4},{4,3},{5,6},{6,5},{7,23},{8,24},{9,10},{1... | collective-permute-start | bytes 208904 | tf_op jit(solution)/shard_map/ppermute | solution.py:521
  21.8 4.3 %collective-permute-start.5 = (f32[136,128]{1,0:T(8,128)S(1)}, f32[136,128]{1,0:T(8,128)S(1)}, u32[]{:S(2)}, u32[]{:S(2)}) collective-permute-start(f32[136,128]{1,0:T(8,128)S(1)} %get-tuple-element.63), channel_id=1, source_target_pairs={{0,1},{1,0},{2,3},{3,2},{4,5},{5,4},{6,7},{7,6},{8,9},{9,8},{10,11... | collective-permute-start | bytes 208904 | tf_op jit(solution)/shard_map/ppermute | solution.py:521
  21.8 9.9 %all-to-all-start.1 = ((f32[8,16,128]{2,1,0:T(8,128)}), f32[8,16,128]{2,1,0:T(8,128)S(1)}, u32[]{:S(2)}, u32[]{:S(2)}) async-start(f32[8,16,128]{2,1,0:T(8,128)} %bitcast.7), calls=%async_computation.1 | async-start | bytes 131072 | tf_op jit(solution)/shard_map/all_to_all | solution.py:620
  26.3 5.7 %collective-permute-start.7 = (f32[16,4,128]{2,1,0:T(4,128)S(1)}, f32[16,4,128]{2,1,0:T(4,128)S(1)}, u32[]{:S(2)}, u32[]{:S(2)}) collective-permute-start(f32[16,4,128]{2,1,0:T(4,128)S(1)} %get-tuple-element.70), channel_id=1, source_target_pairs={{0,8},{1,9},{2,10},{3,11},{4,12},{5,13},{6,14},{7,15},{8,16},{9,17... | collective-permute-start | bytes 98312 | tf_op jit(solution)/shard_map/ppermute | solution.py:521
  27.7 4.3 %collective-permute-start.8 = (f32[16,4,128]{2,1,0:T(4,128)S(1)}, f32[16,4,128]{2,1,0:T(4,128)S(1)}, u32[]{:S(2)}, u32[]{:S(2)}) collective-permute-start(f32[16,4,128]{2,1,0:T(4,128)S(1)} %get-tuple-element.71), channel_id=1, source_target_pairs={{0,24},{1,25},{2,26},{3,27},{4,28},{5,29},{6,30},{7,31},{8,0},{9,1... | collective-permute-start | bytes 98312 | tf_op jit(solution)/shard_map/ppermute | solution.py:521
  30.1 1.9 %copy-start = (f32[4,32,8,128]{3,2,1,0:T(8,128)S(1)}, f32[4,32,8,128]{3,2,1,0:T(8,128)}, u32[]{:S(2)}) copy-start(f32[4,32,8,128]{3,2,1,0:T(8,128)} %param.9) | copy-start | bytes 1572868
